TPU v7x, 256 devices: a whole 4x4x8 slice. The times are simulated.
256 devices in a mesh: tm: 8 (over z_lo, core), space: 32 (over z_hi, x, y).
Axes of the slice: x: 4, y: 4, z: 8 (z_hi: 2, z_lo: 4; z = z_hi * 4 + z_lo), core: 2. Of those that a mesh axis runs over, the one named last changes fastest.
Arguments:
- trajectory: bfloat16 [32, 8, 128, 32, 128], P('tm', None, 'space'), may hold values from -6 to 6
- noise: bfloat16 [32, 8, 128, 32, 128], P('tm', None, 'space'), may hold values from -6 to 6
- start: float32 [8, 128, 32, 128], P(None, 'space'), may hold values from -6 to 6
- conv_weight: bfloat16 [27, 64, 8], replicated, may hold values from -0.4375 to 0.4375
- conv_bias: float32 [64], replicated, may hold values from -3 to 3
- step_embed: float32 [32, 64], P('tm'), may hold values from -3 to 3
- out_weight: bfloat16 [8, 64], replicated, may hold values from -0.375 to 0.375
- decoder: float32 [8], replicated, may hold values from -2 to 2
- angle_index: int32 [32], replicated, may hold values from 0 to 179
- measured: float32 [96, 32, 128], P('space'), may hold values from -6 to 6
- step_scale: float32 [32], P('tm'), may hold values from 0.03 to 0.09
- guide_scale: float32 [32], P('tm'), may hold values from 1 to 3
- noise_scale: float32 [32], P('tm'), may hold values from 0.05 to 0.2
Outputs:
- new_trajectory: float32 [32, 8, 128, 32, 128], P('tm', None, 'space')
All inputs are finite; a program needn't handle non-finite values.
Results may differ from a plain program's by a relative error of at most 0.00065.
Values may be sent and summed in bfloat16 or wider, within the bound.
No kernel may reach another device: no remote copies, remote signals or barrier semaphores. Data moves between devices by JAX's collectives and lax.ppermute only.
A program may use at most 192 MiB of HBM per device.

v0:
```python
import jax
import jax.numpy as jnp
from jax import lax
from jax.sharding import PartitionSpec as P

ANGLES = 180


PROJ = 0.125


def padded_2(shard, sides, width):
    for axis, dim in sides:
        count, length = (lax.axis_size(axis), shard.shape[dim])
        up = [(i, (i + 1) % count) for i in range(count - 1)]
        down = [(j, i) for i, j in up]
        last = lax.slice_in_dim(shard, length - width, length, axis=dim)
        first = lax.slice_in_dim(shard, 0, width, axis=dim)
        before = lax.ppermute(last, axis, up)
        after = lax.ppermute(first, axis, down)
        shard = jnp.concatenate([before, shard, after], axis=dim)
    return shard


def prefix(value, axis, join, neutral):
    count, mine = (lax.axis_size(axis), lax.axis_index(axis))
    pieces = lax.all_gather(value, axis)
    subtotal = jnp.full_like(value, 0) + jnp.asarray(neutral, value.dtype)

    def lap(position, subtotal):
        longer = join(subtotal, pieces[position])
        return jnp.where(position < mine, longer, subtotal)

    return lax.fori_loop(0, count - 1, lap, subtotal)


def hat_table(angle_index, zpos, ycount, rowcount):
    theta = jnp.pi * angle_index.astype(jnp.float32) / ANGLES
    ypos = jnp.arange(ycount).astype(jnp.float32) - (ycount - 1) / 2.0
    spos = jnp.arange(rowcount).astype(jnp.float32) - (rowcount - 1) / 2.0
    coord = (
        ypos[None, None, :] * jnp.cos(theta)[:, None, None]
        + zpos[None, :, None] * jnp.sin(theta)[:, None, None]
    )
    table = jnp.maximum(0.0, 1.0 - jnp.abs(coord[None] - spos[:, None, None, None]))
    return table.reshape(rowcount, theta.shape[0], zpos.shape[0] * ycount)


def on_device(
    trajectory,
    noise,
    start,
    conv_weight,
    conv_bias,
    step_embed,
    out_weight,
    decoder,
    angle_index,
    measured,
    step_scale,
    guide_scale,
    noise_scale,
):
    step_count = trajectory.shape[0]
    planes = trajectory.shape[2]
    ycount = trajectory.shape[3]
    xcount = trajectory.shape[4]
    rows_dev = measured.shape[0]
    slabs = lax.axis_size("space")
    slab_index = lax.axis_index("space")
    total_planes = planes * slabs
    rowcount = rows_dev * slabs
    zpos = (slab_index * planes + jnp.arange(planes)).astype(jnp.float32) - (total_planes - 1) / 2.0
    table = hat_table(angle_index, zpos, ycount, rowcount)
    extended = padded_2(trajectory, (("space", 2),), 1)
    images = []
    for position in range(step_count):
        state32 = trajectory[position].astype(jnp.float32)
        images.append(
            jnp.sum(decoder[:, None, None, None] * state32, axis=0).reshape(planes * ycount, xcount)
        )
    drifts = []
    for position in range(step_count):
        image = images[position]
        own_rows = lax.psum_scatter(
            PROJ * jnp.einsum("svp,px->svx", table, image, precision=lax.Precision.HIGHEST),
            "space",
            scatter_dimension=0,
            tiled=True,
        )
        misfit = own_rows - measured
        summed = jnp.einsum(
            "svp,svx->px",
            table,
            lax.all_gather(misfit, "space", axis=0, tiled=True),
            precision=lax.Precision.HIGHEST,
        )
        back = PROJ * summed
        back = back.reshape(planes, ycount, xcount)
        padded = jnp.pad(extended[position], ((0, 0), (0, 0), (1, 1), (1, 1)))
        windows = []
        for plane_off in range(3):
            for row_off in range(3):
                for col_off in range(3):
                    windows.append(
                        padded[
                            :,
                            plane_off : plane_off + planes,
                            row_off : row_off + ycount,
                            col_off : col_off + xcount,
                        ]
                    )
        patches = jnp.stack(windows, axis=0)
        pre = jnp.einsum(
            "khc,kczyx->hzyx", conv_weight, patches, preferred_element_type=jnp.float32
        )
        pre = pre + conv_bias[:, None, None, None] + step_embed[position][:, None, None, None]
        hidden = jax.nn.silu(pre).astype(jnp.bfloat16)
        eps = jnp.einsum("ch,hzyx->czyx", out_weight, hidden, preferred_element_type=jnp.float32)
        guided = eps - guide_scale[position] * decoder[:, None, None, None] * back[None]
        drifts.append(
            step_scale[position] * guided
            + noise_scale[position] * noise[position].astype(jnp.float32)
        )
    stacked = jnp.stack(drifts, axis=0)
    running = jnp.cumsum(stacked, axis=0)
    block_total = running[-1]
    earlier = prefix(block_total, "tm", jnp.add, jnp.zeros_like(block_total))
    return start[None] + earlier[None] + running


def solution(mesh):
    return jax.shard_map(
        on_device,
        mesh=mesh,
        in_specs=(
            P("tm", None, "space", None, None),
            P("tm", None, "space", None, None),
            P(None, "space", None, None),
            P(),
            P(),
            P("tm", None),
            P(),
            P(),
            P(),
            P("space", None, None),
            P("tm"),
            P("tm"),
            P("tm"),
        ),
        out_specs=P("tm", None, "space", None, None),
        check_vma=False,
    )
```

profile of v0, /device:TPU:6, one launch (start us, length us, event | category | flops | bytes accessed | tf_op | source)
XLA Modules:
  0.0 1449.8 jit_solution(8200093008696451876)
XLA Ops:
  9.0 4.1 bitcast_multiply_fusion.7
  13.1 2.1 copy.1689
  15.2 4.1 bitcast_multiply_fusion.6
  19.3 2.1 copy.1693
  21.9 4.1 bitcast_multiply_fusion.4
  28.3 3.6 collective-permute-start
  32.0 4.5 collective-permute-start.1
  36.5 4.1 bitcast_multiply_fusion.5
  40.6 2.1 copy.1697
  44.3 2.5 broadcast_multiply_fusion.5
  81.3 44.6 %stack.378 = bf16[27,8,4,32,128]{4,0,1,3,2:T(8,128)(2,1)} concatenate(bf16[1,8,4,32,128]{4,0,1,3,2:T(2,128)(2,1)S(1)} %copy.1661, bf16[1,8,4,32,128]{4,0,1,3,2:T(2,128)(2,1)S(1)} %copy.1662, bf16[1,8,4,32,128]{4,0,1,3,2:T(2,128)(2,1)S(1)} %copy.1663, bf16[1,8,4,32,128]{4,0,1,3,2:T(2,128)(2,1)S(1)} %copy.1664, bf16[1,8,4,32,128]{4,0,1,3,2:T(2,128)(2,1)} %copy.1665, ...), dimensions={0} | concatenate | bytes 14155776 | tf_op jit(solution)/shard_map/stack | solution.py:113
  142.8 128.2 %reduce-scatter.5.cloned.1.call-done = f32[3,32,128]{2,1,0:T(8,128)} async-done(((f32[96,32,128]{2,1,0:T(8,128)}), f32[3,32,128]{2,1,0:T(8,128)}) %reduce-scatter.5.cloned.1.call-update) | async-done | bytes 49168 | tf_op jit(solution)/shard_map/reduce_scatter | solution.py:85
  271.0 253.1 %reduce-scatter.7.cloned.1.call-done = f32[3,32,128]{2,1,0:T(8,128)} async-done(((f32[96,32,128]{2,1,0:T(8,128)}), f32[3,32,128]{2,1,0:T(8,128)}) %reduce-scatter.7.cloned.1.call-update) | async-done | bytes 49168 | tf_op jit(solution)/shard_map/reduce_scatter | solution.py:85
  524.1 253.1 %reduce-scatter.11.cloned.1.call-done = f32[3,32,128]{2,1,0:T(8,128)} async-done(((f32[96,32,128]{2,1,0:T(8,128)}), f32[3,32,128]{2,1,0:T(8,128)}) %reduce-scatter.11.cloned.1.call-update) | async-done | bytes 49168 | tf_op jit(solution)/shard_map/reduce_scatter | solution.py:85
  777.2 253.0 %reduce-scatter.9.cloned.1.call-done = f32[3,32,128]{2,1,0:T(8,128)} async-done(((f32[96,32,128]{2,1,0:T(8,128)}), f32[3,32,128]{2,1,0:T(8,128)}) %reduce-scatter.9.cloned.1.call-update) | async-done | bytes 49168 | tf_op jit(solution)/shard_map/reduce_scatter | solution.py:85
  1079.5 6.6 convolution_bitcast_fusion
  1086.1 6.7 convolution_bitcast_fusion.1
  1092.9 3.5 convolution_bitcast_fusion.2
  1096.6 17.9 %all-gather.12.cloned.1.call-done = f32[96,32,128]{2,1,0:T(8,128)} async-done(((f32[3,32,128]{2,1,0:T(8,128)}), f32[96,32,128]{2,1,0:T(8,128)}) %all-gather.12.cloned.1.call-update) | async-done | bytes 1572880 | tf_op jit(solution)/shard_map/all_gather | solution.py:95
  1114.5 5.0 fusion.109
  1119.5 78.5 %all-gather.10.cloned.1.call-done = f32[96,32,128]{2,1,0:T(8,128)} async-done(((f32[3,32,128]{2,1,0:T(8,128)}), f32[96,32,128]{2,1,0:T(8,128)}) %all-gather.10.cloned.1.call-update) | async-done | bytes 1572880 | tf_op jit(solution)/shard_map/all_gather | solution.py:95
  1198.0 5.0 fusion.112
  1203.0 78.7 %all-gather.8.cloned.1.call-done = f32[96,32,128]{2,1,0:T(8,128)} async-done(((f32[3,32,128]{2,1,0:T(8,128)}), f32[96,32,128]{2,1,0:T(8,128)}) %all-gather.8.cloned.1.call-update) | async-done | bytes 1572880 | tf_op jit(solution)/shard_map/all_gather | solution.py:95
  1281.7 5.0 fusion.115
  1286.7 5.5 fusion.90
  1292.2 3.2 fusion.81
  1295.5 3.4 fusion.72
  1298.8 66.5 %all-gather.6.cloned.1.call-done = f32[96,32,128]{2,1,0:T(8,128)} async-done(((f32[3,32,128]{2,1,0:T(8,128)}), f32[96,32,128]{2,1,0:T(8,128)}) %all-gather.6.cloned.1.call-update) | async-done | bytes 1572880 | tf_op jit(solution)/shard_map/all_gather | solution.py:95
  1365.3 5.0 fusion.118
  1370.3 7.8 fusion.96
  1380.4 50.4 %all-gather.14.cloned.1.call-done = f32[8,8,4,32,128]{4,3,2,1,0:T(8,128)} async-done(((f32[1,8,4,32,128]{4,3,2,1,0:T(8,128)}), f32[8,8,4,32,128]{4,3,2,1,0:T(8,128)}) %all-gather.14.cloned.1.call-update) | async-done | bytes 4194320 | tf_op jit(solution)/shard_map/all_gather | solution.py:27
  1430.9 8.8 while.14
  (205 shorter events, 122.1 us)
Async XLA Ops:
  6.5 1073.0 %copy-start = (bf16[27,64,8]{1,2,0:T(8,128)(2,1)S(1)}, bf16[27,64,8]{1,2,0:T(8,128)(2,1)}, u32[]{:S(2)}) copy-start(bf16[27,64,8]{1,2,0:T(8,128)(2,1)} %param.18) | copy-start | bytes 82948
  6.5 264.5 %reduce-scatter.5.cloned.1.call-start = ((), (), s32[]{:S(2)}) async-start(), calls=%async_computation.4 | async-start | bytes 1622016 | tf_op jit(solution)/shard_map/reduce_scatter | solution.py:85
  15.2 509.0 %reduce-scatter.7.cloned.1.call-start = ((), (), s32[]{:S(2)}) async-start(), calls=%async_computation.6 | async-start | bytes 1622016 | tf_op jit(solution)/shard_map/reduce_scatter | solution.py:85
  19.3 8.9 copy-start.1
  21.4 755.8 %reduce-scatter.11.cloned.1.call-start = ((), (), s32[]{:S(2)}) async-start(), calls=%async_computation.10 | async-start | bytes 1622016 | tf_op jit(solution)/shard_map/reduce_scatter | solution.py:85
  28.0 14.9 %copy-start.14 = (f32[4,64]{1,0:T(4,128)S(1)}, f32[4,64]{1,0:T(4,128)}, u32[]{:S(2)}) copy-start(f32[4,64]{1,0:T(4,128)} %param.20) | copy-start | bytes 3076
  28.0 15.0 %copy-start.10 = (f32[4]{0:T(128)S(1)}, f32[4]{0:T(128)}, u32[]{:S(2)}) copy-start(f32[4]{0:T(128)} %param.27) | copy-start | bytes 52
  28.0 15.6 %copy-start.11 = (f32[4]{0:T(128)S(1)}, f32[4]{0:T(128)}, u32[]{:S(2)}) copy-start(f32[4]{0:T(128)} %param.26) | copy-start | bytes 52
  28.0 16.2 %copy-start.13 = (f32[8]{0:T(128)S(1)}, f32[8]{0:T(128)}, u32[]{:S(2)}) copy-start(f32[8]{0:T(128)} %param.22) | copy-start | bytes 100
  28.0 18.7 %copy-start.12 = (f32[4]{0:T(128)S(1)}, f32[4]{0:T(128)}, u32[]{:S(2)}) copy-start(f32[4]{0:T(128)} %param.25) | copy-start | bytes 52
  28.1 19.4 %copy-start.4 = (bf16[4,8,4,32,128]{4,3,2,1,0:T(8,128)(2,1)S(1)}, bf16[4,8,4,32,128]{4,3,2,1,0:T(8,128)(2,1)}, u32[]{:S(2)}) copy-start(bf16[4,8,4,32,128]{4,3,2,1,0:T(8,128)(2,1)} %param.16) | copy-start | bytes 3145732
  28.1 1002.1 %reduce-scatter.9.cloned.1.call-start = ((), (), s32[]{:S(2)}) async-start(), calls=%async_computation.8 | async-start | bytes 1622016 | tf_op jit(solution)/shard_map/reduce_scatter | solution.py:85
  28.3 20.2 %collective-permute-start = (bf16[4,8,1,32,128]{4,1,2,3,0:T(8,128)(2,1)S(1)}, bf16[4,8,1,32,128]{4,1,2,3,0:T(8,128)(2,1)S(1)}, u32[]{:S(2)}, u32[]{:S(2)}) collective-permute-start(bf16[4,8,1,32,128]{4,1,2,3,0:T(8,128)(2,1)S(1)} %copy.1861), channel_id=1, source_target_pairs={{0,1},{1,2},{2,3},{3,4},{4,5},{5,6},{6,7},{7,8},{8,9},{9,10},{10,1... | collective-permute-start | bytes 786440 | tf_op jit(solution)/shard_map/ppermute | solution.py:19
  32.0 17.3 %collective-permute-start.1 = (bf16[4,8,1,32,128]{4,1,2,3,0:T(8,128)(2,1)S(1)}, bf16[4,8,1,32,128]{4,1,2,3,0:T(8,128)(2,1)S(1)}, u32[]{:S(2)}, u32[]{:S(2)}) collective-permute-start(bf16[4,8,1,32,128]{4,1,2,3,0:T(8,128)(2,1)S(1)} %copy.1862), channel_id=1, source_target_pairs={{1,0},{2,1},{3,2},{4,3},{5,4},{6,5},{7,6},{8,7},{9,8},{10,9},{11,1... | collective-permute-start | bytes 786440 | tf_op jit(solution)/shard_map/ppermute | solution.py:20
  42.7 1071.7 %all-gather.12.cloned.1.call-start = ((), (), s32[]{:S(2)}) async-start(), calls=%async_computation.11 | async-start | bytes 1622016 | tf_op jit(solution)/shard_map/all_gather | solution.py:95
  125.9 904.3 %copy-start.9 = (f32[3,32,128]{2,1,0:T(8,128)S(1)}, f32[3,32,128]{2,1,0:T(8,128)}, u32[]{:S(2)}) copy-start(f32[3,32,128]{2,1,0:T(8,128)} %param.24) | copy-start | bytes 147460
  1031.8 166.2 %all-gather.10.cloned.1.call-start = ((), (), s32[]{:S(2)}) async-start(), calls=%async_computation.9 | async-start | bytes 1622016 | tf_op jit(solution)/shard_map/all_gather | solution.py:95
  1050.5 231.2 %all-gather.8.cloned.1.call-start = ((), (), s32[]{:S(2)}) async-start(), calls=%async_computation.7 | async-start | bytes 1622016 | tf_op jit(solution)/shard_map/all_gather | solution.py:95
  1068.9 296.4 %all-gather.6.cloned.1.call-start = ((), (), s32[]{:S(2)}) async-start(), calls=%async_computation.5 | async-start | bytes 1622016 | tf_op jit(solution)/shard_map/all_gather | solution.py:95
  1079.5 13.3 slice-start
  1086.1 6.7 slice-start.1
  1092.8 193.8 %copy-start.8 = (bf16[1,8,4,32,128]{4,3,2,1,0:T(8,128)(2,1)S(1)}, bf16[1,8,4,32,128]{4,3,2,1,0:T(8,128)(2,1)}, u32[]{:S(2)}) copy-start(bf16[1,8,4,32,128]{4,3,2,1,0:T(8,128)(2,1)} %get-tuple-element.231) | copy-start | bytes 786436
  1092.8 193.8 %copy-start.15 = (bf16[8,64]{1,0:T(8,128)(2,1)S(1)}, bf16[8,64]{1,0:T(8,128)(2,1)}, u32[]{:S(2)}) copy-start(bf16[8,64]{1,0:T(8,128)(2,1)} %param.21) | copy-start | bytes 3076
  1092.9 193.8 %copy-start.16 = (f32[64]{0:T(128)S(1)}, f32[64]{0:T(128)}, u32[]{:S(2)}) copy-start(f32[64]{0:T(128)} %param.19) | copy-start | bytes 772
  1096.4 334.5 %all-gather.14.cloned.1.call-start = ((), (), s32[]{:S(2)}) async-start(), calls=%async_computation.12 | async-start | bytes 4718592 | tf_op jit(solution)/shard_map/all_gather | solution.py:27
  1286.7 5.5 copy-start.3
  1286.7 5.5 copy-start.7
  1292.2 3.2 copy-start.2
  1292.2 3.2 copy-start.6
  1295.4 74.9 %copy-start.5 = (bf16[1,8,4,32,128]{4,3,2,1,0:T(8,128)(2,1)S(1)}, bf16[1,8,4,32,128]{4,3,2,1,0:T(8,128)(2,1)}, u32[]{:S(2)}) copy-start(bf16[1,8,4,32,128]{4,3,2,1,0:T(8,128)(2,1)} %get-tuple-element.228) | copy-start | bytes 786436
Sparse Core Ops, SparseCore 0:
  15.3 255.6 reduce-scatter.4
  276.3 247.7 reduce-scatter.6
  529.4 247.7 reduce-scatter.10
  782.4 247.7 reduce-scatter.8
  1033.4 80.9 all-gather.11
  1117.7 80.2 all-gather.9
  1201.4 80.2 all-gather.7
  1285.1 80.2 all-gather.5
  1380.5 50.2 all-gather.13
where the time goes:
time: 1460 us; the launch traced here: 1450 us
  waiting for transfers between devices  1180 us (81%)
  local copies, waits for them, and re-layouts  156 us (11%)
  matrix products  72.7 us (5%)
  other arithmetic  17.8 us (1%)
    reduce_scatter x4, waiting for transfers between devices, on_device(): lax.psum_scatter(PROJ * jnp.einsum('svp,px->svx', table, image, precision...  887 us
    all_gather x4, waiting for transfers between devices, on_device(): lax.all_gather(misfit, 'space', axis=0, tiled=True)  242 us
    another operation x33, local copies, waits for them, and re-layouts, on_device(): patches = jnp.stack(windows, axis=0)  78.8 us
    unnamed x119, local copies, waits for them, and re-layouts  63 us
    all_gather x1, waiting for transfers between devices, prefix(): pieces = lax.all_gather(value, axis)  50.4 us
  transfers between devices with their start and end apart: 11, of which 9 were waited for; matrix products, arithmetic and copies ran while one was open for 14% of the time, Pallas kernels for 0%

commit v1 on v0

v1 whole, which is shorter than its diff:
```python
import functools

import jax
import jax.numpy as jnp
from jax import lax
from jax.experimental import pallas as pl
from jax.experimental.pallas import tpu as pltpu
from jax.sharding import PartitionSpec as P

ANGLES = 180
PROJ = 0.125
NV = 32
NS = 96
WIN = 24
PAD = 168
MSG = 24
F32 = jnp.float32
BF16 = jnp.bfloat16
VMEM = pl.BlockSpec(memory_space=pltpu.VMEM)
SMEM = pl.BlockSpec(memory_space=pltpu.SMEM)


def params(mib):
    return pltpu.CompilerParams(vmem_limit_bytes=mib << 20)


def cost(flops, size, trans=0):
    return pl.CostEstimate(flops=flops, bytes_accessed=size, transcendentals=trans)


def prep_kernel(dec, wk, traj, meas, xp, cum, tot, mm, scr):
    for z in range(4):
        run = None
        for k in range(4):
            acc = None
            for c in range(8):
                v = traj[k, c, z].astype(F32)
                scr[k % 2, c * 32 : (c + 1) * 32, :] = v
                term = dec[c] * v
                acc = term if acc is None else acc + term
            acc = wk[k] * acc
            run = acc if run is None else run + acc
            cum[k, z * 16 : z * 16 + 16, :] = run[:16]
            cum[k, 64 + z * 16 : 64 + z * 16 + 16, :] = run[16:]
            for y in range(0, 32, 2):
                rows = jnp.concatenate(
                    [scr[k % 2, pl.ds(y, 8, stride=32), :], scr[k % 2, pl.ds(y + 1, 8, stride=32), :]], axis=0
                )
                xp[k, z, y * 8 : y * 8 + 16, :] = rows.astype(BF16)
        tot[z * 16 : z * 16 + 16, :] = run[:16]
        tot[64 + z * 16 : 64 + z * 16 + 16, :] = run[16:]
    tot[128:136, :] = jnp.full((8, 128), wk[0] + wk[1] + wk[2] + wk[3], F32)
    mm[...] = jnp.zeros_like(mm)
    for s in range(3):
        x = meas[s]
        tall = jnp.concatenate([x] + [pltpu.roll(x, 128 - 32 * i, 1) for i in range(1, 4)], axis=0)
        mm[pl.ds(s, 32, stride=8), :] = tall.T[:32]


def prep(dec, wk, traj, meas):
    return pl.pallas_call(
        prep_kernel,
        out_shape=(
            jax.ShapeDtypeStruct((4, 4, 256, 128), BF16),
            jax.ShapeDtypeStruct((4, 128, 128), F32),
            jax.ShapeDtypeStruct((136, 128), F32),
            jax.ShapeDtypeStruct((256, 128), F32),
        ),
        in_specs=[SMEM, SMEM, VMEM, VMEM],
        out_specs=(VMEM, VMEM, VMEM, VMEM),
        scratch_shapes=[pltpu.VMEM((2, 256, 128), F32)],
        compiler_params=params(16),
        cost_estimate=cost(4_000_000, 2_600_000),
        name="prep",
    )(dec, wk, traj, meas)


def message_kernel(wk, cum, before, mm, msg, wcol):
    for k in range(4):
        flipped = (cum[k] + before[:128]).T
        for i in range(4):
            msg[pl.ds(4 * i + k, 32, stride=MSG), :] = flipped[32 * i : 32 * i + 32]
    for d in range(32):
        msg[d * MSG + 16 : d * MSG + 24, :] = mm[d * 8 : d * 8 + 8, :]
    sub = lax.broadcasted_iota(jnp.int32, (8, 128), 0) % 4
    w = before[128:136]
    for k in range(4):
        w = w + jnp.where(sub >= k, wk[k], 0.0)
    wcol[...] = w


def message(wk, cum, before, mm):
    return pl.pallas_call(
        message_kernel,
        out_shape=(jax.ShapeDtypeStruct((32 * MSG, 128), F32), jax.ShapeDtypeStruct((8, 128), F32)),
        in_specs=[SMEM, VMEM, VMEM, VMEM],
        out_specs=(VMEM, VMEM),
        compiler_params=params(16),
        cost_estimate=cost(100_000, 900_000),
        name="message",
    )(wk, cum, before, mm)


def conv_kernel(zs, refs_of, ns_in, scale, nscale, *refs):
    ins, rest = refs[:ns_in], refs[ns_in:]
    wt, wo, noise, start = rest[:4]
    extra = rest[4:]
    if len(extra) == 4:
        done, run_ref, tot_ref, scr = extra
    else:
        run_ref, tot_ref, scr = extra
        done = None
    planes = refs_of(ins)
    lane = lax.broadcasted_iota(jnp.int32, (16, 128), 1)
    zero = jnp.zeros((8, 128), BF16)
    for p, plane in enumerate(planes):
        for k in range(4):
            for e in range(3):
                scr[p, e, k, 0:16, :] = jnp.zeros((16, 128), BF16)
                scr[p, e, k, 256:272, :] = jnp.zeros((16, 128), BF16)
            held = zero.astype(F32)
            rows = plane(k)
            for r in range(17):
                if r < 16:
                    cur = rows(r).astype(F32)
                    v = jnp.concatenate([held, cur[:8]], axis=0)
                    held = cur[8:]
                else:
                    v = jnp.concatenate([held, zero.astype(F32)], axis=0)
                left = jnp.where(lane == 0, 0.0, pltpu.roll(v, 1, 1))
                right = jnp.where(lane == 127, 0.0, pltpu.roll(v, 127, 1))
                scr[p, 0, k, r * 16 : r * 16 + 16, :] = left.astype(BF16)
                scr[p, 1, k, r * 16 : r * 16 + 16, :] = v.astype(BF16)
                scr[p, 2, k, r * 16 : r * 16 + 16, :] = right.astype(BF16)
    row = lax.broadcasted_iota(jnp.int32, (16, 256), 0)
    kk = lax.broadcasted_iota(jnp.int32, (16, 256), 1) // 128
    ones = [jnp.where((row < 12) & (row // 3 == kk + 2 * q), 1.0, 0.0).astype(BF16) for q in range(2)]

    def block(step, carry):
        zi, yb = step // 2, step % 2
        first = zi * (1 if zs == (1, 2) else 3)
        zrow = pl.multiple_of(yb * 16, 16)
        acc = [None, None]
        grain = [noise[k, :, zs[0] + zi * (zs[1] - zs[0]), pl.ds(zrow, 16), :].astype(F32) for k in range(4)]
        begin = start[:, zs[0] + zi * (zs[1] - zs[0]), pl.ds(zrow, 16), :]
        for q in range(2):
            for half in range(2):
                hidden = []
                for jj in range(2):
                    top = pl.multiple_of((yb * 4 + half * 2 + jj) * 32, 32)
                    parts = []
                    for e in range(3):
                        for a in range(3):
                            parts.append(
                                jnp.concatenate(
                                    [scr[first + a, e, 2 * q + i, pl.ds(top, 48), :] for i in range(2)], axis=1
                                )
                            )
                    parts.append(ones[q])
                    patch = jnp.concatenate(parts, axis=0)
                    pre = jnp.dot(wt[...], patch, preferred_element_type=F32)
                    hidden.append((pre + pre * jnp.tanh(pre)).astype(BF16))
                eps = jnp.dot(wo[...], jnp.concatenate(hidden, axis=0), preferred_element_type=F32)
                for i in range(2):
                    k = 2 * q + i
                    term = scale[k] * eps[:, i * 128 : i * 128 + 128].reshape(8, 8, 128)
                    term = term + nscale[k] * grain[k][:, half * 8 : half * 8 + 8]
                    acc[half] = term if acc[half] is None else acc[half] + term
                    at = pl.multiple_of(yb * 16 + half * 8, 8)
                    run_ref[k, :, zi, pl.ds(at, 8), :] = acc[half] + begin[:, half * 8 : half * 8 + 8]
        for half in range(2):
            at = pl.multiple_of(yb * 16 + half * 8, 8)
            tot_ref[:, (zs[0] + zi * (zs[1] - zs[0])) if done is not None else zi, pl.ds(at, 8), :] = acc[half]
        return carry

    lax.fori_loop(0, 4, block, 0)
    if done is not None:
        for z in range(2):
            tot_ref[:, 1 + z] = done[:, z]


def conv(zs, planes, scale, nscale, wt, wo, noise, start, done=None):
    inner = zs == (1, 2)

    def refs_of(ins):
        own = ins[0]

        def of(ref, z):
            if z is None:
                return lambda k: (lambda r: ref[k, r * 16 : r * 16 + 16, :])
            return lambda k: (lambda r: ref[k, z, r * 16 : r * 16 + 16, :])

        if inner:
            return [of(own, z) for z in range(4)]
        return [of(ins[1], None), of(own, 0), of(own, 1), of(own, 2), of(own, 3), of(ins[2], None)]

    more = [] if done is None else [done]
    depth = 2 if done is None else 4
    return pl.pallas_call(
        functools.partial(conv_kernel, zs, refs_of, len(planes)),
        out_shape=(
            jax.ShapeDtypeStruct((4, 8, 2, 32, 128), F32),
            jax.ShapeDtypeStruct((8, depth, 32, 128), F32),
        ),
        in_specs=[SMEM, SMEM] + [VMEM] * (len(planes) + 4 + len(more)),
        out_specs=(VMEM, VMEM),
        scratch_shapes=[pltpu.VMEM((4 if inner else 6, 3, 4, 272, 128), BF16)],
        compiler_params=params(40),
        cost_estimate=cost(6_000_000_000, 4_000_000, 2_000_000),
        name="conv_inner" if inner else "conv_outer",
    )(scale, nscale, *planes, wt, wo, noise, start, *more)


def project_kernel(base, off, cosv, sinv, wcol, got, out, table, sino, meas):
    lane = lax.broadcasted_iota(jnp.int32, (16, 128), 1)
    low = lane < 64
    sino[...] = jnp.zeros_like(sino)
    for d in range(32):
        meas[3 * d : 3 * d + 3, :] = got[d * MSG + 16 : d * MSG + 19, :]
    cell = lax.broadcasted_iota(jnp.int32, (8, 256), 1)
    dy = (cell % 16).astype(F32)
    dz = (cell // 16).astype(F32)
    sub = lax.broadcasted_iota(jnp.int32, (8, 256), 0).astype(F32)

    def where_rows(t, v):
        return v * PAD + 24 + base[t * NV + v]

    def forward(zt, carry):
        slab = [got[pl.ds(pl.multiple_of((4 * zt + i) * MSG, 8), 16), :] for i in range(4)]
        flip = [pltpu.roll(s, 64, 1) for s in slab]
        tiles = [
            jnp.concatenate([jnp.where(low, slab[0], flip[1]), jnp.where(low, slab[2], flip[3])], axis=1),
            jnp.concatenate([jnp.where(low, flip[0], slab[1]), jnp.where(low, flip[2], slab[3])], axis=1),
        ]
        for yt in range(2):
            t = zt * 2 + yt
            image = tiles[yt]
            hi = image.astype(BF16)
            lo = (image - hi.astype(F32)).astype(BF16)
            gap = jnp.zeros((16, 256), BF16)
            columns = jnp.concatenate([gap, gap, hi, gap, lo, gap, gap, gap], axis=0)
            columns = jnp.concatenate([columns, columns], axis=1)
            for v in range(0, NV, 2):
                rows = []
                for u in (v, v + 1):
                    at = dy * cosv[u] + dz * sinv[u] + off[t * NV + u]
                    for b in range(3):
                        rows.append(jnp.maximum(0.0, 1.0 - jnp.abs(at - (sub + 8.0 * b))))
                hat = jnp.concatenate(rows, axis=0)
                top = hat.astype(BF16)
                rest = (hat - top.astype(F32)).astype(BF16)
                table[t, v * WIN : (v + 2) * WIN, 0:256] = top
                table[t, v * WIN : (v + 2) * WIN, 256:512] = rest
            sums = lax.dot_general(table[t], columns, (((1,), (1,)), ((), ())), preferred_element_type=F32)
            for v in range(NV):
                at = pl.ds(where_rows(t, v), WIN)
                sino[at, :] = sino[at, :] + sums[v * WIN : (v + 1) * WIN]
        return carry

    lax.fori_loop(0, 8, forward, 0)

    wide = lax.broadcasted_iota(jnp.int32, (NS, 128), 1)

    def misfit(v, carry):
        at = pl.multiple_of(v * PAD, 8)
        rows = sino[pl.ds(at + 24, NS), :]
        rows = PROJ * (rows + pltpu.roll(rows, 96, 1))
        hi = rows.astype(BF16).astype(F32)
        lo = pltpu.roll(rows - hi, 32, 1)
        seen = pltpu.roll(meas[...], lax.rem(128 + 24 - v, 128), 1)
        seen_hi = seen.astype(BF16).astype(F32)
        seen_lo = pltpu.roll(seen - seen_hi, 1, 1)
        spread = jnp.where(
            (wide >= 32) & (wide < 48),
            hi,
            jnp.where(
                (wide >= 64) & (wide < 80),
                lo,
                jnp.where(wide % 32 == 24, seen_hi, jnp.where(wide % 32 == 25, seen_lo, 0.0)),
            ),
        )
        sino[pl.ds(at, 24), :] = jnp.zeros((24, 128), F32)
        sino[pl.ds(at + 24, NS), :] = spread
        sino[pl.ds(at + 120, 48), :] = jnp.zeros((48, 128), F32)
        return carry

    lax.fori_loop(0, NV, misfit, 0)

    upper = lax.broadcasted_iota(jnp.int32, (8, 256), 0) < 4
    wk = jnp.concatenate([wcol[...], wcol[...]], axis=1)

    def backward(zt, carry):
        tiles = []
        for yt in range(2):
            t = zt * 2 + yt
            rows = jnp.concatenate([sino[pl.ds(where_rows(t, v), WIN), :] for v in range(NV)], axis=0)
            sums = lax.dot_general(
                rows.astype(BF16), table[t], (((0,), (0,)), ((), ())), preferred_element_type=F32
            )
            sums = sums[:, :256] + sums[:, 256:]
            pair = []
            for h in range(2):
                seen = [
                    sums[24 + 32 * i : 25 + 32 * i] + sums[25 + 32 * i : 26 + 32 * i] for i in (2 * h, 2 * h + 1)
                ]
                ours = sums[32 + 8 * h : 40 + 8 * h] + sums[64 + 8 * h : 72 + 8 * h]
                pair.append(PROJ * (ours - wk * jnp.where(upper, seen[0], seen[1])))
            tiles.append(jnp.concatenate(pair, axis=0))
        for h in range(2):
            a, b = (tile[:, 128 * h : 128 * h + 128] for tile in tiles)
            at = pl.multiple_of((4 * zt + 2 * h) * 16, 16)
            out[pl.ds(at, 16), :] = jnp.where(low, a, pltpu.roll(b, 64, 1))
            out[pl.ds(at + 16, 16), :] = jnp.where(low, pltpu.roll(a, 64, 1), b)
        return carry

    lax.fori_loop(0, 8, backward, 0)


def project(base, off, cosv, sinv, wcol, got):
    return pl.pallas_call(
        project_kernel,
        out_shape=jax.ShapeDtypeStruct((512, 128), F32),
        in_specs=[SMEM, SMEM, SMEM, SMEM, VMEM, VMEM],
        out_specs=VMEM,
        scratch_shapes=[
            pltpu.VMEM((16, NV * WIN, 512), BF16),
            pltpu.VMEM((NV * PAD, 128), F32),
            pltpu.VMEM((NS, 128), F32),
        ],
        compiler_params=params(40),
        cost_estimate=cost(8_000_000_000, 2_000_000),
        name="project",
    )(base, off, cosv, sinv, wcol, got)


def final_kernel(dec, back, inner, outer, before, new):
    k = pl.program_id(0)
    columns = jnp.concatenate([back[pl.ds(4 * i + k, 32, stride=16), :] for i in range(4)], axis=0)
    cells = columns.T
    for z in range(4):
        guide = jnp.concatenate([cells[z * 16 : z * 16 + 16], cells[64 + z * 16 : 80 + z * 16]], axis=0)
        own = inner[0, :, z - 1] if z in (1, 2) else outer[0, :, z // 3]
        for c in range(8):
            new[0, c, z] = own[c] + before[c, z] - dec[c] * guide


def final(dec, back, inner, outer, before):
    whole = pl.BlockSpec((512, 128), lambda k: (0, 0))
    part = pl.BlockSpec((1, 8, 2, 32, 128), lambda k: (k, 0, 0, 0, 0))
    return pl.pallas_call(
        final_kernel,
        grid=(4,),
        out_shape=jax.ShapeDtypeStruct((4, 8, 4, 32, 128), F32),
        in_specs=[SMEM, whole, part, part, pl.BlockSpec((8, 4, 32, 128), lambda k: (0, 0, 0, 0))],
        out_specs=pl.BlockSpec((1, 8, 4, 32, 128), lambda k: (k, 0, 0, 0, 0)),
        compiler_params=params(24),
        cost_estimate=cost(2_000_000, 5_000_000),
        name="final",
    )(dec, back, inner, outer, before)


def shifted(value, axis, step):
    count = lax.axis_size(axis)
    return lax.ppermute(value, axis, [(i, i + step) for i in range(count) if 0 <= i + step < count])


def earlier(value):
    odd = (lax.axis_index("tm") % 2).astype(F32)
    other = lax.ppermute(value, "tm", [(i, i ^ 1) for i in range(lax.axis_size("tm"))])
    total = value + other
    before = odd * other
    near = shifted(total, "tm", 2)
    far = shifted(total + near, "tm", 4)
    return before + near + far


def conv_tables(conv_weight, conv_bias, step_embed, out_weight):
    w = (conv_weight.astype(F32) * 0.5).reshape(3, 3, 3, 64, 8)
    w = w.transpose(3, 2, 0, 1, 4)
    rows = [jnp.pad(w, ((0, 0), (0, 0), (0, 0), (o, 3 - o), (0, 0))).reshape(64, 432) for o in range(4)]
    bias = 0.5 * (conv_bias[None] + step_embed)
    hi = lax.reduce_precision(bias, 8, 7)
    mid = lax.reduce_precision(bias - hi, 8, 7)
    low = bias - hi - mid
    extra = jnp.stack([hi, mid, low], axis=1).reshape(12, 64).T
    extra = jnp.pad(extra, ((0, 0), (0, 4)))
    wt = jnp.concatenate([jnp.concatenate([r, extra], axis=1) for r in rows], axis=0).astype(BF16)
    wo = out_weight[:, None, None, :] * jnp.eye(8, dtype=BF16)[None, :, :, None]
    return wt, wo.reshape(64, 512)


def windows(angle_index):
    theta = jnp.pi * angle_index.astype(F32) / ANGLES
    cosv, sinv = jnp.cos(theta), jnp.sin(theta)
    tile = jnp.arange(16)
    z0 = (16 * (tile // 2)).astype(F32) - 63.5
    y0 = (16 * (tile % 2)).astype(F32) - 15.5
    corner = y0[:, None] * cosv[None] + z0[:, None] * sinv[None] + 47.5
    least = corner + jnp.minimum(0.0, 15.0 * cosv)[None] + jnp.minimum(0.0, 15.0 * sinv)[None]
    base = jnp.floor(least - 0.001)
    return base.astype(jnp.int32).reshape(512), (corner - base).reshape(512), cosv, sinv


def on_device(
    trajectory,
    noise,
    start,
    conv_weight,
    conv_bias,
    step_embed,
    out_weight,
    decoder,
    angle_index,
    measured,
    step_scale,
    guide_scale,
    noise_scale,
):
    weight = step_scale * guide_scale
    xp, cum, tot, mm = prep(decoder, weight, trajectory, measured)
    up = shifted(xp[:, 3], "space", 1)
    down = shifted(xp[:, 0], "space", -1)
    before_image = earlier(tot)
    wt, wo = conv_tables(conv_weight, conv_bias, step_embed, out_weight)
    base, off, cosv, sinv = windows(angle_index)
    inner, part = conv((1, 2), [xp], step_scale, noise_scale, wt, wo, noise, start)
    outer, own = conv((0, 3), [xp, up, down], step_scale, noise_scale, wt, wo, noise, start, part)
    before = earlier(own)
    msg, wcol = message(weight, cum, before_image, mm)
    got = lax.all_to_all(msg.reshape(32, MSG, 128), "space", 0, 0, tiled=True)
    back = project(base, off, cosv, sinv, wcol, got.reshape(32 * MSG, 128))
    back = lax.all_to_all(back.reshape(32, 16, 128), "space", 0, 0, tiled=True)
    return final(decoder, back.reshape(512, 128), inner, outer, before)


def solution(mesh):
    return jax.shard_map(
        on_device,
        mesh=mesh,
        in_specs=(
            P("tm", None, "space", None, None),
            P("tm", None, "space", None, None),
            P(None, "space", None, None),
            P(),
            P(),
            P("tm", None),
            P(),
            P(),
            P(),
            P("space", None, None),
            P("tm"),
            P("tm"),
            P("tm"),
        ),
        out_specs=P("tm", None, "space", None, None),
        check_vma=False,
    )
```

time: 1460 us -> 133 us (0.09)
  waiting for transfers between devices: 1180 us -> 23.5 us
  local copies, waits for them, and re-layouts: 156 us -> 10.5 us
  matrix products: 72.7 us -> 0 us
  starting transfers between devices: 9.23 us -> 50.5 us
  Pallas kernels: 0 us -> 37 us
    reduce_scatter x4 -> x0, waiting for transfers between devices: 887 us -> none  [on_device(): lax.psum_scatter(PROJ * jnp.einsum('svp,px->svx', table, image, precision...]
    all_gather x5 -> x0, waiting for transfers between devices: 292 us -> none  [the longest x4 242 us: on_device(): lax.all_gather(misfit, 'space', axis=0, tiled=True)]
    another operation x33 -> x3, local copies, waits for them, and re-layouts: 78.8 us -> 0.03 us  [on_device(): patches = jnp.stack(windows, axis=0)]
    dot_general x15 -> x0, matrix products: 72.7 us -> none  [the longest x4 19.9 us: on_device(): jnp.einsum('svp,svx->px', table, lax.all_gather(misfit, 'space', axis=0,...]
    unnamed x119 -> x36, local copies, waits for them, and re-layouts: 63 us -> 7.85 us
    pallas_call x0 -> x6, Pallas kernels: none -> 37 us  [the longest x1 17.3 us: project(): pl.pallas_call(project_kernel, out_shape=jax.ShapeDtypeStruct((512, 128),...]
    all_to_all x0 -> x2, starting transfers between devices: none -> 23.6 us  [the longest x1 12.4 us: on_device(): got = lax.all_to_all(msg.reshape(32, MSG, 128), 'space', 0, 0, tiled=True)]
    ppermute x2 -> x8, starting transfers between devices: 8.08 us -> 27 us  [the longest x6 26.8 us: shifted(): lax.ppermute(value, axis, [(i, i + step) for i in range(count) if 0 <= i...]
  transfers between devices with their start and end apart: 11 -> 10, of which waited for: 9 -> 2; matrix products, arithmetic and copies ran while one was open for 14% -> 8% of each run, Pallas kernels for 0% -> 25%
where the time goes in v1:
time: 133 us; the launch traced here: 130 us
  starting transfers between devices  50.5 us (38%)
  Pallas kernels  37 us (28%)
  waiting for transfers between devices  23.5 us (18%)
  local copies, waits for them, and re-layouts  10.5 us (8%)
  other arithmetic  8.36 us (6%)
    ppermute x6, starting transfers between devices, shifted(): lax.ppermute(value, axis, [(i, i + step) for i in range(count) if 0 <= i...  26.8 us
    pallas_call x1, Pallas kernels, project(): pl.pallas_call(project_kernel, out_shape=jax.ShapeDtypeStruct((512, 128),...  17.3 us
    pallas_call x2, Pallas kernels, conv(): pl.pallas_call(functools.partial(conv_kernel, zs, refs_of, len(planes)),...  13.7 us
    ppermute x6, waiting for transfers between devices, shifted(): lax.ppermute(value, axis, [(i, i + step) for i in range(count) if 0 <= i...  13.5 us
    all_to_all x1, starting transfers between devices, on_device(): got = lax.all_to_all(msg.reshape(32, MSG, 128), 'space', 0, 0, tiled=True)  12.4 us
    all_to_all x1, starting transfers between devices, on_device(): back = lax.all_to_all(back.reshape(32, 16, 128), 'space', 0, 0, tiled=True)  11.1 us
    all_to_all x1, waiting for transfers between devices, on_device(): back = lax.all_to_all(back.reshape(32, 16, 128), 'space', 0, 0, tiled=True)  9.98 us
    unnamed x36, local copies, waits for them, and re-layouts  7.85 us
  transfers between devices with their start and end apart: 10, of which 2 were waited for; matrix products, arithmetic and copies ran while one was open for 8% of the time, Pallas kernels for 25%

profile of v1, /device:TPU:6, one launch (start us, length us, event | category | flops | bytes accessed | tf_op | source)
XLA Modules:
  0.0 130.3 jit_solution(18183211049719304894)
XLA Ops:
  0.0 0.7 mul.108.wk
  0.7 1.2 copy-done
  1.9 0.8 copy-done.3
  2.7 0.7 copy-done.4
  3.4 2.0 %prep.1 = (bf16[4,4,256,128]{3,2,1,0:T(8,128)(2,1)S(1)}, f32[4,128,128]{2,1,0:T(8,128)S(1)}, f32[136,128]{1,0:T(8,128)S(1)}, f32[256,128]{1,0:T(8,128)S(1)}) custom-call(f32[8]{0:T(128)S(1)} %copy-done.4, f32[4]{0:T(128)S(1)} %mul.108.wk, bf16[4,8,4,32,128]{4,3,2,1,0:T(8,128)(2,1)S(1)} %copy-done, f32[3,32,128]{2,1,0:T(8,128)S(1)} %copy-done.3), custom_call_target="tpu_custom_call" | custom-call | flops 4000000 | bytes 2600000 | tf_op jit(solution)/shard_map/prep/pallas_call | solution.py:61
  5.5 1.0 slice_bitcast_fusion
  6.5 3.5 %collective-permute-start.3 = (bf16[4,256,128]{2,1,0:T(8,128)(2,1)}, bf16[4,256,128]{2,1,0:T(8,128)(2,1)S(1)}, u32[]{:S(2)}, u32[]{:S(2)}) collective-permute-start(bf16[4,256,128]{2,1,0:T(8,128)(2,1)} %get-tuple-element.26), channel_id=1, source_target_pairs={{0,1},{1,2},{2,3},{3,4},{4,5},{5,6},{6,7},{7,8},{8,9},{9,10},{10,1... | collective-permute-start | bytes 786440 | tf_op jit(solution)/shard_map/ppermute | solution.py:364
  10.0 4.5 %collective-permute-start.4 = (bf16[4,256,128]{2,1,0:T(8,128)(2,1)}, bf16[4,256,128]{2,1,0:T(8,128)(2,1)S(1)}, u32[]{:S(2)}, u32[]{:S(2)}) collective-permute-start(bf16[4,256,128]{2,1,0:T(8,128)(2,1)} %get-tuple-element.25), channel_id=1, source_target_pairs={{1,0},{2,1},{3,2},{4,3},{5,4},{6,5},{7,6},{8,7},{9,8},{10,9},{11,1... | collective-permute-start | bytes 786440 | tf_op jit(solution)/shard_map/ppermute | solution.py:364
  15.6 3.8 %collective-permute-start.1 = (f32[136,128]{1,0:T(8,128)S(1)}, f32[136,128]{1,0:T(8,128)S(1)}, u32[]{:S(2)}, u32[]{:S(2)}) collective-permute-start(f32[136,128]{1,0:T(8,128)S(1)} %add.128), channel_id=1, source_target_pairs={{0,64},{32,96},{64,128},{96,160},{128,192},{160,224},{1,65},{33,97... | collective-permute-start | bytes 208904 | tf_op jit(solution)/shard_map/ppermute | solution.py:364
  19.4 1.2 copy-done.6
  20.7 1.0 copy-done.8
  21.7 6.7 %conv_inner.1 = (f32[4,8,2,32,128]{4,3,2,1,0:T(8,128)S(1)}, f32[8,2,32,128]{3,2,1,0:T(8,128)S(1)}) custom-call(f32[4]{0:T(128)S(1)} %copy-done.11, f32[4]{0:T(128)S(1)} %copy-done.12, bf16[4,4,256,128]{3,2,1,0:T(8,128)(2,1)S(1)} %get-tuple-element.20.refs_0_, bf16[256,448]{1,0:T(8,128)(2,1)S(1)} %maximum_maximum_fusion.refs_1_.refs_3_, ...), custom_call_target="tpu_custom_call" | custom-call | flops 6000000000 | bytes 4000000 | tf_op jit(solution)/shard_map/conv_inner/pallas_call | solution.py:199
  28.4 0.6 add.130
  29.1 5.8 %collective-permute-start.2 = (f32[136,128]{1,0:T(8,128)}, f32[136,128]{1,0:T(8,128)}, u32[]{:S(2)}, u32[]{:S(2)}) collective-permute-start(f32[136,128]{1,0:T(8,128)} %add.130), channel_id=1, source_target_pairs={{0,128},{32,160},{64,192},{96,224},{1,129},{33,161},{65,193},{97,2... | collective-permute-start | bytes 208904 | tf_op jit(solution)/shard_map/ppermute | solution.py:364
  34.9 0.7 copy-done.9
  35.6 1.2 copy-done.2
  36.8 0.9 copy-done.10
  37.8 7.0 %conv_outer.1 = (f32[4,8,2,32,128]{4,3,2,1,0:T(8,128)S(1)}, f32[8,4,32,128]{3,2,1,0:T(8,128)S(1)}) custom-call(f32[4]{0:T(128)S(1)} %copy-done.11, f32[4]{0:T(128)S(1)} %copy-done.12, bf16[4,4,256,128]{3,2,1,0:T(8,128)(2,1)S(1)} %copy-done.2, bf16[4,256,128]{2,1,0:T(8,128)(2,1)S(1)} %collective-permute-done.3.refs_1_, bf16[4,256,128]{2,1,0:T(8,128)(2,1)S(1)} %copy-done.10, ...), custom_call_target="tpu_custom_call" | custom-call | flops 6000000000 | bytes 4000000 | tf_op jit(solution)/shard_map/conv_outer/pallas_call | solution.py:199
  44.9 0.9 add_add_fusion.1.before
  45.8 1.4 %message.1 = (f32[768,128]{1,0:T(8,128)}, f32[8,128]{1,0:T(8,128)S(1)}) custom-call(f32[4]{0:T(128)S(1)} %mul.108.wk, f32[4,128,128]{2,1,0:T(8,128)S(1)} %get-tuple-element.15.cum, f32[136,128]{1,0:T(8,128)S(1)} %add_add_fusion.1.before, f32[256,128]{1,0:T(8,128)S(1)} %get-tuple-element.17.mm), custom_call_target="tpu_custom_call" | custom-call | flops 100000 | bytes 900000 | tf_op jit(solution)/shard_map/message/pallas_call | solution.py:93
  47.2 12.4 %all-to-all-start = ((f32[32,24,128]{2,1,0:T(8,128)}), f32[32,24,128]{2,1,0:T(8,128)S(1)}, u32[]{:S(2)}, u32[]{:S(2)}) async-start(f32[32,24,128]{2,1,0:T(8,128)} %bitcast), calls=%async_computation | async-start | bytes 786432 | tf_op jit(solution)/shard_map/all_to_all | solution.py:430
  60.3 1.9 %add.134 = f32[8,4,32,128]{3,2,1,0:T(8,128)} add(f32[8,4,32,128]{3,2,1,0:T(8,128)S(1)} %get-tuple-element.24, f32[8,4,32,128]{3,2,1,0:T(8,128)} %collective-permute-done.5) | non-fusion elementwise | flops 131072 | bytes 1572864 | tf_op jit(solution)/shard_map/add | solution.py:370
  62.2 4.4 %collective-permute-start.6 = (f32[8,4,32,128]{3,2,1,0:T(8,128)}, f32[8,4,32,128]{3,2,1,0:T(8,128)S(1)}, u32[]{:S(2)}, u32[]{:S(2)}) collective-permute-start(f32[8,4,32,128]{3,2,1,0:T(8,128)} %add.134), channel_id=1, source_target_pairs={{0,64},{32,96},{64,128},{96,160},{128,192},{160,224},{1,65},{33,97... | collective-permute-start | bytes 1572872 | tf_op jit(solution)/shard_map/ppermute | solution.py:364
  66.8 0.7 add.124
  67.6 13.5 %collective-permute-done.6 = f32[8,4,32,128]{3,2,1,0:T(8,128)S(1)} collective-permute-done((f32[8,4,32,128]{3,2,1,0:T(8,128)}, f32[8,4,32,128]{3,2,1,0:T(8,128)S(1)}, u32[]{:S(2)}, u32[]{:S(2)}) %collective-permute-start.6) | collective-permute-done | bytes 524320 | tf_op jit(solution)/shard_map/ppermute | solution.py:364
  81.2 1.9 %add.136 = f32[8,4,32,128]{3,2,1,0:T(8,128)} add(f32[8,4,32,128]{3,2,1,0:T(8,128)} %add.134, f32[8,4,32,128]{3,2,1,0:T(8,128)S(1)} %collective-permute-done.6) | non-fusion elementwise | flops 131072 | bytes 1572864 | tf_op jit(solution)/shard_map/add | solution.py:373
  83.1 4.8 %collective-permute-start.7 = (f32[8,4,32,128]{3,2,1,0:T(8,128)}, f32[8,4,32,128]{3,2,1,0:T(8,128)}, u32[]{:S(2)}, u32[]{:S(2)}) collective-permute-start(f32[8,4,32,128]{3,2,1,0:T(8,128)} %add.136), channel_id=1, source_target_pairs={{0,128},{32,160},{64,192},{96,224},{1,129},{33,161},{65,193},{97,2... | collective-permute-start | bytes 1572872 | tf_op jit(solution)/shard_map/ppermute | solution.py:364
  87.9 17.3 %project.1 = f32[512,128]{1,0:T(8,128)} custom-call(s32[512]{0:T(512)S(1)} %get-tuple-element.32.base, f32[512]{0:T(512)S(1)} %get-tuple-element.31.off, f32[32]{0:T(128)S(1)} %get-tuple-element.39.cosv, f32[32]{0:T(128)S(1)} %get-tuple-element.38.sinv, f32[8,128]{1,0:T(8,128)S(1)} %get-tuple-element.18.wcol, f32[768,128]{1,0:T(8,128)S(1)} %bitcast.26), custom_call_target="tpu_custom_call" | custom-call | flops 8000000000 | bytes 2000000 | tf_op jit(solution)/shard_map/project/pallas_call | solution.py:320
  105.2 11.1 %all-to-all-start.1 = ((f32[32,16,128]{2,1,0:T(8,128)}), f32[32,16,128]{2,1,0:T(8,128)S(1)}, u32[]{:S(2)}, u32[]{:S(2)}) async-start(f32[32,16,128]{2,1,0:T(8,128)} %bitcast.2), calls=%async_computation.1 | async-start | bytes 524288 | tf_op jit(solution)/shard_map/all_to_all | solution.py:432
  116.3 1.4 %add_add_fusion.before = f32[8,4,32,128]{3,2,1,0:T(8,128)S(1)} fusion(f32[8,4,32,128]{3,2,1,0:T(8,128)} %collective-permute-done.7, f32[8,4,32,128]{3,2,1,0:T(8,128)S(1)} %collective-permute-done.6, f32[8,4,32,128]{3,2,1,0:T(8,128)} %collective-permute-done.5, f32[]{:T(128)S(6)} %convert_element_type.50), kind=kLoop, calls=%fused_computation | loop fusion | flops 393216 | bytes 2097156 | tf_op jit(solution)/shard_map/add | solution.py:374
  117.7 10.0 %all-to-all-done.1 = f32[32,16,128]{2,1,0:T(8,128)S(1)} async-done(((f32[32,16,128]{2,1,0:T(8,128)}), f32[32,16,128]{2,1,0:T(8,128)S(1)}, u32[]{:S(2)}, u32[]{:S(2)}) %all-to-all-start.1) | async-done | bytes 262176 | tf_op jit(solution)/shard_map/all_to_all | solution.py:432
  127.7 2.6 %final.1 = f32[4,8,4,32,128]{4,3,2,1,0:T(8,128)} custom-call(f32[8]{0:T(128)S(1)} %copy-done.5, f32[512,128]{1,0:T(8,128)S(1)} %bitcast.25, f32[4,8,2,32,128]{4,3,2,1,0:T(8,128)S(1)} %get-tuple-element.21.inner, f32[4,8,2,32,128]{4,3,2,1,0:T(8,128)S(1)} %get-tuple-element.23.outer, f32[8,4,32,128]{3,2,1,0:T(8,128)S(1)} %add_add_fusion.before), custom_call_target="tpu_custom_call" | custom-call | flops 2000000 | bytes 5000000 | tf_op jit(solution)/shard_map/final/pallas_call | solution.py:350
  (64 shorter events, 2.2 us)
Async XLA Ops:
  0.0 14.5 %copy-start.17 = (f32[64]{0:T(128)S(1)}, f32[64]{0:T(128)}, u32[]{:S(2)}) copy-start(f32[64]{0:T(128)} %param.17) | copy-start | bytes 772
  0.7 1.2 copy-start
  1.9 0.8 copy-start.3
  2.7 0.7 copy-start.4
  3.4 11.1 %copy-start.15 = (f32[4,64]{1,0:T(4,128)S(1)}, f32[4,64]{1,0:T(4,128)}, u32[]{:S(2)}) copy-start(f32[4,64]{1,0:T(4,128)} %param.18) | copy-start | bytes 3076
  3.4 11.3 %copy-start.13 = (bf16[27,64,8]{1,2,0:T(8,128)(2,1)S(1)}, bf16[27,64,8]{1,2,0:T(8,128)(2,1)}, u32[]{:S(2)}) copy-start(bf16[27,64,8]{1,2,0:T(8,128)(2,1)} %param.16) | copy-start | bytes 82948
  3.4 11.8 %copy-start.14 = (bf16[8,64]{1,0:T(8,128)(2,1)S(1)}, bf16[8,64]{1,0:T(8,128)(2,1)}, u32[]{:S(2)}) copy-start(bf16[8,64]{1,0:T(8,128)(2,1)} %param.19) | copy-start | bytes 3076
  5.4 23.1 %copy-start.1 = (bf16[4,4,256,128]{3,2,1,0:T(8,128)(2,1)}, bf16[4,4,256,128]{3,2,1,0:T(8,128)(2,1)S(1)}, u32[]{:S(2)}) copy-start(bf16[4,4,256,128]{3,2,1,0:T(8,128)(2,1)S(1)} %get-tuple-element.20.refs_0_) | copy-start | bytes 3145732
  5.4 14.1 %copy-start.11 = (f32[4]{0:T(128)S(1)}, f32[4]{0:T(128)}, u32[]{:S(2)}) copy-start(f32[4]{0:T(128)} %scale.3) | copy-start | bytes 52
  5.4 14.0 %copy-start.12 = (f32[4]{0:T(128)S(1)}, f32[4]{0:T(128)}, u32[]{:S(2)}) copy-start(f32[4]{0:T(128)} %nscale.3) | copy-start | bytes 52
  5.4 10.2 %collective-permute-start = (f32[136,128]{1,0:T(8,128)S(1)}, f32[136,128]{1,0:T(8,128)S(1)}, u32[]{:S(2)}, u32[]{:S(2)}) collective-permute-start(f32[136,128]{1,0:T(8,128)S(1)} %get-tuple-element.16), channel_id=1, source_target_pairs={{0,32},{32,0},{64,96},{96,64},{128,160},{160,128},{192,224},{224,1... | collective-permute-start | bytes 208904 | tf_op jit(solution)/shard_map/ppermute | solution.py:369
  6.5 28.4 %collective-permute-start.3 = (bf16[4,256,128]{2,1,0:T(8,128)(2,1)}, bf16[4,256,128]{2,1,0:T(8,128)(2,1)S(1)}, u32[]{:S(2)}, u32[]{:S(2)}) collective-permute-start(bf16[4,256,128]{2,1,0:T(8,128)(2,1)} %get-tuple-element.26), channel_id=1, source_target_pairs={{0,1},{1,2},{2,3},{3,4},{4,5},{5,6},{6,7},{7,8},{8,9},{9,10},{10,1... | collective-permute-start | bytes 786440 | tf_op jit(solution)/shard_map/ppermute | solution.py:364
  10.0 24.9 %collective-permute-start.4 = (bf16[4,256,128]{2,1,0:T(8,128)(2,1)}, bf16[4,256,128]{2,1,0:T(8,128)(2,1)S(1)}, u32[]{:S(2)}, u32[]{:S(2)}) collective-permute-start(bf16[4,256,128]{2,1,0:T(8,128)(2,1)} %get-tuple-element.25), channel_id=1, source_target_pairs={{1,0},{2,1},{3,2},{4,3},{5,4},{6,5},{7,6},{8,7},{9,8},{10,9},{11,1... | collective-permute-start | bytes 786440 | tf_op jit(solution)/shard_map/ppermute | solution.py:364
  15.6 12.8 %collective-permute-start.1 = (f32[136,128]{1,0:T(8,128)S(1)}, f32[136,128]{1,0:T(8,128)S(1)}, u32[]{:S(2)}, u32[]{:S(2)}) collective-permute-start(f32[136,128]{1,0:T(8,128)S(1)} %add.128), channel_id=1, source_target_pairs={{0,64},{32,96},{64,128},{96,160},{128,192},{160,224},{1,65},{33,97... | collective-permute-start | bytes 208904 | tf_op jit(solution)/shard_map/ppermute | solution.py:364
  19.4 1.2 copy-start.6
  20.7 1.0 copy-start.8
  21.7 13.9 %copy-start.7 = (bf16[4,8,4,32,128]{4,3,2,1,0:T(8,128)(2,1)S(1)}, bf16[4,8,4,32,128]{4,3,2,1,0:T(8,128)(2,1)}, u32[]{:S(2)}) copy-start(bf16[4,8,4,32,128]{4,3,2,1,0:T(8,128)(2,1)} %refs_5_.1) | copy-start | bytes 3145732
  29.1 15.8 %collective-permute-start.2 = (f32[136,128]{1,0:T(8,128)}, f32[136,128]{1,0:T(8,128)}, u32[]{:S(2)}, u32[]{:S(2)}) collective-permute-start(f32[136,128]{1,0:T(8,128)} %add.130), channel_id=1, source_target_pairs={{0,128},{32,160},{64,192},{96,224},{1,129},{33,161},{65,193},{97,2... | collective-permute-start | bytes 208904 | tf_op jit(solution)/shard_map/ppermute | solution.py:364
  34.9 0.7 copy-start.9
  35.6 1.2 copy-start.2
  36.8 0.9 copy-start.10
  37.8 21.9 %copy-start.16 = (s32[32]{0:T(128)S(1)}, s32[32]{0:T(128)}, u32[]{:S(2)}) copy-start(s32[32]{0:T(128)} %param.21) | copy-start | bytes 388
  44.8 15.5 %collective-permute-start.5 = (f32[8,4,32,128]{3,2,1,0:T(8,128)S(1)}, f32[8,4,32,128]{3,2,1,0:T(8,128)}, u32[]{:S(2)}, u32[]{:S(2)}) collective-permute-start(f32[8,4,32,128]{3,2,1,0:T(8,128)S(1)} %get-tuple-element.24), channel_id=1, source_target_pairs={{0,32},{32,0},{64,96},{96,64},{128,160},{160,128},{192,224},{224,1... | collective-permute-start | bytes 1572872 | tf_op jit(solution)/shard_map/ppermute | solution.py:369
  47.2 40.6 %all-to-all-start = ((f32[32,24,128]{2,1,0:T(8,128)}), f32[32,24,128]{2,1,0:T(8,128)S(1)}, u32[]{:S(2)}, u32[]{:S(2)}) async-start(f32[32,24,128]{2,1,0:T(8,128)} %bitcast), calls=%async_computation | async-start | bytes 786432 | tf_op jit(solution)/shard_map/all_to_all | solution.py:430
  62.2 18.9 %collective-permute-start.6 = (f32[8,4,32,128]{3,2,1,0:T(8,128)}, f32[8,4,32,128]{3,2,1,0:T(8,128)S(1)}, u32[]{:S(2)}, u32[]{:S(2)}) collective-permute-start(f32[8,4,32,128]{3,2,1,0:T(8,128)} %add.134), channel_id=1, source_target_pairs={{0,64},{32,96},{64,128},{96,160},{128,192},{160,224},{1,65},{33,97... | collective-permute-start | bytes 1572872 | tf_op jit(solution)/shard_map/ppermute | solution.py:364
  83.1 33.3 %collective-permute-start.7 = (f32[8,4,32,128]{3,2,1,0:T(8,128)}, f32[8,4,32,128]{3,2,1,0:T(8,128)}, u32[]{:S(2)}, u32[]{:S(2)}) collective-permute-start(f32[8,4,32,128]{3,2,1,0:T(8,128)} %add.136), channel_id=1, source_target_pairs={{0,128},{32,160},{64,192},{96,224},{1,129},{33,161},{65,193},{97,2... | collective-permute-start | bytes 1572872 | tf_op jit(solution)/shard_map/ppermute | solution.py:364
  105.2 22.5 %copy-start.5 = (f32[8]{0:T(128)S(1)}, f32[8]{0:T(128)}, u32[]{:S(2)}) copy-start(f32[8]{0:T(128)} %dec.3) | copy-start | bytes 100
  105.2 22.5 %all-to-all-start.1 = ((f32[32,16,128]{2,1,0:T(8,128)}), f32[32,16,128]{2,1,0:T(8,128)S(1)}, u32[]{:S(2)}, u32[]{:S(2)}) async-start(f32[32,16,128]{2,1,0:T(8,128)} %bitcast.2), calls=%async_computation.1 | async-start | bytes 524288 | tf_op jit(solution)/shard_map/all_to_all | solution.py:432

commit v2 on v1

--- a/solution.py
+++ b/solution.py
@@ -18,23 +18,45 @@
 BF16 = jnp.bfloat16
 VMEM = pl.BlockSpec(memory_space=pltpu.VMEM)
 SMEM = pl.BlockSpec(memory_space=pltpu.SMEM)
+ANY = pl.BlockSpec(memory_space=pl.ANY)
+HBM = pl.BlockSpec(memory_space=pltpu.HBM)
 
 
 def params(mib):
     return pltpu.CompilerParams(vmem_limit_bytes=mib << 20)
 
 
+def in_hbm(*values):
+    return [pltpu.with_memory_space_constraint(v, pltpu.HBM) for v in values]
+
+
 def cost(flops, size, trans=0):
     return pl.CostEstimate(flops=flops, bytes_accessed=size, transcendentals=trans)
 
 
-def prep_kernel(dec, wk, traj, meas, xp, cum, tot, mm, scr):
+def prep_kernel(
+    dec_from, scale_from, guide_from, source, meas_from, xp, top, bottom, cum, tot, mm, dec, scale, guide, meas, traj, sems, scr
+):
+    small = [(dec_from, dec), (scale_from, scale), (guide_from, guide), (meas_from, meas)]
+    small = [pltpu.make_async_copy(a, b, sems.at[4 + i]) for i, (a, b) in enumerate(small)]
+    copies = [pltpu.make_async_copy(source.at[:, :, z], traj.at[z], sems.at[z]) for z in range(4)]
+    for copy in small + copies:
+        copy.start()
+    for copy in small:
+        copy.wait()
+    wk = [scale[k] * guide[k] for k in range(4)]
+    mm[...] = jnp.zeros_like(mm)
+    for s in range(3):
+        x = meas[s]
+        tall = jnp.concatenate([x] + [pltpu.roll(x, 128 - 32 * i, 1) for i in range(1, 4)], axis=0)
+        mm[pl.ds(s, 32, stride=8), :] = tall.T[:32]
     for z in range(4):
+        copies[z].wait()
         run = None
         for k in range(4):
             acc = None
             for c in range(8):
-                v = traj[k, c, z].astype(F32)
+                v = traj[z, k, c].astype(F32)
                 scr[k % 2, c * 32 : (c + 1) * 32, :] = v
                 term = dec[c] * v
                 acc = term if acc is None else acc + term
@@ -46,74 +68,115 @@
                 rows = jnp.concatenate(
                     [scr[k % 2, pl.ds(y, 8, stride=32), :], scr[k % 2, pl.ds(y + 1, 8, stride=32), :]], axis=0
                 )
-                xp[k, z, y * 8 : y * 8 + 16, :] = rows.astype(BF16)
+                rows = rows.astype(BF16)
+                xp[k, z, y * 8 : y * 8 + 16, :] = rows
+                if z == 0:
+                    bottom[k, y * 8 : y * 8 + 16, :] = rows
+                if z == 3:
+                    top[k, y * 8 : y * 8 + 16, :] = rows
         tot[z * 16 : z * 16 + 16, :] = run[:16]
         tot[64 + z * 16 : 64 + z * 16 + 16, :] = run[16:]
     tot[128:136, :] = jnp.full((8, 128), wk[0] + wk[1] + wk[2] + wk[3], F32)
-    mm[...] = jnp.zeros_like(mm)
-    for s in range(3):
-        x = meas[s]
-        tall = jnp.concatenate([x] + [pltpu.roll(x, 128 - 32 * i, 1) for i in range(1, 4)], axis=0)
-        mm[pl.ds(s, 32, stride=8), :] = tall.T[:32]
-
-
-def prep(dec, wk, traj, meas):
+
+
+def prep(dec, scale, guide, traj, meas):
     return pl.pallas_call(
         prep_kernel,
         out_shape=(
             jax.ShapeDtypeStruct((4, 4, 256, 128), BF16),
+            jax.ShapeDtypeStruct((4, 256, 128), BF16),
+            jax.ShapeDtypeStruct((4, 256, 128), BF16),
             jax.ShapeDtypeStruct((4, 128, 128), F32),
             jax.ShapeDtypeStruct((136, 128), F32),
             jax.ShapeDtypeStruct((256, 128), F32),
         ),
-        in_specs=[SMEM, SMEM, VMEM, VMEM],
-        out_specs=(VMEM, VMEM, VMEM, VMEM),
-        scratch_shapes=[pltpu.VMEM((2, 256, 128), F32)],
+        in_specs=[HBM] * 5,
+        out_specs=(VMEM,) * 6,
+        scratch_shapes=[
+            pltpu.SMEM((8,), F32),
+            pltpu.SMEM((4,), F32),
+            pltpu.SMEM((4,), F32),
+            pltpu.VMEM((3, 32, 128), F32),
+            pltpu.VMEM((4, 4, 8, 32, 128), BF16),
+            pltpu.SemaphoreType.DMA((8,)),
+            pltpu.VMEM((2, 256, 128), F32),
+        ],
         compiler_params=params(16),
         cost_estimate=cost(4_000_000, 2_600_000),
         name="prep",
-    )(dec, wk, traj, meas)
-
-
-def message_kernel(wk, cum, before, mm, msg, wcol):
+    )(*in_hbm(dec, scale, guide, traj, meas))
+
+
+def message_kernel(scale, guide, odd, cum, other, one, two, three, mm, held, msg, passed):
+    wk = [scale[k] * guide[k] for k in range(4)]
+    before = jnp.where(odd[0] == 0, 0.0, other[...]) + (one[...] + two[...] + three[...])
     for k in range(4):
         flipped = (cum[k] + before[:128]).T
         for i in range(4):
             msg[pl.ds(4 * i + k, 32, stride=MSG), :] = flipped[32 * i : 32 * i + 32]
-    for d in range(32):
-        msg[d * MSG + 16 : d * MSG + 24, :] = mm[d * 8 : d * 8 + 8, :]
-    sub = lax.broadcasted_iota(jnp.int32, (8, 128), 0) % 4
+    sub = lax.broadcasted_iota(jnp.int32, (8, 128), 0)
     w = before[128:136]
     for k in range(4):
-        w = w + jnp.where(sub >= k, wk[k], 0.0)
-    wcol[...] = w
-
-
-def message(wk, cum, before, mm):
+        w = w + jnp.where(sub % 4 >= k, wk[k], 0.0)
+    for d in range(32):
+        msg[d * MSG + 16 : d * MSG + 24, :] = jnp.where(sub >= 4, w, mm[d * 8 : d * 8 + 8, :])
+
+
+def message(scale, guide, odd, cum, parts, mm, held):
     return pl.pallas_call(
         message_kernel,
-        out_shape=(jax.ShapeDtypeStruct((32 * MSG, 128), F32), jax.ShapeDtypeStruct((8, 128), F32)),
-        in_specs=[SMEM, VMEM, VMEM, VMEM],
-        out_specs=(VMEM, VMEM),
-        compiler_params=params(16),
+        out_shape=(
+            jax.ShapeDtypeStruct((32 * MSG, 128), F32),
+            jax.ShapeDtypeStruct(held.shape, held.dtype),
+        ),
+        in_specs=[SMEM, SMEM, SMEM] + [VMEM] * 6 + [ANY],
+        out_specs=(VMEM, ANY),
+        input_output_aliases={9: 1},
+        compiler_params=params(8),
         cost_estimate=cost(100_000, 900_000),
         name="message",
-    )(wk, cum, before, mm)
+    )(scale, guide, odd, cum, *parts, mm, held)
 
 
 def conv_kernel(zs, refs_of, ns_in, scale, nscale, *refs):
-    ins, rest = refs[:ns_in], refs[ns_in:]
-    wt, wo, noise, start = rest[:4]
+    ins, rest = list(refs[:ns_in]), refs[ns_in:]
+    wt, wo, noise_from, start_from = rest[:4]
     extra = rest[4:]
-    if len(extra) == 4:
-        done, run_ref, tot_ref, scr = extra
+    done = None
+    fetched = {}
+    if ns_in == 3:
+        done_from, odd, extra = extra[0], extra[1], extra[2:]
+        run_ref, tot_ref, give_ref, scr, noise, start, sems, held_planes, done, more_sems = extra
+        sources = [ins[1], ins[0].at[:, 0], ins[0].at[:, 1], ins[0].at[:, 2], ins[0].at[:, 3], ins[2]]
+        for p, source in enumerate(sources):
+            fetched[p] = pltpu.make_async_copy(source, held_planes.at[p], more_sems.at[p])
+            fetched[p].start()
+        fetched[6] = pltpu.make_async_copy(done_from, done, more_sems.at[6])
+        fetched[6].start()
+        ins = [held_planes]
     else:
-        run_ref, tot_ref, scr = extra
-        done = None
+        run_ref, tot_ref, scr, noise, start, sems = extra
+
+    def put(value, z, rows):
+        if done is None:
+            tot_ref[:, z, rows, :] = value
+        else:
+            low, high = value[:4], value[4:]
+            tot_ref[:, z, rows, :] = jnp.where(odd[0] == 0, low, high)
+            give_ref[:, z, rows, :] = jnp.where(odd[0] == 0, high, low)
+
+    copies = []
+    for i, z in enumerate(zs):
+        copies.append(pltpu.make_async_copy(noise_from.at[:, :, z], noise.at[i], sems.at[0, i]))
+        copies.append(pltpu.make_async_copy(start_from.at[:, z], start.at[i], sems.at[1, i]))
+    for copy in copies:
+        copy.start()
     planes = refs_of(ins)
     lane = lax.broadcasted_iota(jnp.int32, (16, 128), 1)
     zero = jnp.zeros((8, 128), BF16)
     for p, plane in enumerate(planes):
+        if fetched:
+            fetched[p].wait()
         for k in range(4):
             for e in range(3):
                 scr[p, e, k, 0:16, :] = jnp.zeros((16, 128), BF16)
@@ -132,86 +195,101 @@
                 scr[p, 0, k, r * 16 : r * 16 + 16, :] = left.astype(BF16)
                 scr[p, 1, k, r * 16 : r * 16 + 16, :] = v.astype(BF16)
                 scr[p, 2, k, r * 16 : r * 16 + 16, :] = right.astype(BF16)
-    row = lax.broadcasted_iota(jnp.int32, (16, 256), 0)
-    kk = lax.broadcasted_iota(jnp.int32, (16, 256), 1) // 128
-    ones = [jnp.where((row < 12) & (row // 3 == kk + 2 * q), 1.0, 0.0).astype(BF16) for q in range(2)]
+    row = lax.broadcasted_iota(jnp.int32, (16, 512), 0)
+    kk = lax.broadcasted_iota(jnp.int32, (16, 512), 1) // 128
+    ones = jnp.where((row < 12) & (row // 3 == kk), 1.0, 0.0).astype(BF16)
+
+    for copy in copies:
+        copy.wait()
 
     def block(step, carry):
         zi, yb = step // 2, step % 2
         first = zi * (1 if zs == (1, 2) else 3)
         zrow = pl.multiple_of(yb * 16, 16)
-        acc = [None, None]
-        grain = [noise[k, :, zs[0] + zi * (zs[1] - zs[0]), pl.ds(zrow, 16), :].astype(F32) for k in range(4)]
-        begin = start[:, zs[0] + zi * (zs[1] - zs[0]), pl.ds(zrow, 16), :]
-        for q in range(2):
-            for half in range(2):
-                hidden = []
-                for jj in range(2):
-                    top = pl.multiple_of((yb * 4 + half * 2 + jj) * 32, 32)
-                    parts = []
-                    for e in range(3):
-                        for a in range(3):
-                            parts.append(
-                                jnp.concatenate(
-                                    [scr[first + a, e, 2 * q + i, pl.ds(top, 48), :] for i in range(2)], axis=1
-                                )
-                            )
-                    parts.append(ones[q])
-                    patch = jnp.concatenate(parts, axis=0)
-                    pre = jnp.dot(wt[...], patch, preferred_element_type=F32)
-                    hidden.append((pre + pre * jnp.tanh(pre)).astype(BF16))
-                eps = jnp.dot(wo[...], jnp.concatenate(hidden, axis=0), preferred_element_type=F32)
-                for i in range(2):
-                    k = 2 * q + i
-                    term = scale[k] * eps[:, i * 128 : i * 128 + 128].reshape(8, 8, 128)
-                    term = term + nscale[k] * grain[k][:, half * 8 : half * 8 + 8]
-                    acc[half] = term if acc[half] is None else acc[half] + term
-                    at = pl.multiple_of(yb * 16 + half * 8, 8)
-                    run_ref[k, :, zi, pl.ds(at, 8), :] = acc[half] + begin[:, half * 8 : half * 8 + 8]
+        grain = [noise[zi, k, :, pl.ds(zrow, 16), :].astype(F32) for k in range(4)]
+        begin = start[zi, :, pl.ds(zrow, 16), :]
         for half in range(2):
+            hidden = []
+            for jj in range(2):
+                top = pl.multiple_of((yb * 4 + half * 2 + jj) * 32, 32)
+                parts = []
+                for e in range(3):
+                    for a in range(3):
+                        parts.append(
+                            jnp.concatenate([scr[first + a, e, k, pl.ds(top, 48), :] for k in range(4)], axis=1)
+                        )
+                parts.append(ones)
+                patch = jnp.concatenate(parts, axis=0)
+                pre = jnp.dot(wt[...], patch, preferred_element_type=F32)
+                hidden.append((pre + pre * jnp.tanh(pre)).astype(BF16))
+            eps = jnp.dot(wo[...], jnp.concatenate(hidden, axis=0), preferred_element_type=F32)
             at = pl.multiple_of(yb * 16 + half * 8, 8)
-            tot_ref[:, (zs[0] + zi * (zs[1] - zs[0])) if done is not None else zi, pl.ds(at, 8), :] = acc[half]
+            acc = None
+            for k in range(4):
+                term = scale[k] * eps[:, k * 128 : k * 128 + 128].reshape(8, 8, 128)
+                term = term + nscale[k] * grain[k][:, half * 8 : half * 8 + 8]
+                acc = term if acc is None else acc + term
+                run_ref[k, :, zi, pl.ds(at, 8), :] = acc + begin[:, half * 8 : half * 8 + 8]
+            put(acc, zi if done is None else 3 * zi, pl.ds(at, 8))
         return carry
 
     lax.fori_loop(0, 4, block, 0)
     if done is not None:
+        fetched[6].wait()
         for z in range(2):
-            tot_ref[:, 1 + z] = done[:, z]
-
-
-def conv(zs, planes, scale, nscale, wt, wo, noise, start, done=None):
+            put(done[:, z], 1 + z, pl.ds(0, 32))
+
+
+def conv(zs, planes, scale, nscale, wt, wo, noise, start, done=None, odd=None):
     inner = zs == (1, 2)
 
     def refs_of(ins):
         own = ins[0]
 
-        def of(ref, z):
-            if z is None:
-                return lambda k: (lambda r: ref[k, r * 16 : r * 16 + 16, :])
-            return lambda k: (lambda r: ref[k, z, r * 16 : r * 16 + 16, :])
-
-        if inner:
-            return [of(own, z) for z in range(4)]
-        return [of(ins[1], None), of(own, 0), of(own, 1), of(own, 2), of(own, 3), of(ins[2], None)]
-
-    more = [] if done is None else [done]
-    depth = 2 if done is None else 4
+        def of(z):
+            if inner:
+                return lambda k: (lambda r: own[k, z, r * 16 : r * 16 + 16, :])
+            return lambda k: (lambda r: own[z, k, r * 16 : r * 16 + 16, :])
+
+        return [of(z) for z in range(4 if inner else 6)]
+
+    more = [] if done is None else [*in_hbm(done), odd]
+    extra = []
+    if not inner:
+        planes = in_hbm(*planes)
+        extra = [
+            pltpu.VMEM((6, 4, 256, 128), BF16),
+            pltpu.VMEM((8, 2, 32, 128), F32),
+            pltpu.SemaphoreType.DMA((7,)),
+        ]
+    sums = [jax.ShapeDtypeStruct((8, 2, 32, 128), F32)]
+    if done is not None:
+        sums = [jax.ShapeDtypeStruct((4, 4, 32, 128), F32)] * 2
     return pl.pallas_call(
         functools.partial(conv_kernel, zs, refs_of, len(planes)),
         out_shape=(
             jax.ShapeDtypeStruct((4, 8, 2, 32, 128), F32),
-            jax.ShapeDtypeStruct((8, depth, 32, 128), F32),
+            *sums,
         ),
-        in_specs=[SMEM, SMEM] + [VMEM] * (len(planes) + 4 + len(more)),
-        out_specs=(VMEM, VMEM),
-        scratch_shapes=[pltpu.VMEM((4 if inner else 6, 3, 4, 272, 128), BF16)],
-        compiler_params=params(40),
+        in_specs=[SMEM, SMEM]
+        + [VMEM if inner else HBM] * len(planes)
+        + [VMEM, VMEM, HBM, HBM]
+        + [HBM, SMEM][: len(more)],
+        out_specs=(VMEM,) * (1 + len(sums)),
+        scratch_shapes=[
+            pltpu.VMEM((4 if inner else 6, 3, 4, 272, 128), BF16),
+            pltpu.VMEM((2, 4, 8, 32, 128), BF16),
+            pltpu.VMEM((2, 8, 32, 128), F32),
+            pltpu.SemaphoreType.DMA((2, 2)),
+            *extra,
+        ],
+        compiler_params=params(16),
         cost_estimate=cost(6_000_000_000, 4_000_000, 2_000_000),
         name="conv_inner" if inner else "conv_outer",
-    )(scale, nscale, *planes, wt, wo, noise, start, *more)
-
-
-def project_kernel(base, off, cosv, sinv, wcol, got, out, table, sino, meas):
+    )(scale, nscale, *planes, wt, wo, *in_hbm(noise, start), *more)
+
+
+def project_kernel(base, off, cosv, sinv, got, out, table, sino, meas):
     lane = lax.broadcasted_iota(jnp.int32, (16, 128), 1)
     low = lane < 64
     sino[...] = jnp.zeros_like(sino)
@@ -261,7 +339,7 @@
 
     wide = lax.broadcasted_iota(jnp.int32, (NS, 128), 1)
 
-    def misfit(v, carry):
+    def misfit(v):
         at = pl.multiple_of(v * PAD, 8)
         rows = sino[pl.ds(at + 24, NS), :]
         rows = PROJ * (rows + pltpu.roll(rows, 96, 1))
@@ -282,12 +360,18 @@
         sino[pl.ds(at, 24), :] = jnp.zeros((24, 128), F32)
         sino[pl.ds(at + 24, NS), :] = spread
         sino[pl.ds(at + 120, 48), :] = jnp.zeros((48, 128), F32)
+
+    def misfits(group, carry):
+        for v in range(4):
+            misfit(group * 4 + v)
         return carry
 
-    lax.fori_loop(0, NV, misfit, 0)
+    lax.fori_loop(0, NV // 4, misfits, 0)
 
     upper = lax.broadcasted_iota(jnp.int32, (8, 256), 0) < 4
-    wk = jnp.concatenate([wcol[...], wcol[...]], axis=1)
+    wk = got[16:24, :]
+    wk = jnp.where(upper[:, :128], pltpu.roll(wk, 4, 0), wk)
+    wk = jnp.concatenate([wk, wk], axis=1)
 
     def backward(zt, carry):
         tiles = []
@@ -316,47 +400,86 @@
     lax.fori_loop(0, 8, backward, 0)
 
 
-def project(base, off, cosv, sinv, wcol, got):
+def project(base, off, cosv, sinv, got):
     return pl.pallas_call(
         project_kernel,
         out_shape=jax.ShapeDtypeStruct((512, 128), F32),
-        in_specs=[SMEM, SMEM, SMEM, SMEM, VMEM, VMEM],
+        in_specs=[SMEM, SMEM, SMEM, SMEM, VMEM],
         out_specs=VMEM,
         scratch_shapes=[
             pltpu.VMEM((16, NV * WIN, 512), BF16),
             pltpu.VMEM((NV * PAD, 128), F32),
             pltpu.VMEM((NS, 128), F32),
         ],
-        compiler_params=params(40),
+        compiler_params=params(22),
         cost_estimate=cost(8_000_000_000, 2_000_000),
         name="project",
-    )(base, off, cosv, sinv, wcol, got)
-
-
-def final_kernel(dec, back, inner, outer, before, new):
+    )(base, off, cosv, sinv, got)
+
+
+def final_kernel(dec, odd, back, inner, outer, mine, theirs, new):
     k = pl.program_id(0)
     columns = jnp.concatenate([back[pl.ds(4 * i + k, 32, stride=16), :] for i in range(4)], axis=0)
     cells = columns.T
     for z in range(4):
         guide = jnp.concatenate([cells[z * 16 : z * 16 + 16], cells[64 + z * 16 : 80 + z * 16]], axis=0)
-        own = inner[0, :, z - 1] if z in (1, 2) else outer[0, :, z // 3]
         for c in range(8):
-            new[0, c, z] = own[c] + before[c, z] - dec[c] * guide
-
-
-def final(dec, back, inner, outer, before):
+            own = inner[0, c, z - 1] if z in (1, 2) else outer[0, c, z // 3]
+            before = jnp.where(odd[0] == c // 4, mine[c % 4, z], theirs[c % 4, z])
+            new[0, c, z] = own + before - dec[c] * guide
+
+
+def final(dec, odd, back, inner, outer, mine, theirs):
     whole = pl.BlockSpec((512, 128), lambda k: (0, 0))
     part = pl.BlockSpec((1, 8, 2, 32, 128), lambda k: (k, 0, 0, 0, 0))
+    half = pl.BlockSpec((4, 4, 32, 128), lambda k: (0, 0, 0, 0))
     return pl.pallas_call(
         final_kernel,
         grid=(4,),
         out_shape=jax.ShapeDtypeStruct((4, 8, 4, 32, 128), F32),
-        in_specs=[SMEM, whole, part, part, pl.BlockSpec((8, 4, 32, 128), lambda k: (0, 0, 0, 0))],
+        in_specs=[SMEM, SMEM, whole, part, part, half, half],
         out_specs=pl.BlockSpec((1, 8, 4, 32, 128), lambda k: (k, 0, 0, 0, 0)),
-        compiler_params=params(24),
+        compiler_params=params(16),
         cost_estimate=cost(2_000_000, 5_000_000),
         name="final",
-    )(dec, back, inner, outer, before)
+    )(*in_hbm(dec), odd, back, inner, outer, mine, theirs)
+
+
+def add_kernel(a, b, held, out, passed):
+    out[...] = a[...] + b[...]
+
+
+def add_then(a, b, held):
+    return pl.pallas_call(
+        add_kernel,
+        out_shape=(jax.ShapeDtypeStruct(a.shape, F32), jax.ShapeDtypeStruct(held.shape, held.dtype)),
+        in_specs=[VMEM, VMEM, ANY],
+        out_specs=(VMEM, ANY),
+        input_output_aliases={2: 1},
+        compiler_params=params(4),
+        cost_estimate=cost(100_000, 800_000),
+        name="add_then",
+    )(a, b, held)
+
+
+def send_kernel(odd, near, far, keep, given, held, send, mine, passed):
+    first = odd[0] == 0
+    chips = near[...] + far[...]
+    send[...] = chips + jnp.where(first, keep[...], 0.0)
+    mine[...] = chips + jnp.where(first, 0.0, given[...])
+
+
+def send_then(odd, near, far, keep, given, held):
+    return pl.pallas_call(
+        send_kernel,
+        out_shape=(jax.ShapeDtypeStruct(near.shape, F32),) * 2 + (jax.ShapeDtypeStruct(held.shape, held.dtype),),
+        in_specs=[SMEM, VMEM, VMEM, VMEM, VMEM, ANY],
+        out_specs=(VMEM, VMEM, ANY),
+        input_output_aliases={5: 2},
+        compiler_params=params(4),
+        cost_estimate=cost(100_000, 1_500_000),
+        name="send_then",
+    )(odd, near, far, keep, given, held)
 
 
 def shifted(value, axis, step):
@@ -364,14 +487,8 @@
     return lax.ppermute(value, axis, [(i, i + step) for i in range(count) if 0 <= i + step < count])
 
 
-def earlier(value):
-    odd = (lax.axis_index("tm") % 2).astype(F32)
-    other = lax.ppermute(value, "tm", [(i, i ^ 1) for i in range(lax.axis_size("tm"))])
-    total = value + other
-    before = odd * other
-    near = shifted(total, "tm", 2)
-    far = shifted(total + near, "tm", 4)
-    return before + near + far
+def other_core(value):
+    return lax.ppermute(value, "tm", [(i, i ^ 1) for i in range(lax.axis_size("tm"))])
 
 
 def conv_tables(conv_weight, conv_bias, step_embed, out_weight):
@@ -416,21 +533,30 @@
     guide_scale,
     noise_scale,
 ):
-    weight = step_scale * guide_scale
-    xp, cum, tot, mm = prep(decoder, weight, trajectory, measured)
-    up = shifted(xp[:, 3], "space", 1)
-    down = shifted(xp[:, 0], "space", -1)
-    before_image = earlier(tot)
+    odd = (lax.axis_index("tm") % 2).reshape(1)
+    xp, top, bottom, cum, tot, mm = prep(decoder, step_scale, guide_scale, trajectory, measured)
+    up = shifted(top, "space", 1)
+    down = shifted(bottom, "space", -1)
+    other = other_core(tot)
     wt, wo = conv_tables(conv_weight, conv_bias, step_embed, out_weight)
     base, off, cosv, sinv = windows(angle_index)
     inner, part = conv((1, 2), [xp], step_scale, noise_scale, wt, wo, noise, start)
-    outer, own = conv((0, 3), [xp, up, down], step_scale, noise_scale, wt, wo, noise, start, part)
-    before = earlier(own)
-    msg, wcol = message(weight, cum, before_image, mm)
+    both = tot + other
+    parts = [other] + [shifted(both, "tm", 2 * i) for i in (1, 2, 3)]
+    outer, keep, give = conv((0, 3), [xp, up, down], step_scale, noise_scale, wt, wo, noise, start, part, odd)
+    msg, give = message(step_scale, guide_scale, odd, cum, parts, mm, give)
+    given = other_core(give)
+    chip, msg = add_then(keep, given, msg)
+    near = shifted(chip, "tm", 2)
     got = lax.all_to_all(msg.reshape(32, MSG, 128), "space", 0, 0, tiled=True)
-    back = project(base, off, cosv, sinv, wcol, got.reshape(32 * MSG, 128))
+    two, got = add_then(chip, near, got)
+    far = shifted(two, "tm", 4)
+    back = project(base, off, cosv, sinv, got.reshape(32 * MSG, 128))
+    send, mine, back = send_then(odd, near, far, keep, given, back)
+    (send,) = in_hbm(send)
+    theirs = other_core(send)
     back = lax.all_to_all(back.reshape(32, 16, 128), "space", 0, 0, tiled=True)
-    return final(decoder, back.reshape(512, 128), inner, outer, before)
+    return final(decoder, odd, back.reshape(512, 128), inner, outer, mine, theirs)
 
 
 def solution(mesh):

time: 133 us -> 117 us (0.88)
  other arithmetic: 8.36 us -> 3.13 us
  local copies, waits for them, and re-layouts: 10.5 us -> 5.42 us
  starting transfers between devices: 50.5 us -> 45.9 us
    add x6 -> x1, other arithmetic: 6.75 us -> 0.01 us  [on_device(): both = tot + other]
    unnamed x36 -> x18, local copies, waits for them, and re-layouts: 7.85 us -> 1.42 us
    ppermute x6 -> x7, waiting for transfers between devices: 13.5 us -> 8.02 us  [shifted(): lax.ppermute(value, axis, [(i, i + step) for i in range(count) if 0 <= i...]
    ppermute x2 -> x3, waiting for transfers between devices: 0.01 us -> 3.27 us  [other_core(): lax.ppermute(value, 'tm', [(i, i ^ 1) for i in range(lax.axis_size('tm'))])]
    ppermute x6 -> x7, starting transfers between devices: 26.8 us -> 24 us  [shifted(): lax.ppermute(value, axis, [(i, i + step) for i in range(count) if 0 <= i...]
    pallas_call x1, Pallas kernels: 17.3 us -> 15.4 us  [project(): pl.pallas_call(project_kernel, out_shape=jax.ShapeDtypeStruct((512, 128),...]
    all_to_all x1, starting transfers between devices: 11.1 us -> 9.3 us  [on_device(): back = lax.all_to_all(back.reshape(32, 16, 128), 'space', 0, 0, tiled=True)]
    add x4, local copies, waits for them, and re-layouts: 0.83 us -> 2.6 us  [windows(): corner + jnp.minimum(0.0, 15.0 * cosv)[None]]
  transfers between devices with their start and end apart: 10 -> 12, of which waited for: 2 -> 5; matrix products, arithmetic and copies ran while one was open for 8% -> 6% of each run, Pallas kernels for 25% -> 26%
where the time goes in v2:
time: 117 us; the launch traced here: 114 us
  starting transfers between devices  45.9 us (39%)
  Pallas kernels  36.9 us (32%)
  waiting for transfers between devices  22.6 us (19%)
  local copies, waits for them, and re-layouts  5.42 us (5%)
  other arithmetic  3.13 us (3%)
    ppermute x7, starting transfers between devices, shifted(): lax.ppermute(value, axis, [(i, i + step) for i in range(count) if 0 <= i...  24 us
    pallas_call x1, Pallas kernels, project(): pl.pallas_call(project_kernel, out_shape=jax.ShapeDtypeStruct((512, 128),...  15.4 us
    pallas_call x2, Pallas kernels, conv(): pl.pallas_call(functools.partial(conv_kernel, zs, refs_of, len(planes)),...  13.8 us
    all_to_all x1, starting transfers between devices, on_device(): got = lax.all_to_all(msg.reshape(32, MSG, 128), 'space', 0, 0, tiled=True)  12.4 us
    all_to_all x1, waiting for transfers between devices, on_device(): back = lax.all_to_all(back.reshape(32, 16, 128), 'space', 0, 0, tiled=True)  9.56 us
    all_to_all x1, starting transfers between devices, on_device(): back = lax.all_to_all(back.reshape(32, 16, 128), 'space', 0, 0, tiled=True)  9.3 us
    ppermute x7, waiting for transfers between devices, shifted(): lax.ppermute(value, axis, [(i, i + step) for i in range(count) if 0 <= i...  8.02 us
    ppermute x3, waiting for transfers between devices, other_core(): lax.ppermute(value, 'tm', [(i, i ^ 1) for i in range(lax.axis_size('tm'))])  3.27 us
  transfers between devices with their start and end apart: 12, of which 5 were waited for; matrix products, arithmetic and copies ran while one was open for 6% of the time, Pallas kernels for 26%

profile of v2, /device:TPU:6, one launch (start us, length us, event | category | flops | bytes accessed | tf_op | source)
XLA Modules:
  0.0 114.2 jit_solution(3724637947350888318)
XLA Ops:
  0.0 3.1 %prep.1 = (bf16[4,4,256,128]{3,2,1,0:T(8,128)(2,1)S(1)}, bf16[4,256,128]{2,1,0:T(8,128)(2,1)}, bf16[4,256,128]{2,1,0:T(8,128)(2,1)S(1)}, f32[4,128,128]{2,1,0:T(...) custom-call(f32[8]{0:T(128)} %dec.1, f32[4]{0:T(128)} %scale.5, f32[4]{0:T(128)} %guide.1, ...), custom_call_target="tpu_custom_call" | custom-call | flops 4000000 | bytes 2600000 | tf_op jit(solution)/shard_map/prep/pallas_call | solution.py:83
  3.1 3.5 %collective-permute-start = (bf16[4,256,128]{2,1,0:T(8,128)(2,1)}, bf16[4,256,128]{2,1,0:T(8,128)(2,1)}, u32[]{:S(2)}, u32[]{:S(2)}) collective-permute-start(bf16[4,256,128]{2,1,0:T(8,128)(2,1)} %get-tuple-element.26), channel_id=1, source_target_pairs={{0,1},{1,2},{2,3},{3,4},{4,5},{5,6},{6,7},{7,8},{8,9},{9,10},{10,1... | collective-permute-start | bytes 786440 | tf_op jit(solution)/shard_map/ppermute | solution.py:487
  6.6 4.5 %collective-permute-start.1 = (bf16[4,256,128]{2,1,0:T(8,128)(2,1)S(1)}, bf16[4,256,128]{2,1,0:T(8,128)(2,1)}, u32[]{:S(2)}, u32[]{:S(2)}) collective-permute-start(bf16[4,256,128]{2,1,0:T(8,128)(2,1)S(1)} %get-tuple-element.27), channel_id=1, source_target_pairs={{1,0},{2,1},{3,2},{4,3},{5,4},{6,5},{7,6},{8,7},{9,8},{10,9},{11,1... | collective-permute-start | bytes 786440 | tf_op jit(solution)/shard_map/ppermute | solution.py:487
  11.2 0.7 reduce-precision_bitcast_fusion.1
  12.1 0.8 multiply_convert_fusion
  13.5 0.1 mul.90.refs_2_.refs_4_
  13.8 6.6 %conv_inner.1 = (f32[4,8,2,32,128]{4,3,2,1,0:T(8,128)S(1)}, f32[8,2,32,128]{3,2,1,0:T(8,128)S(1)}) custom-call(f32[4]{0:T(128)S(1)} %copy-done, f32[4]{0:T(128)S(1)} %copy-done.4, bf16[4,4,256,128]{3,2,1,0:T(8,128)(2,1)S(1)} %get-tuple-element.25.refs_0_, bf16[256,448]{1,0:T(8,128)(2,1)S(1)} %maximum_maximum_fusion.refs_1_.refs_3_, ...), custom_call_target="tpu_custom_call" | custom-call | flops 6000000000 | bytes 4000000 | tf_op jit(solution)/shard_map/conv_inner/pallas_call | solution.py:268
  20.4 0.7 copy-done.5
  21.1 3.8 %collective-permute-start.3 = (f32[136,128]{1,0:T(8,128)S(1)}, f32[136,128]{1,0:T(8,128)S(1)}, u32[]{:S(2)}, u32[]{:S(2)}) collective-permute-start(f32[136,128]{1,0:T(8,128)S(1)} %add.97), channel_id=1, source_target_pairs={{0,64},{32,96},{64,128},{96,160},{128,192},{160,224},{1,65},{33,97... | collective-permute-start | bytes 208904 | tf_op jit(solution)/shard_map/ppermute | solution.py:487
  24.9 5.2 %collective-permute-start.4 = (f32[136,128]{1,0:T(8,128)S(1)}, f32[136,128]{1,0:T(8,128)S(1)}, u32[]{:S(2)}, u32[]{:S(2)}) collective-permute-start(f32[136,128]{1,0:T(8,128)S(1)} %add.97), channel_id=1, source_target_pairs={{0,128},{32,160},{64,192},{96,224},{1,129},{33,161},{65,193},{97,2... | collective-permute-start | bytes 208904 | tf_op jit(solution)/shard_map/ppermute | solution.py:487
  30.1 1.3 %collective-permute-start.5 = (f32[136,128]{1,0:T(8,128)S(1)}, f32[136,128]{1,0:T(8,128)S(1)}, u32[]{:S(2)}, u32[]{:S(2)}) collective-permute-start(f32[136,128]{1,0:T(8,128)S(1)} %add.97), channel_id=1, source_target_pairs={{0,192},{32,224},{1,193},{33,225},{2,194},{34,226},{3,195},{35,227... | collective-permute-start | bytes 208904 | tf_op jit(solution)/shard_map/ppermute | solution.py:487
  31.5 7.2 %conv_outer.1 = (f32[4,8,2,32,128]{4,3,2,1,0:T(8,128)S(1)}, f32[4,4,32,128]{3,2,1,0:T(8,128)S(1)}, f32[4,4,32,128]{3,2,1,0:T(8,128)S(1)}) custom-call(f32[4]{0:T(128)S(1)} %copy-done, f32[4]{0:T(128)S(1)} %copy-done.4, bf16[4,4,256,128]{3,2,1,0:T(8,128)(2,1)} %copy-done.2, bf16[4,256,128]{2,1,0:T(8,128)(2,1)} %collective-permute-done.refs_1_, ...), custom_call_target="tpu_custom_call" | custom-call | flops 6000000000 | bytes 4000000 | tf_op jit(solution)/shard_map/conv_outer/pallas_call | solution.py:268
  38.7 1.4 %message.1 = (f32[768,128]{1,0:T(8,128)}, f32[4,4,32,128]{3,2,1,0:T(8,128)S(1)}) custom-call(f32[4]{0:T(128)S(1)} %copy-done, f32[4]{0:T(128)S(1)} %copy-done.1, s32[1]{0:T(128)} %bitcast.refs_8_.odd, f32[4,128,128]{2,1,0:T(8,128)S(1)} %get-tuple-element.30.cum, f32[136,128]{1,0:T(8,128)S(1)} %collective-permute-done.2.other, ...), custom_call_target="tpu_custom_call", output_to_operand_aliasing={{1}: (9, {})} | custom-call | flops 100000 | bytes 900000 | tf_op jit(solution)/shard_map/message/pallas_call | solution.py:126
  40.2 1.5 %collective-permute-done.6.b.given = f32[4,4,32,128]{3,2,1,0:T(8,128)S(1)} collective-permute-done((f32[4,4,32,128]{3,2,1,0:T(8,128)S(1)}, f32[4,4,32,128]{3,2,1,0:T(8,128)S(1)}, u32[]{:S(2)}, u32[]{:S(2)}) %collective-permute-start.6) | collective-permute-done | bytes 262176 | tf_op jit(solution)/shard_map/ppermute | solution.py:491
  41.7 12.4 %all-to-all-start = ((f32[32,24,128]{2,1,0:T(8,128)}), f32[32,24,128]{2,1,0:T(8,128)S(1)}, u32[]{:S(2)}, u32[]{:S(2)}) async-start(f32[32,24,128]{2,1,0:T(8,128)} %bitcast.11), calls=%async_computation | async-start | bytes 786432 | tf_op jit(solution)/shard_map/all_to_all | solution.py:551
  54.2 0.6 multiply_minimum_fusion.1
  54.8 1.5 %collective-permute-start.7 = (f32[4,4,32,128]{3,2,1,0:T(8,128)S(1)}, f32[4,4,32,128]{3,2,1,0:T(8,128)S(1)}, u32[]{:S(2)}, u32[]{:S(2)}) collective-permute-start(f32[4,4,32,128]{3,2,1,0:T(8,128)S(1)} %get-tuple-element.36.a), channel_id=1, source_target_pairs={{0,64},{32,96},{64,128},{96,160},{128,192},{160,224},{1,65},{33,97... | collective-permute-start | bytes 786440 | tf_op jit(solution)/shard_map/ppermute | solution.py:487
  56.4 0.7 add.102
  57.0 0.6 add.103
  57.6 0.7 add.104
  58.3 0.7 add.106
  59.0 0.7 add.107
  59.7 0.7 fusion.10
  60.4 8.0 %collective-permute-done.7.b.near = f32[4,4,32,128]{3,2,1,0:T(8,128)S(1)} collective-permute-done((f32[4,4,32,128]{3,2,1,0:T(8,128)S(1)}, f32[4,4,32,128]{3,2,1,0:T(8,128)S(1)}, u32[]{:S(2)}, u32[]{:S(2)}) %collective-permute-start.7) | collective-permute-done | bytes 262176 | tf_op jit(solution)/shard_map/ppermute | solution.py:487
  68.4 1.7 %all-to-all-done.held = f32[32,24,128]{2,1,0:T(8,128)S(1)} async-done(((f32[32,24,128]{2,1,0:T(8,128)}), f32[32,24,128]{2,1,0:T(8,128)S(1)}, u32[]{:S(2)}, u32[]{:S(2)}) %all-to-all-start) | async-done | bytes 393248 | tf_op jit(solution)/shard_map/all_to_all | solution.py:551
  70.1 4.2 %collective-permute-start.8 = (f32[4,4,32,128]{3,2,1,0:T(8,128)S(1)}, f32[4,4,32,128]{3,2,1,0:T(8,128)S(1)}, u32[]{:S(2)}, u32[]{:S(2)}) collective-permute-start(f32[4,4,32,128]{3,2,1,0:T(8,128)S(1)} %get-tuple-element.38), channel_id=1, source_target_pairs={{0,128},{32,160},{64,192},{96,224},{1,129},{33,161},{65,193},{97,2... | collective-permute-start | bytes 786440 | tf_op jit(solution)/shard_map/ppermute | solution.py:487
  74.3 15.4 %project.1.held = f32[512,128]{1,0:T(8,128)} custom-call(s32[512]{0:T(512)S(1)} %get-tuple-element.50.base, f32[512]{0:T(512)S(1)} %get-tuple-element.49.off, f32[32]{0:T(128)S(1)} %get-tuple-element.57.cosv, f32[32]{0:T(128)S(1)} %get-tuple-element.56.sinv, f32[768,128]{1,0:T(8,128)S(1)} %bitcast.22), custom_call_target="tpu_custom_call" | custom-call | flops 8000000000 | bytes 2000000 | tf_op jit(solution)/shard_map/project/pallas_call | solution.py:404
  89.9 0.7 copy-done.3
  90.6 9.3 %all-to-all-start.1 = ((f32[32,16,128]{2,1,0:T(8,128)}), f32[32,16,128]{2,1,0:T(8,128)S(1)}, u32[]{:S(2)}, u32[]{:S(2)}) async-start(f32[32,16,128]{2,1,0:T(8,128)} %bitcast.13), calls=%async_computation.1 | async-start | bytes 524288 | tf_op jit(solution)/shard_map/all_to_all | solution.py:558
  100.0 1.7 %collective-permute-done.9.theirs = f32[4,4,32,128]{3,2,1,0:T(8,128)S(1)} collective-permute-done((f32[4,4,32,128]{3,2,1,0:T(8,128)}, f32[4,4,32,128]{3,2,1,0:T(8,128)S(1)}, u32[]{:S(2)}, u32[]{:S(2)}) %collective-permute-start.9) | collective-permute-done | bytes 262176 | tf_op jit(solution)/shard_map/ppermute | solution.py:491
  101.7 9.6 %all-to-all-done.1 = f32[32,16,128]{2,1,0:T(8,128)S(1)} async-done(((f32[32,16,128]{2,1,0:T(8,128)}), f32[32,16,128]{2,1,0:T(8,128)S(1)}, u32[]{:S(2)}, u32[]{:S(2)}) %all-to-all-start.1) | async-done | bytes 262176 | tf_op jit(solution)/shard_map/all_to_all | solution.py:558
  111.3 3.0 %final.1 = f32[4,8,4,32,128]{4,3,2,1,0:T(8,128)} custom-call(f32[8]{0:T(128)} %dec.1, s32[1]{0:T(128)} %bitcast.refs_8_.odd, f32[512,128]{1,0:T(8,128)S(1)} %bitcast.23, f32[4,8,2,32,128]{4,3,2,1,0:T(8,128)S(1)} %get-tuple-element.41.inner, f32[4,8,2,32,128]{4,3,2,1,0:T(8,128)S(1)} %get-tuple-element.42.outer, f32[4,4,32,128]{3,2,1,0:T(8,128)S(1)} %get-tuple-element.43.mine, ...), custom_call_target="tpu_custom_call" | custom-call | flops 2000000 | bytes 5000000 | tf_op jit(solution)/shard_map/final/pallas_call | solution.py:436
  (46 shorter events, 1.3 us)
Async XLA Ops:
  0.0 13.8 %copy-start = (f32[4]{0:T(128)S(1)}, f32[4]{0:T(128)}, u32[]{:S(2)}) copy-start(f32[4]{0:T(128)} %scale.5) | copy-start | bytes 52
  0.0 13.4 %copy-start.7 = (bf16[8,64]{1,0:T(8,128)(2,1)S(1)}, bf16[8,64]{1,0:T(8,128)(2,1)}, u32[]{:S(2)}) copy-start(bf16[8,64]{1,0:T(8,128)(2,1)} %param.19) | copy-start | bytes 3076
  0.0 13.8 %copy-start.4 = (f32[4]{0:T(128)S(1)}, f32[4]{0:T(128)}, u32[]{:S(2)}) copy-start(f32[4]{0:T(128)} %nscale.3) | copy-start | bytes 52
  3.1 17.2 %copy-start.2 = (bf16[4,4,256,128]{3,2,1,0:T(8,128)(2,1)}, bf16[4,4,256,128]{3,2,1,0:T(8,128)(2,1)S(1)}, u32[]{:S(2)}) copy-start(bf16[4,4,256,128]{3,2,1,0:T(8,128)(2,1)S(1)} %get-tuple-element.25.refs_0_) | copy-start | bytes 3145732
  3.1 28.3 %collective-permute-start = (bf16[4,256,128]{2,1,0:T(8,128)(2,1)}, bf16[4,256,128]{2,1,0:T(8,128)(2,1)}, u32[]{:S(2)}, u32[]{:S(2)}) collective-permute-start(bf16[4,256,128]{2,1,0:T(8,128)(2,1)} %get-tuple-element.26), channel_id=1, source_target_pairs={{0,1},{1,2},{2,3},{3,4},{4,5},{5,6},{6,7},{7,8},{8,9},{9,10},{10,1... | collective-permute-start | bytes 786440 | tf_op jit(solution)/shard_map/ppermute | solution.py:487
  6.6 24.8 %collective-permute-start.1 = (bf16[4,256,128]{2,1,0:T(8,128)(2,1)S(1)}, bf16[4,256,128]{2,1,0:T(8,128)(2,1)}, u32[]{:S(2)}, u32[]{:S(2)}) collective-permute-start(bf16[4,256,128]{2,1,0:T(8,128)(2,1)S(1)} %get-tuple-element.27), channel_id=1, source_target_pairs={{1,0},{2,1},{3,2},{4,3},{5,4},{6,5},{7,6},{8,7},{9,8},{10,9},{11,1... | collective-permute-start | bytes 786440 | tf_op jit(solution)/shard_map/ppermute | solution.py:487
  11.1 10.0 %collective-permute-start.2 = (f32[136,128]{1,0:T(8,128)S(1)}, f32[136,128]{1,0:T(8,128)S(1)}, u32[]{:S(2)}, u32[]{:S(2)}) collective-permute-start(f32[136,128]{1,0:T(8,128)S(1)} %get-tuple-element.31), channel_id=1, source_target_pairs={{0,32},{32,0},{64,96},{96,64},{128,160},{160,128},{192,224},{224,1... | collective-permute-start | bytes 208904 | tf_op jit(solution)/shard_map/ppermute | solution.py:491
  20.4 0.7 copy-start.5
  21.1 17.6 %collective-permute-start.3 = (f32[136,128]{1,0:T(8,128)S(1)}, f32[136,128]{1,0:T(8,128)S(1)}, u32[]{:S(2)}, u32[]{:S(2)}) collective-permute-start(f32[136,128]{1,0:T(8,128)S(1)} %add.97), channel_id=1, source_target_pairs={{0,64},{32,96},{64,128},{96,160},{128,192},{160,224},{1,65},{33,97... | collective-permute-start | bytes 208904 | tf_op jit(solution)/shard_map/ppermute | solution.py:487
  24.9 13.7 %collective-permute-start.4 = (f32[136,128]{1,0:T(8,128)S(1)}, f32[136,128]{1,0:T(8,128)S(1)}, u32[]{:S(2)}, u32[]{:S(2)}) collective-permute-start(f32[136,128]{1,0:T(8,128)S(1)} %add.97), channel_id=1, source_target_pairs={{0,128},{32,160},{64,192},{96,224},{1,129},{33,161},{65,193},{97,2... | collective-permute-start | bytes 208904 | tf_op jit(solution)/shard_map/ppermute | solution.py:487
  30.1 8.6 %collective-permute-start.5 = (f32[136,128]{1,0:T(8,128)S(1)}, f32[136,128]{1,0:T(8,128)S(1)}, u32[]{:S(2)}, u32[]{:S(2)}) collective-permute-start(f32[136,128]{1,0:T(8,128)S(1)} %add.97), channel_id=1, source_target_pairs={{0,192},{32,224},{1,193},{33,225},{2,194},{34,226},{3,195},{35,227... | collective-permute-start | bytes 208904 | tf_op jit(solution)/shard_map/ppermute | solution.py:487
  31.5 7.3 %copy-start.1 = (f32[4]{0:T(128)S(1)}, f32[4]{0:T(128)}, u32[]{:S(2)}) copy-start(f32[4]{0:T(128)} %guide.1) | copy-start | bytes 52
  38.7 15.5 %copy-start.8 = (s32[32]{0:T(128)S(1)}, s32[32]{0:T(128)}, u32[]{:S(2)}) copy-start(s32[32]{0:T(128)} %param.21) | copy-start | bytes 388
  40.2 1.5 %collective-permute-start.6 = (f32[4,4,32,128]{3,2,1,0:T(8,128)S(1)}, f32[4,4,32,128]{3,2,1,0:T(8,128)S(1)}, u32[]{:S(2)}, u32[]{:S(2)}) collective-permute-start(f32[4,4,32,128]{3,2,1,0:T(8,128)S(1)} %get-tuple-element.34), channel_id=1, source_target_pairs={{0,32},{32,0},{64,96},{96,64},{128,160},{160,128},{192,224},{224,1... | collective-permute-start | bytes 786440 | tf_op jit(solution)/shard_map/ppermute | solution.py:491
  41.7 28.4 %all-to-all-start = ((f32[32,24,128]{2,1,0:T(8,128)}), f32[32,24,128]{2,1,0:T(8,128)S(1)}, u32[]{:S(2)}, u32[]{:S(2)}) async-start(f32[32,24,128]{2,1,0:T(8,128)} %bitcast.11), calls=%async_computation | async-start | bytes 786432 | tf_op jit(solution)/shard_map/all_to_all | solution.py:551
  54.8 13.5 %collective-permute-start.7 = (f32[4,4,32,128]{3,2,1,0:T(8,128)S(1)}, f32[4,4,32,128]{3,2,1,0:T(8,128)S(1)}, u32[]{:S(2)}, u32[]{:S(2)}) collective-permute-start(f32[4,4,32,128]{3,2,1,0:T(8,128)S(1)} %get-tuple-element.36.a), channel_id=1, source_target_pairs={{0,64},{32,96},{64,128},{96,160},{128,192},{160,224},{1,65},{33,97... | collective-permute-start | bytes 786440 | tf_op jit(solution)/shard_map/ppermute | solution.py:487
  70.1 19.7 %collective-permute-start.8 = (f32[4,4,32,128]{3,2,1,0:T(8,128)S(1)}, f32[4,4,32,128]{3,2,1,0:T(8,128)S(1)}, u32[]{:S(2)}, u32[]{:S(2)}) collective-permute-start(f32[4,4,32,128]{3,2,1,0:T(8,128)S(1)} %get-tuple-element.38), channel_id=1, source_target_pairs={{0,128},{32,160},{64,192},{96,224},{1,129},{33,161},{65,193},{97,2... | collective-permute-start | bytes 786440 | tf_op jit(solution)/shard_map/ppermute | solution.py:487
  89.9 0.7 copy-start.3
  90.6 20.7 %all-to-all-start.1 = ((f32[32,16,128]{2,1,0:T(8,128)}), f32[32,16,128]{2,1,0:T(8,128)S(1)}, u32[]{:S(2)}, u32[]{:S(2)}) async-start(f32[32,16,128]{2,1,0:T(8,128)} %bitcast.13), calls=%async_computation.1 | async-start | bytes 524288 | tf_op jit(solution)/shard_map/all_to_all | solution.py:558
  99.9 1.8 %collective-permute-start.9 = (f32[4,4,32,128]{3,2,1,0:T(8,128)}, f32[4,4,32,128]{3,2,1,0:T(8,128)S(1)}, u32[]{:S(2)}, u32[]{:S(2)}) collective-permute-start(f32[4,4,32,128]{3,2,1,0:T(8,128)} %copy-done.3), channel_id=1, source_target_pairs={{0,32},{32,0},{64,96},{96,64},{128,160},{160,128},{192,224},{224,1... | collective-permute-start | bytes 786440 | tf_op jit(solution)/shard_map/ppermute | solution.py:491
  101.7 9.6 %copy-start.6 = (f32[4,4,32,128]{3,2,1,0:T(8,128)}, f32[4,4,32,128]{3,2,1,0:T(8,128)S(1)}, u32[]{:S(2)}) copy-start(f32[4,4,32,128]{3,2,1,0:T(8,128)S(1)} %collective-permute-done.9.theirs) | copy-start | bytes 786436

commit v3 on v2

--- a/solution.py
+++ b/solution.py
@@ -34,22 +34,52 @@
     return pl.CostEstimate(flops=flops, bytes_accessed=size, transcendentals=trans)
 
 
-def prep_kernel(
-    dec_from, scale_from, guide_from, source, meas_from, xp, top, bottom, cum, tot, mm, dec, scale, guide, meas, traj, sems, scr
-):
-    small = [(dec_from, dec), (scale_from, scale), (guide_from, guide), (meas_from, meas)]
+def conv_tables(cw, bias, embed, ow, wt, wo, tall):
+    tall[...] = jnp.zeros_like(tall)
+    for e in range(3):
+        for a in range(3):
+            for b in range(3):
+                at = (e * 3 + a) * 48 + b * 8
+                tall[at : at + 8, 0:64] = 0.5 * cw[9 * a + 3 * b + e].astype(F32)
+    both = 0.5 * (bias[...].reshape(1, 64) + embed[...])
+    hi = both.astype(BF16).astype(F32)
+    mid = (both - hi).astype(BF16).astype(F32)
+    for i, piece in enumerate((hi, mid, both - hi - mid)):
+        tall[512 + 48 + 4 * i : 512 + 52 + 4 * i, 0:64] = piece
+    flat = tall[0:512, :].T[:64]
+    shift = tall[512:640, :].T[:64]
+    shift = jnp.concatenate([jnp.zeros((64, 384), F32), shift], axis=1)
+    for o in range(4):
+        moved = flat if o == 0 else pltpu.roll(flat, 8 * o, 1)
+        wt[o * 64 : o * 64 + 64, :] = (moved + shift)[:, :448].astype(BF16)
+    out = ow[...].astype(F32)
+    out = jnp.concatenate([out, out], axis=1)
+    out = jnp.concatenate([out] * 4, axis=1)
+    lane = lax.broadcasted_iota(jnp.int32, (8, 512), 1) // 64
+    own = lane == lax.broadcasted_iota(jnp.int32, (8, 512), 0)
+    for c in range(0, 8, 2):
+        rows = [jnp.where(own, jnp.broadcast_to(out[i : i + 1], (8, 512)), 0.0) for i in (c, c + 1)]
+        wo[c * 8 : c * 8 + 16, :] = jnp.concatenate(rows, axis=0).astype(BF16)
+
+
+def prep_kernel(*refs):
+    source = refs[8]
+    xp, top, bottom, cum, tot, mm, wt, wo = refs[9:17]
+    dec, scale, guide, meas, cw, bias, embed, ow, traj, sems, scr, tall = refs[17:]
+    small = list(zip(refs[:8], (dec, scale, guide, meas, cw, bias, embed, ow)))
     small = [pltpu.make_async_copy(a, b, sems.at[4 + i]) for i, (a, b) in enumerate(small)]
     copies = [pltpu.make_async_copy(source.at[:, :, z], traj.at[z], sems.at[z]) for z in range(4)]
-    for copy in small + copies:
+    for copy in copies + small:
         copy.start()
     for copy in small:
         copy.wait()
+    conv_tables(cw, bias, embed, ow, wt, wo, tall)
     wk = [scale[k] * guide[k] for k in range(4)]
     mm[...] = jnp.zeros_like(mm)
     for s in range(3):
         x = meas[s]
-        tall = jnp.concatenate([x] + [pltpu.roll(x, 128 - 32 * i, 1) for i in range(1, 4)], axis=0)
-        mm[pl.ds(s, 32, stride=8), :] = tall.T[:32]
+        stack = jnp.concatenate([x] + [pltpu.roll(x, 128 - 32 * i, 1) for i in range(1, 4)], axis=0)
+        mm[pl.ds(s, 32, stride=8), :] = stack.T[:32]
     for z in range(4):
         copies[z].wait()
         run = None
@@ -79,7 +109,8 @@
     tot[128:136, :] = jnp.full((8, 128), wk[0] + wk[1] + wk[2] + wk[3], F32)
 
 
-def prep(dec, scale, guide, traj, meas):
+def prep(dec, scale, guide, meas, conv_weight, conv_bias, step_embed, out_weight, traj):
+    conv_weight = conv_weight.swapaxes(1, 2)
     return pl.pallas_call(
         prep_kernel,
         out_shape=(
@@ -89,25 +120,32 @@
             jax.ShapeDtypeStruct((4, 128, 128), F32),
             jax.ShapeDtypeStruct((136, 128), F32),
             jax.ShapeDtypeStruct((256, 128), F32),
+            jax.ShapeDtypeStruct((256, 448), BF16),
+            jax.ShapeDtypeStruct((64, 512), BF16),
         ),
-        in_specs=[HBM] * 5,
-        out_specs=(VMEM,) * 6,
+        in_specs=[HBM] * 9,
+        out_specs=(VMEM,) * 8,
         scratch_shapes=[
             pltpu.SMEM((8,), F32),
             pltpu.SMEM((4,), F32),
             pltpu.SMEM((4,), F32),
             pltpu.VMEM((3, 32, 128), F32),
+            pltpu.VMEM((27, 8, 64), BF16),
+            pltpu.VMEM((64,), F32),
+            pltpu.VMEM((4, 64), F32),
+            pltpu.VMEM((8, 64), BF16),
             pltpu.VMEM((4, 4, 8, 32, 128), BF16),
-            pltpu.SemaphoreType.DMA((8,)),
+            pltpu.SemaphoreType.DMA((12,)),
             pltpu.VMEM((2, 256, 128), F32),
+            pltpu.VMEM((640, 128), F32),
         ],
         compiler_params=params(16),
         cost_estimate=cost(4_000_000, 2_600_000),
         name="prep",
-    )(*in_hbm(dec, scale, guide, traj, meas))
-
-
-def message_kernel(scale, guide, odd, cum, other, one, two, three, mm, held, msg, passed):
+    )(*in_hbm(dec, scale, guide, meas, conv_weight, conv_bias, step_embed, out_weight, traj))
+
+
+def message_kernel(scale, guide, odd, cum, other, one, two, three, mm, after, msg):
     wk = [scale[k] * guide[k] for k in range(4)]
     before = jnp.where(odd[0] == 0, 0.0, other[...]) + (one[...] + two[...] + three[...])
     for k in range(4):
@@ -122,20 +160,16 @@
         msg[d * MSG + 16 : d * MSG + 24, :] = jnp.where(sub >= 4, w, mm[d * 8 : d * 8 + 8, :])
 
 
-def message(scale, guide, odd, cum, parts, mm, held):
+def message(scale, guide, odd, cum, parts, mm, after):
     return pl.pallas_call(
         message_kernel,
-        out_shape=(
-            jax.ShapeDtypeStruct((32 * MSG, 128), F32),
-            jax.ShapeDtypeStruct(held.shape, held.dtype),
-        ),
+        out_shape=jax.ShapeDtypeStruct((32 * MSG, 128), F32),
         in_specs=[SMEM, SMEM, SMEM] + [VMEM] * 6 + [ANY],
-        out_specs=(VMEM, ANY),
-        input_output_aliases={9: 1},
+        out_specs=VMEM,
         compiler_params=params(8),
         cost_estimate=cost(100_000, 900_000),
         name="message",
-    )(scale, guide, odd, cum, *parts, mm, held)
+    )(*in_hbm(scale, guide), odd, cum, *parts, mm, after)
 
 
 def conv_kernel(zs, refs_of, ns_in, scale, nscale, *refs):
@@ -145,22 +179,23 @@
     done = None
     fetched = {}
     if ns_in == 3:
-        done_from, odd, extra = extra[0], extra[1], extra[2:]
-        run_ref, tot_ref, give_ref, scr, noise, start, sems, held_planes, done, more_sems = extra
+        done_from, odd, extra = extra[:2], extra[2], extra[4:]
+        run_ref, tot_ref, give_ref, scr, noise, start, sems, held_planes, done, begun, more_sems = extra
         sources = [ins[1], ins[0].at[:, 0], ins[0].at[:, 1], ins[0].at[:, 2], ins[0].at[:, 3], ins[2]]
         for p, source in enumerate(sources):
             fetched[p] = pltpu.make_async_copy(source, held_planes.at[p], more_sems.at[p])
             fetched[p].start()
-        fetched[6] = pltpu.make_async_copy(done_from, done, more_sems.at[6])
-        fetched[6].start()
+        for i in range(2):
+            fetched[6 + i] = pltpu.make_async_copy(done_from[i].at[3, :, 0], done.at[i], more_sems.at[6 + i])
+            fetched[8 + i] = pltpu.make_async_copy(start_from.at[:, 1 + i], begun.at[i], more_sems.at[8 + i])
+            fetched[6 + i].start()
+            fetched[8 + i].start()
         ins = [held_planes]
     else:
-        run_ref, tot_ref, scr, noise, start, sems = extra
+        run_ref, scr, noise, start, sems = extra[1:] if len(extra) == 6 else extra
 
     def put(value, z, rows):
-        if done is None:
-            tot_ref[:, z, rows, :] = value
-        else:
+        if done is not None:
             low, high = value[:4], value[4:]
             tot_ref[:, z, rows, :] = jnp.where(odd[0] == 0, low, high)
             give_ref[:, z, rows, :] = jnp.where(odd[0] == 0, high, low)
@@ -197,14 +232,14 @@
                 scr[p, 2, k, r * 16 : r * 16 + 16, :] = right.astype(BF16)
     row = lax.broadcasted_iota(jnp.int32, (16, 512), 0)
     kk = lax.broadcasted_iota(jnp.int32, (16, 512), 1) // 128
-    ones = jnp.where((row < 12) & (row // 3 == kk), 1.0, 0.0).astype(BF16)
+    ones = jnp.where((row < 12) & (row % 4 == kk), 1.0, 0.0).astype(BF16)
 
     for copy in copies:
         copy.wait()
 
     def block(step, carry):
         zi, yb = step // 2, step % 2
-        first = zi * (1 if zs == (1, 2) else 3)
+        first = 3 * zi
         zrow = pl.multiple_of(yb * 16, 16)
         grain = [noise[zi, k, :, pl.ds(zrow, 16), :].astype(F32) for k in range(4)]
         begin = start[zi, :, pl.ds(zrow, 16), :]
@@ -230,66 +265,69 @@
                 term = term + nscale[k] * grain[k][:, half * 8 : half * 8 + 8]
                 acc = term if acc is None else acc + term
                 run_ref[k, :, zi, pl.ds(at, 8), :] = acc + begin[:, half * 8 : half * 8 + 8]
-            put(acc, zi if done is None else 3 * zi, pl.ds(at, 8))
+            put(acc, 3 * zi, pl.ds(at, 8))
         return carry
 
-    lax.fori_loop(0, 4, block, 0)
+    lax.fori_loop(0, 2 * len(zs), block, 0)
     if done is not None:
-        fetched[6].wait()
         for z in range(2):
-            put(done[:, z], 1 + z, pl.ds(0, 32))
-
-
-def conv(zs, planes, scale, nscale, wt, wo, noise, start, done=None, odd=None):
-    inner = zs == (1, 2)
+            fetched[6 + z].wait()
+            fetched[8 + z].wait()
+            put(done[z] - begun[z], 1 + z, pl.ds(0, 32))
+
+
+def conv(zs, planes, scale, nscale, wt, wo, noise, start, done=None, odd=None, after=None):
+    inner = len(zs) == 1
 
     def refs_of(ins):
         own = ins[0]
 
         def of(z):
             if inner:
-                return lambda k: (lambda r: own[k, z, r * 16 : r * 16 + 16, :])
+                return lambda k: (lambda r: own[k, zs[0] - 1 + z, r * 16 : r * 16 + 16, :])
             return lambda k: (lambda r: own[z, k, r * 16 : r * 16 + 16, :])
 
-        return [of(z) for z in range(4 if inner else 6)]
-
-    more = [] if done is None else [*in_hbm(done), odd]
+        return [of(z) for z in range(3 * len(zs))]
+
+    more = [] if after is None else [after]
+    more = more if done is None else [*done, odd, after]
     extra = []
     if not inner:
         planes = in_hbm(*planes)
         extra = [
             pltpu.VMEM((6, 4, 256, 128), BF16),
-            pltpu.VMEM((8, 2, 32, 128), F32),
-            pltpu.SemaphoreType.DMA((7,)),
+            pltpu.VMEM((2, 8, 32, 128), F32),
+            pltpu.VMEM((2, 8, 32, 128), F32),
+            pltpu.SemaphoreType.DMA((10,)),
         ]
-    sums = [jax.ShapeDtypeStruct((8, 2, 32, 128), F32)]
+    sums = []
     if done is not None:
         sums = [jax.ShapeDtypeStruct((4, 4, 32, 128), F32)] * 2
     return pl.pallas_call(
         functools.partial(conv_kernel, zs, refs_of, len(planes)),
         out_shape=(
-            jax.ShapeDtypeStruct((4, 8, 2, 32, 128), F32),
+            jax.ShapeDtypeStruct((4, 8, len(zs), 32, 128), F32),
             *sums,
         ),
         in_specs=[SMEM, SMEM]
         + [VMEM if inner else HBM] * len(planes)
         + [VMEM, VMEM, HBM, HBM]
-        + [HBM, SMEM][: len(more)],
+        + ([ANY, ANY, SMEM, ANY] if done is not None else [ANY] * len(more)),
         out_specs=(VMEM,) * (1 + len(sums)),
         scratch_shapes=[
-            pltpu.VMEM((4 if inner else 6, 3, 4, 272, 128), BF16),
-            pltpu.VMEM((2, 4, 8, 32, 128), BF16),
-            pltpu.VMEM((2, 8, 32, 128), F32),
+            pltpu.VMEM((3 * len(zs), 3, 4, 272, 128), BF16),
+            pltpu.VMEM((len(zs), 4, 8, 32, 128), BF16),
+            pltpu.VMEM((len(zs), 8, 32, 128), F32),
             pltpu.SemaphoreType.DMA((2, 2)),
             *extra,
         ],
         compiler_params=params(16),
-        cost_estimate=cost(6_000_000_000, 4_000_000, 2_000_000),
-        name="conv_inner" if inner else "conv_outer",
-    )(scale, nscale, *planes, wt, wo, *in_hbm(noise, start), *more)
-
-
-def project_kernel(base, off, cosv, sinv, got, out, table, sino, meas):
+        cost_estimate=cost(3_000_000_000 * len(zs), 2_000_000 * len(zs), 1_000_000 * len(zs)),
+        name=f"conv_{zs[0]}" if inner else "conv_outer",
+    )(*in_hbm(scale, nscale), *planes, wt, wo, *in_hbm(noise, start), *more)
+
+
+def project_kernel(base, off, cosv, sinv, got, out, table, sino, meas, seen_hi, seen_lo):
     lane = lax.broadcasted_iota(jnp.int32, (16, 128), 1)
     low = lane < 64
     sino[...] = jnp.zeros_like(sino)
@@ -337,36 +375,37 @@
 
     lax.fori_loop(0, 8, forward, 0)
 
-    wide = lax.broadcasted_iota(jnp.int32, (NS, 128), 1)
+    whole = meas[...]
+    whole_hi = whole.astype(BF16).astype(F32)
+    seen_hi[...] = whole_hi
+    seen_lo[...] = pltpu.roll(whole - whole_hi, 1, 1)
+    wide = lax.broadcasted_iota(jnp.int32, (8, 128), 1)
+    is_hi = (wide >= 32) & (wide < 48)
+    is_lo = (wide >= 64) & (wide < 80)
+    is_seen = wide % 32 == 24
+    is_rest = wide % 32 == 25
 
     def misfit(v):
         at = pl.multiple_of(v * PAD, 8)
-        rows = sino[pl.ds(at + 24, NS), :]
-        rows = PROJ * (rows + pltpu.roll(rows, 96, 1))
-        hi = rows.astype(BF16).astype(F32)
-        lo = pltpu.roll(rows - hi, 32, 1)
-        seen = pltpu.roll(meas[...], lax.rem(128 + 24 - v, 128), 1)
-        seen_hi = seen.astype(BF16).astype(F32)
-        seen_lo = pltpu.roll(seen - seen_hi, 1, 1)
-        spread = jnp.where(
-            (wide >= 32) & (wide < 48),
-            hi,
-            jnp.where(
-                (wide >= 64) & (wide < 80),
-                lo,
-                jnp.where(wide % 32 == 24, seen_hi, jnp.where(wide % 32 == 25, seen_lo, 0.0)),
-            ),
-        )
+        turn = lax.rem(128 + 24 - v, 128)
+        for r in range(0, NS, 8):
+            rows = sino[pl.ds(at + 24 + r, 8), :]
+            rows = PROJ * (rows + pltpu.roll(rows, 96, 1))
+            hi = rows.astype(BF16).astype(F32)
+            lo = pltpu.roll(rows - hi, 32, 1)
+            top = pltpu.roll(seen_hi[r : r + 8, :], turn, 1)
+            rest = pltpu.roll(seen_lo[r : r + 8, :], turn, 1)
+            spread = jnp.where(is_hi, hi, jnp.where(is_lo, lo, 0.0))
+            sino[pl.ds(at + 24 + r, 8), :] = jnp.where(is_seen, top, jnp.where(is_rest, rest, spread))
         sino[pl.ds(at, 24), :] = jnp.zeros((24, 128), F32)
-        sino[pl.ds(at + 24, NS), :] = spread
         sino[pl.ds(at + 120, 48), :] = jnp.zeros((48, 128), F32)
 
     def misfits(group, carry):
-        for v in range(4):
-            misfit(group * 4 + v)
+        for v in range(16):
+            misfit(group * 16 + v)
         return carry
 
-    lax.fori_loop(0, NV // 4, misfits, 0)
+    lax.fori_loop(0, NV // 16, misfits, 0)
 
     upper = lax.broadcasted_iota(jnp.int32, (8, 256), 0) < 4
     wk = got[16:24, :]
@@ -410,6 +449,8 @@
             pltpu.VMEM((16, NV * WIN, 512), BF16),
             pltpu.VMEM((NV * PAD, 128), F32),
             pltpu.VMEM((NS, 128), F32),
+            pltpu.VMEM((NS, 128), F32),
+            pltpu.VMEM((NS, 128), F32),
         ],
         compiler_params=params(22),
         cost_estimate=cost(8_000_000_000, 2_000_000),
@@ -417,32 +458,33 @@
     )(base, off, cosv, sinv, got)
 
 
-def final_kernel(dec, odd, back, inner, outer, mine, theirs, new):
+def final_kernel(dec, odd, back, one, two, outer, mine, theirs, new):
     k = pl.program_id(0)
     columns = jnp.concatenate([back[pl.ds(4 * i + k, 32, stride=16), :] for i in range(4)], axis=0)
     cells = columns.T
     for z in range(4):
         guide = jnp.concatenate([cells[z * 16 : z * 16 + 16], cells[64 + z * 16 : 80 + z * 16]], axis=0)
         for c in range(8):
-            own = inner[0, c, z - 1] if z in (1, 2) else outer[0, c, z // 3]
+            own = (one, two)[z - 1][0, c, 0] if z in (1, 2) else outer[0, c, z // 3]
             before = jnp.where(odd[0] == c // 4, mine[c % 4, z], theirs[c % 4, z])
             new[0, c, z] = own + before - dec[c] * guide
 
 
-def final(dec, odd, back, inner, outer, mine, theirs):
+def final(dec, odd, back, one, two, outer, mine, theirs):
     whole = pl.BlockSpec((512, 128), lambda k: (0, 0))
     part = pl.BlockSpec((1, 8, 2, 32, 128), lambda k: (k, 0, 0, 0, 0))
+    single = pl.BlockSpec((1, 8, 1, 32, 128), lambda k: (k, 0, 0, 0, 0))
     half = pl.BlockSpec((4, 4, 32, 128), lambda k: (0, 0, 0, 0))
     return pl.pallas_call(
         final_kernel,
         grid=(4,),
         out_shape=jax.ShapeDtypeStruct((4, 8, 4, 32, 128), F32),
-        in_specs=[SMEM, SMEM, whole, part, part, half, half],
+        in_specs=[SMEM, SMEM, whole, single, single, part, half, half],
         out_specs=pl.BlockSpec((1, 8, 4, 32, 128), lambda k: (k, 0, 0, 0, 0)),
         compiler_params=params(16),
         cost_estimate=cost(2_000_000, 5_000_000),
         name="final",
-    )(*in_hbm(dec), odd, back, inner, outer, mine, theirs)
+    )(*in_hbm(dec), odd, back, one, two, outer, *in_hbm(mine), theirs)
 
 
 def add_kernel(a, b, held, out, passed):
@@ -462,24 +504,23 @@
     )(a, b, held)
 
 
-def send_kernel(odd, near, far, keep, given, held, send, mine, passed):
+def send_kernel(odd, near, far, keep, given, send, mine):
     first = odd[0] == 0
     chips = near[...] + far[...]
     send[...] = chips + jnp.where(first, keep[...], 0.0)
     mine[...] = chips + jnp.where(first, 0.0, given[...])
 
 
-def send_then(odd, near, far, keep, given, held):
+def send_on(odd, near, far, keep, given):
     return pl.pallas_call(
         send_kernel,
-        out_shape=(jax.ShapeDtypeStruct(near.shape, F32),) * 2 + (jax.ShapeDtypeStruct(held.shape, held.dtype),),
-        in_specs=[SMEM, VMEM, VMEM, VMEM, VMEM, ANY],
-        out_specs=(VMEM, VMEM, ANY),
-        input_output_aliases={5: 2},
+        out_shape=(jax.ShapeDtypeStruct(near.shape, F32),) * 2,
+        in_specs=[SMEM, VMEM, VMEM, VMEM, VMEM],
+        out_specs=(VMEM, VMEM),
         compiler_params=params(4),
         cost_estimate=cost(100_000, 1_500_000),
-        name="send_then",
-    )(odd, near, far, keep, given, held)
+        name="send_on",
+    )(odd, near, far, keep, given)
 
 
 def shifted(value, axis, step):
@@ -489,21 +530,6 @@
 
 def other_core(value):
     return lax.ppermute(value, "tm", [(i, i ^ 1) for i in range(lax.axis_size("tm"))])
-
-
-def conv_tables(conv_weight, conv_bias, step_embed, out_weight):
-    w = (conv_weight.astype(F32) * 0.5).reshape(3, 3, 3, 64, 8)
-    w = w.transpose(3, 2, 0, 1, 4)
-    rows = [jnp.pad(w, ((0, 0), (0, 0), (0, 0), (o, 3 - o), (0, 0))).reshape(64, 432) for o in range(4)]
-    bias = 0.5 * (conv_bias[None] + step_embed)
-    hi = lax.reduce_precision(bias, 8, 7)
-    mid = lax.reduce_precision(bias - hi, 8, 7)
-    low = bias - hi - mid
-    extra = jnp.stack([hi, mid, low], axis=1).reshape(12, 64).T
-    extra = jnp.pad(extra, ((0, 0), (0, 4)))
-    wt = jnp.concatenate([jnp.concatenate([r, extra], axis=1) for r in rows], axis=0).astype(BF16)
-    wo = out_weight[:, None, None, :] * jnp.eye(8, dtype=BF16)[None, :, :, None]
-    return wt, wo.reshape(64, 512)
 
 
 def windows(angle_index):
@@ -534,29 +560,31 @@
     noise_scale,
 ):
     odd = (lax.axis_index("tm") % 2).reshape(1)
-    xp, top, bottom, cum, tot, mm = prep(decoder, step_scale, guide_scale, trajectory, measured)
+    xp, top, bottom, cum, tot, mm, wt, wo = prep(
+        decoder, step_scale, guide_scale, measured, conv_weight, conv_bias, step_embed, out_weight, trajectory
+    )
     up = shifted(top, "space", 1)
     down = shifted(bottom, "space", -1)
     other = other_core(tot)
-    wt, wo = conv_tables(conv_weight, conv_bias, step_embed, out_weight)
     base, off, cosv, sinv = windows(angle_index)
-    inner, part = conv((1, 2), [xp], step_scale, noise_scale, wt, wo, noise, start)
+    own = (step_scale, noise_scale, wt, wo, noise, start)
+    (one,) = conv((1,), [xp], *own)
     both = tot + other
     parts = [other] + [shifted(both, "tm", 2 * i) for i in (1, 2, 3)]
-    outer, keep, give = conv((0, 3), [xp, up, down], step_scale, noise_scale, wt, wo, noise, start, part, odd)
-    msg, give = message(step_scale, guide_scale, odd, cum, parts, mm, give)
+    (two,) = conv((2,), [xp], *own, after=both)
+    msg = message(step_scale, guide_scale, odd, cum, parts, mm, two)
+    got = lax.all_to_all(msg.reshape(32, MSG, 128), "space", 0, 0, tiled=True)
+    outer, keep, give = conv((0, 3), [xp, up, down], *own, (one, two), odd, msg)
     given = other_core(give)
-    chip, msg = add_then(keep, given, msg)
+    chip, got = add_then(keep, given, got)
     near = shifted(chip, "tm", 2)
-    got = lax.all_to_all(msg.reshape(32, MSG, 128), "space", 0, 0, tiled=True)
-    two, got = add_then(chip, near, got)
-    far = shifted(two, "tm", 4)
     back = project(base, off, cosv, sinv, got.reshape(32 * MSG, 128))
-    send, mine, back = send_then(odd, near, far, keep, given, back)
-    (send,) = in_hbm(send)
+    chips, back = add_then(chip, near, back)
+    far = shifted(chips, "tm", 4)
+    send, mine = send_on(odd, near, far, keep, given)
     theirs = other_core(send)
     back = lax.all_to_all(back.reshape(32, 16, 128), "space", 0, 0, tiled=True)
-    return final(decoder, odd, back.reshape(512, 128), inner, outer, mine, theirs)
+    return final(decoder, odd, back.reshape(512, 128), one, two, outer, mine, theirs)
 
 
 def solution(mesh):

time: 117 us -> 104 us (0.89); the launches traced: 114 us -> 103 us
  waiting for transfers between devices: 22.6 us -> 17.3 us
  local copies, waits for them, and re-layouts: 5.42 us -> 0.96 us
  other arithmetic: 3.13 us -> 0.81 us
  Pallas kernels: 36.9 us -> 39.2 us
  starting transfers between devices: 45.9 us -> 44.7 us
    ppermute x7, waiting for transfers between devices: 8.02 us -> 0.02 us  [shifted(): lax.ppermute(value, axis, [(i, i + step) for i in range(count) if 0 <= i...]
    all_to_all x1, waiting for transfers between devices: 1.71 us -> 5.36 us  [on_device(): got = lax.all_to_all(msg.reshape(32, MSG, 128), 'space', 0, 0, tiled=True)]
    add x4, local copies, waits for them, and re-layouts: 2.6 us -> 0.16 us  [windows(): corner + jnp.minimum(0.0, 15.0 * cosv)[None]]
    ppermute x3, waiting for transfers between devices: 3.27 us -> 1.19 us  [other_core(): lax.ppermute(value, 'tm', [(i, i ^ 1) for i in range(lax.axis_size('tm'))])]
    pallas_call x2 -> x3, Pallas kernels: 13.8 us -> 15.8 us  [conv(): pl.pallas_call(functools.partial(conv_kernel, zs, refs_of, len(planes)),...]
    all_to_all x1, starting transfers between devices: 9.3 us -> 7.43 us  [on_device(): back = lax.all_to_all(back.reshape(32, 16, 128), 'space', 0, 0, tiled=True)]
    pallas_call x1, Pallas kernels: 15.4 us -> 13.7 us  [project(): pl.pallas_call(project_kernel, out_shape=jax.ShapeDtypeStruct((512, 128),...]
    another operation x3 -> x0, other arithmetic: 1.53 us -> none
  transfers between devices with their start and end apart: 12 -> 12, of which waited for: 5 -> 3; matrix products, arithmetic and copies ran while one was open for 6% -> 1% of each run, Pallas kernels for 26% -> 31%
where the time goes in v3:
time: 104 us; the launch traced here: 103 us
  starting transfers between devices  44.7 us (43%)
  Pallas kernels  39.2 us (38%)
  waiting for transfers between devices  17.3 us (17%)
    ppermute x7, starting transfers between devices, shifted(): lax.ppermute(value, axis, [(i, i + step) for i in range(count) if 0 <= i...  24.6 us
    pallas_call x3, Pallas kernels, conv(): pl.pallas_call(functools.partial(conv_kernel, zs, refs_of, len(planes)),...  15.8 us
    pallas_call x1, Pallas kernels, project(): pl.pallas_call(project_kernel, out_shape=jax.ShapeDtypeStruct((512, 128),...  13.7 us
    all_to_all x1, starting transfers between devices, on_device(): got = lax.all_to_all(msg.reshape(32, MSG, 128), 'space', 0, 0, tiled=True)  12.4 us
    all_to_all x1, waiting for transfers between devices, on_device(): back = lax.all_to_all(back.reshape(32, 16, 128), 'space', 0, 0, tiled=True)  10.8 us
    all_to_all x1, starting transfers between devices, on_device(): back = lax.all_to_all(back.reshape(32, 16, 128), 'space', 0, 0, tiled=True)  7.43 us
    all_to_all x1, waiting for transfers between devices, on_device(): got = lax.all_to_all(msg.reshape(32, MSG, 128), 'space', 0, 0, tiled=True)  5.36 us
    pallas_call x1, Pallas kernels, prep(): pl.pallas_call(prep_kernel, out_shape=(jax.ShapeDtypeStruct((4, 4, 256, 1...  3.72 us
  transfers between devices with their start and end apart: 12, of which 3 were waited for; matrix products, arithmetic and copies ran while one was open for 1% of the time, Pallas kernels for 31%

profile of v3, /device:TPU:6, one launch (start us, length us, event | category | flops | bytes accessed | tf_op | source)
XLA Modules:
  0.0 103.3 jit_solution(2548147784348487324)
XLA Ops:
  0.0 3.7 %prep.1 = (bf16[4,4,256,128]{3,2,1,0:T(8,128)(2,1)S(1)}, bf16[4,256,128]{2,1,0:T(8,128)(2,1)}, bf16[4,256,128]{2,1,0:T(8,128)(2,1)S(1)}, f32[4,128,128]{2,1,0:T(...) custom-call(f32[8]{0:T(128)} %dec.1, f32[4]{0:T(128)} %scale.7, ...), custom_call_target="tpu_custom_call" | custom-call | flops 4000000 | bytes 2600000 | tf_op jit(solution)/shard_map/prep/pallas_call | solution.py:114
  3.7 0.0 copy-start.1
  3.8 0.1 collective-permute-start.2
  3.9 3.5 %collective-permute-start = (bf16[4,256,128]{2,1,0:T(8,128)(2,1)}, bf16[4,256,128]{2,1,0:T(8,128)(2,1)}, u32[]{:S(2)}, u32[]{:S(2)}) collective-permute-start(bf16[4,256,128]{2,1,0:T(8,128)(2,1)} %get-tuple-element.23), channel_id=1, source_target_pairs={{0,1},{1,2},{2,3},{3,4},{4,5},{5,6},{6,7},{7,8},{8,9},{9,10},{10,1... | collective-permute-start | bytes 786440 | tf_op jit(solution)/shard_map/ppermute | solution.py:528
  7.3 4.5 %collective-permute-start.1 = (bf16[4,256,128]{2,1,0:T(8,128)(2,1)S(1)}, bf16[4,256,128]{2,1,0:T(8,128)(2,1)}, u32[]{:S(2)}, u32[]{:S(2)}) collective-permute-start(bf16[4,256,128]{2,1,0:T(8,128)(2,1)S(1)} %get-tuple-element.24), channel_id=1, source_target_pairs={{1,0},{2,1},{3,2},{4,3},{5,4},{6,5},{7,6},{8,7},{9,8},{10,9},{11,1... | collective-permute-start | bytes 786440 | tf_op jit(solution)/shard_map/ppermute | solution.py:528
  11.8 0.7 multiply_minimum_fusion.1
  12.5 4.2 %conv_1.1.refs_7_.one = f32[4,8,1,32,128]{4,3,2,1,0:T(8,128)S(1)} custom-call(f32[4]{0:T(128)} %scale.7, f32[4]{0:T(128)} %nscale.5, bf16[4,4,256,128]{3,2,1,0:T(8,128)(2,1)S(1)} %get-tuple-element.22.refs_0_, bf16[256,448]{1,0:T(8,128)(2,1)S(1)} %get-tuple-element.25.refs_1_.refs_3_, bf16[64,512]{1,0:T(8,128)(2,1)S(1)} %get-tuple-element.26.refs_2_.refs_4_, ...), custom_call_target="tpu_custom_call" | custom-call | flops 3000000000 | bytes 2000000 | tf_op jit(solution)/shard_map/conv_1/pallas_call | solution.py:306
  16.8 3.8 %collective-permute-start.3 = (f32[136,128]{1,0:T(8,128)S(1)}, f32[136,128]{1,0:T(8,128)S(1)}, u32[]{:S(2)}, u32[]{:S(2)}) collective-permute-start(f32[136,128]{1,0:T(8,128)S(1)} %add.77.refs_5_), channel_id=1, source_target_pairs={{0,64},{32,96},{64,128},{96,160},{128,192},{160,224},{1,65},{33,97... | collective-permute-start | bytes 208904 | tf_op jit(solution)/shard_map/ppermute | solution.py:528
  20.6 5.2 %collective-permute-start.4 = (f32[136,128]{1,0:T(8,128)S(1)}, f32[136,128]{1,0:T(8,128)S(1)}, u32[]{:S(2)}, u32[]{:S(2)}) collective-permute-start(f32[136,128]{1,0:T(8,128)S(1)} %add.77.refs_5_), channel_id=1, source_target_pairs={{0,128},{32,160},{64,192},{96,224},{1,129},{33,161},{65,193},{97,2... | collective-permute-start | bytes 208904 | tf_op jit(solution)/shard_map/ppermute | solution.py:528
  25.8 1.3 %collective-permute-start.5 = (f32[136,128]{1,0:T(8,128)S(1)}, f32[136,128]{1,0:T(8,128)S(1)}, u32[]{:S(2)}, u32[]{:S(2)}) collective-permute-start(f32[136,128]{1,0:T(8,128)S(1)} %add.77.refs_5_), channel_id=1, source_target_pairs={{0,192},{32,224},{1,193},{33,225},{2,194},{34,226},{3,195},{35,227... | collective-permute-start | bytes 208904 | tf_op jit(solution)/shard_map/ppermute | solution.py:528
  27.1 4.2 %conv_2.1.after.refs_8_.two = f32[4,8,1,32,128]{4,3,2,1,0:T(8,128)S(1)} custom-call(f32[4]{0:T(128)} %scale.7, f32[4]{0:T(128)} %nscale.5, bf16[4,4,256,128]{3,2,1,0:T(8,128)(2,1)S(1)} %get-tuple-element.22.refs_0_, bf16[256,448]{1,0:T(8,128)(2,1)S(1)} %get-tuple-element.25.refs_1_.refs_3_, bf16[64,512]{1,0:T(8,128)(2,1)S(1)} %get-tuple-element.26.refs_2_.refs_4_, ...), custom_call_target="tpu_custom_call" | custom-call | flops 3000000000 | bytes 2000000 | tf_op jit(solution)/shard_map/conv_2/pallas_call | solution.py:306
  31.4 0.0 collective-permute-done.4.two
  31.4 0.0 collective-permute-done.5.three
  31.4 1.6 %message.1.refs_10_ = f32[768,128]{1,0:T(8,128)} custom-call(f32[4]{0:T(128)} %scale.7, f32[4]{0:T(128)} %guide.1, s32[1]{0:T(128)} %bitcast.odd.refs_9_, f32[4,128,128]{2,1,0:T(8,128)S(1)} %get-tuple-element.28.cum, f32[136,128]{1,0:T(8,128)S(1)} %collective-permute-done.2.other, f32[136,128]{1,0:T(8,128)S(1)} %collective-permute-done.3.one, ...), custom_call_target="tpu_custom_call" | custom-call | flops 100000 | bytes 900000 | tf_op jit(solution)/shard_map/message/pallas_call | solution.py:164
  33.0 12.4 %all-to-all-start = ((f32[32,24,128]{2,1,0:T(8,128)}), f32[32,24,128]{2,1,0:T(8,128)S(1)}, u32[]{:S(2)}, u32[]{:S(2)}) async-start(f32[32,24,128]{2,1,0:T(8,128)} %bitcast.2), calls=%async_computation | async-start | bytes 786432 | tf_op jit(solution)/shard_map/all_to_all | solution.py:576
  45.4 7.3 %conv_outer.1 = (f32[4,8,2,32,128]{4,3,2,1,0:T(8,128)S(1)}, f32[4,4,32,128]{3,2,1,0:T(8,128)S(1)}, f32[4,4,32,128]{3,2,1,0:T(8,128)S(1)}) custom-call(f32[4]{0:T(128)} %scale.7, f32[4]{0:T(128)} %nscale.5, bf16[4,4,256,128]{3,2,1,0:T(8,128)(2,1)} %copy-done.1, bf16[4,256,128]{2,1,0:T(8,128)(2,1)} %collective-permute-done.refs_1_, ...), custom_call_target="tpu_custom_call" | custom-call | flops 6000000000 | bytes 4000000 | tf_op jit(solution)/shard_map/conv_outer/pallas_call | solution.py:306
  52.8 0.1 collective-permute-start.6
  52.9 0.1 add_add_fusion
  52.9 0.1 add.82
  53.0 0.1 add.84
  53.1 0.1 add.87
  53.2 1.2 %collective-permute-done.6.b.given = f32[4,4,32,128]{3,2,1,0:T(8,128)S(1)} collective-permute-done((f32[4,4,32,128]{3,2,1,0:T(8,128)S(1)}, f32[4,4,32,128]{3,2,1,0:T(8,128)S(1)}, u32[]{:S(2)}, u32[]{:S(2)}) %collective-permute-start.6) | collective-permute-done | bytes 262176 | tf_op jit(solution)/shard_map/ppermute | solution.py:532
  54.4 5.4 %all-to-all-done.held = f32[32,24,128]{2,1,0:T(8,128)S(1)} async-done(((f32[32,24,128]{2,1,0:T(8,128)}), f32[32,24,128]{2,1,0:T(8,128)S(1)}, u32[]{:S(2)}, u32[]{:S(2)}) %all-to-all-start) | async-done | bytes 393248 | tf_op jit(solution)/shard_map/all_to_all | solution.py:576
  59.8 1.9 %collective-permute-start.7 = (f32[4,4,32,128]{3,2,1,0:T(8,128)S(1)}, f32[4,4,32,128]{3,2,1,0:T(8,128)S(1)}, u32[]{:S(2)}, u32[]{:S(2)}) collective-permute-start(f32[4,4,32,128]{3,2,1,0:T(8,128)S(1)} %get-tuple-element.32.a), channel_id=1, source_target_pairs={{0,64},{32,96},{64,128},{96,160},{128,192},{160,224},{1,65},{33,97... | collective-permute-start | bytes 786440 | tf_op jit(solution)/shard_map/ppermute | solution.py:528
  61.7 13.7 %project.1.held = f32[512,128]{1,0:T(8,128)} custom-call(s32[512]{0:T(512)S(1)} %get-tuple-element.40.base, f32[512]{0:T(512)S(1)} %get-tuple-element.39.off, f32[32]{0:T(128)S(1)} %get-tuple-element.44.cosv, f32[32]{0:T(128)S(1)} %get-tuple-element.43.sinv, f32[768,128]{1,0:T(8,128)S(1)} %bitcast.6), custom_call_target="tpu_custom_call" | custom-call | flops 8000000000 | bytes 2000000 | tf_op jit(solution)/shard_map/project/pallas_call | solution.py:443
  75.4 0.7 add_then.3
  76.1 4.5 %collective-permute-start.8 = (f32[4,4,32,128]{3,2,1,0:T(8,128)}, f32[4,4,32,128]{3,2,1,0:T(8,128)S(1)}, u32[]{:S(2)}, u32[]{:S(2)}) collective-permute-start(f32[4,4,32,128]{3,2,1,0:T(8,128)} %get-tuple-element.36), channel_id=1, source_target_pairs={{0,128},{32,160},{64,192},{96,224},{1,129},{33,161},{65,193},{97,2... | collective-permute-start | bytes 786440 | tf_op jit(solution)/shard_map/ppermute | solution.py:528
  80.6 7.4 %all-to-all-start.1 = ((f32[32,16,128]{2,1,0:T(8,128)}), f32[32,16,128]{2,1,0:T(8,128)S(1)}, u32[]{:S(2)}, u32[]{:S(2)}) async-start(f32[32,16,128]{2,1,0:T(8,128)} %bitcast.4), calls=%async_computation.1 | async-start | bytes 524288 | tf_op jit(solution)/shard_map/all_to_all | solution.py:586
  88.0 0.8 send_on.1
  88.8 0.7 copy-done
  89.5 10.8 %all-to-all-done.1 = f32[32,16,128]{2,1,0:T(8,128)S(1)} async-done(((f32[32,16,128]{2,1,0:T(8,128)}), f32[32,16,128]{2,1,0:T(8,128)S(1)}, u32[]{:S(2)}, u32[]{:S(2)}) %all-to-all-start.1) | async-done | bytes 262176 | tf_op jit(solution)/shard_map/all_to_all | solution.py:586
  100.3 3.0 %final.1 = f32[4,8,4,32,128]{4,3,2,1,0:T(8,128)} custom-call(f32[8]{0:T(128)} %dec.1, s32[1]{0:T(128)} %bitcast.odd.refs_9_, f32[512,128]{1,0:T(8,128)S(1)} %bitcast.7, f32[4,8,1,32,128]{4,3,2,1,0:T(8,128)S(1)} %conv_1.1.refs_7_.one, f32[4,8,1,32,128]{4,3,2,1,0:T(8,128)S(1)} %conv_2.1.after.refs_8_.two, f32[4,8,2,32,128]{4,3,2,1,0:T(8,128)S(1)} %get-tuple-element.35.outer, ...), custom_call_target="tpu_custom_call" | custom-call | flops 2000000 | bytes 5000000 | tf_op jit(solution)/shard_map/final/pallas_call | solution.py:478
  (20 shorter events, 0.1 us)
Async XLA Ops:
  3.7 23.4 %copy-start.1 = (bf16[4,4,256,128]{3,2,1,0:T(8,128)(2,1)}, bf16[4,4,256,128]{3,2,1,0:T(8,128)(2,1)S(1)}, u32[]{:S(2)}) copy-start(bf16[4,4,256,128]{3,2,1,0:T(8,128)(2,1)S(1)} %get-tuple-element.22.refs_0_) | copy-start | bytes 3145732
  3.7 23.4 %copy-start.2 = (bf16[64,512]{1,0:T(8,128)(2,1)}, bf16[64,512]{1,0:T(8,128)(2,1)S(1)}, u32[]{:S(2)}) copy-start(bf16[64,512]{1,0:T(8,128)(2,1)S(1)} %get-tuple-element.26.refs_2_.refs_4_) | copy-start | bytes 196612
  3.8 13.0 %collective-permute-start.2 = (f32[136,128]{1,0:T(8,128)S(1)}, f32[136,128]{1,0:T(8,128)S(1)}, u32[]{:S(2)}, u32[]{:S(2)}) collective-permute-start(f32[136,128]{1,0:T(8,128)S(1)} %get-tuple-element.27), channel_id=1, source_target_pairs={{0,32},{32,0},{64,96},{96,64},{128,160},{160,128},{192,224},{224,1... | collective-permute-start | bytes 208904 | tf_op jit(solution)/shard_map/ppermute | solution.py:532
  3.9 41.5 %collective-permute-start = (bf16[4,256,128]{2,1,0:T(8,128)(2,1)}, bf16[4,256,128]{2,1,0:T(8,128)(2,1)}, u32[]{:S(2)}, u32[]{:S(2)}) collective-permute-start(bf16[4,256,128]{2,1,0:T(8,128)(2,1)} %get-tuple-element.23), channel_id=1, source_target_pairs={{0,1},{1,2},{2,3},{3,4},{4,5},{5,6},{6,7},{7,8},{8,9},{9,10},{10,1... | collective-permute-start | bytes 786440 | tf_op jit(solution)/shard_map/ppermute | solution.py:528
  7.3 38.0 %collective-permute-start.1 = (bf16[4,256,128]{2,1,0:T(8,128)(2,1)S(1)}, bf16[4,256,128]{2,1,0:T(8,128)(2,1)}, u32[]{:S(2)}, u32[]{:S(2)}) collective-permute-start(bf16[4,256,128]{2,1,0:T(8,128)(2,1)S(1)} %get-tuple-element.24), channel_id=1, source_target_pairs={{1,0},{2,1},{3,2},{4,3},{5,4},{6,5},{7,6},{8,7},{9,8},{10,9},{11,1... | collective-permute-start | bytes 786440 | tf_op jit(solution)/shard_map/ppermute | solution.py:528
  16.8 14.6 %collective-permute-start.3 = (f32[136,128]{1,0:T(8,128)S(1)}, f32[136,128]{1,0:T(8,128)S(1)}, u32[]{:S(2)}, u32[]{:S(2)}) collective-permute-start(f32[136,128]{1,0:T(8,128)S(1)} %add.77.refs_5_), channel_id=1, source_target_pairs={{0,64},{32,96},{64,128},{96,160},{128,192},{160,224},{1,65},{33,97... | collective-permute-start | bytes 208904 | tf_op jit(solution)/shard_map/ppermute | solution.py:528
  20.6 10.7 %collective-permute-start.4 = (f32[136,128]{1,0:T(8,128)S(1)}, f32[136,128]{1,0:T(8,128)S(1)}, u32[]{:S(2)}, u32[]{:S(2)}) collective-permute-start(f32[136,128]{1,0:T(8,128)S(1)} %add.77.refs_5_), channel_id=1, source_target_pairs={{0,128},{32,160},{64,192},{96,224},{1,129},{33,161},{65,193},{97,2... | collective-permute-start | bytes 208904 | tf_op jit(solution)/shard_map/ppermute | solution.py:528
  25.8 5.6 %collective-permute-start.5 = (f32[136,128]{1,0:T(8,128)S(1)}, f32[136,128]{1,0:T(8,128)S(1)}, u32[]{:S(2)}, u32[]{:S(2)}) collective-permute-start(f32[136,128]{1,0:T(8,128)S(1)} %add.77.refs_5_), channel_id=1, source_target_pairs={{0,192},{32,224},{1,193},{33,225},{2,194},{34,226},{3,195},{35,227... | collective-permute-start | bytes 208904 | tf_op jit(solution)/shard_map/ppermute | solution.py:528
  31.4 14.0 %copy-start.3 = (bf16[64,512]{1,0:T(8,128)(2,1)S(1)}, bf16[64,512]{1,0:T(8,128)(2,1)}, u32[]{:S(2)}) copy-start(bf16[64,512]{1,0:T(8,128)(2,1)} %copy-done.2) | copy-start | bytes 196612
  33.0 26.8 %all-to-all-start = ((f32[32,24,128]{2,1,0:T(8,128)}), f32[32,24,128]{2,1,0:T(8,128)S(1)}, u32[]{:S(2)}, u32[]{:S(2)}) async-start(f32[32,24,128]{2,1,0:T(8,128)} %bitcast.2), calls=%async_computation | async-start | bytes 786432 | tf_op jit(solution)/shard_map/all_to_all | solution.py:576
  52.8 1.6 %collective-permute-start.6 = (f32[4,4,32,128]{3,2,1,0:T(8,128)S(1)}, f32[4,4,32,128]{3,2,1,0:T(8,128)S(1)}, u32[]{:S(2)}, u32[]{:S(2)}) collective-permute-start(f32[4,4,32,128]{3,2,1,0:T(8,128)S(1)} %get-tuple-element.31), channel_id=1, source_target_pairs={{0,32},{32,0},{64,96},{96,64},{128,160},{160,128},{192,224},{224,1... | collective-permute-start | bytes 786440 | tf_op jit(solution)/shard_map/ppermute | solution.py:532
  59.8 15.6 %collective-permute-start.7 = (f32[4,4,32,128]{3,2,1,0:T(8,128)S(1)}, f32[4,4,32,128]{3,2,1,0:T(8,128)S(1)}, u32[]{:S(2)}, u32[]{:S(2)}) collective-permute-start(f32[4,4,32,128]{3,2,1,0:T(8,128)S(1)} %get-tuple-element.32.a), channel_id=1, source_target_pairs={{0,64},{32,96},{64,128},{96,160},{128,192},{160,224},{1,65},{33,97... | collective-permute-start | bytes 786440 | tf_op jit(solution)/shard_map/ppermute | solution.py:528
  76.1 11.9 %collective-permute-start.8 = (f32[4,4,32,128]{3,2,1,0:T(8,128)}, f32[4,4,32,128]{3,2,1,0:T(8,128)S(1)}, u32[]{:S(2)}, u32[]{:S(2)}) collective-permute-start(f32[4,4,32,128]{3,2,1,0:T(8,128)} %get-tuple-element.36), channel_id=1, source_target_pairs={{0,128},{32,160},{64,192},{96,224},{1,129},{33,161},{65,193},{97,2... | collective-permute-start | bytes 786440 | tf_op jit(solution)/shard_map/ppermute | solution.py:528
  80.6 19.7 %all-to-all-start.1 = ((f32[32,16,128]{2,1,0:T(8,128)}), f32[32,16,128]{2,1,0:T(8,128)S(1)}, u32[]{:S(2)}, u32[]{:S(2)}) async-start(f32[32,16,128]{2,1,0:T(8,128)} %bitcast.4), calls=%async_computation.1 | async-start | bytes 524288 | tf_op jit(solution)/shard_map/all_to_all | solution.py:586
  88.8 0.7 copy-start
  89.5 10.8 %collective-permute-start.9 = (f32[4,4,32,128]{3,2,1,0:T(8,128)}, f32[4,4,32,128]{3,2,1,0:T(8,128)S(1)}, u32[]{:S(2)}, u32[]{:S(2)}) collective-permute-start(f32[4,4,32,128]{3,2,1,0:T(8,128)} %get-tuple-element.38), channel_id=1, source_target_pairs={{0,32},{32,0},{64,96},{96,64},{128,160},{160,128},{192,224},{224,1... | collective-permute-start | bytes 786440 | tf_op jit(solution)/shard_map/ppermute | solution.py:532

commit v4 on v3

--- a/solution.py
+++ b/solution.py
@@ -234,15 +234,15 @@
     kk = lax.broadcasted_iota(jnp.int32, (16, 512), 1) // 128
     ones = jnp.where((row < 12) & (row % 4 == kk), 1.0, 0.0).astype(BF16)
 
-    for copy in copies:
-        copy.wait()
+    lazy = len(zs) == 1
+    if not lazy:
+        for copy in copies:
+            copy.wait()
 
     def block(step, carry):
         zi, yb = step // 2, step % 2
         first = 3 * zi
         zrow = pl.multiple_of(yb * 16, 16)
-        grain = [noise[zi, k, :, pl.ds(zrow, 16), :].astype(F32) for k in range(4)]
-        begin = start[zi, :, pl.ds(zrow, 16), :]
         for half in range(2):
             hidden = []
             for jj in range(2):
@@ -259,6 +259,16 @@
                 hidden.append((pre + pre * jnp.tanh(pre)).astype(BF16))
             eps = jnp.dot(wo[...], jnp.concatenate(hidden, axis=0), preferred_element_type=F32)
             at = pl.multiple_of(yb * 16 + half * 8, 8)
+            if half == 0:
+                if lazy:
+
+                    @pl.when(step == 0)
+                    def _():
+                        for copy in copies:
+                            copy.wait()
+
+                grain = [noise[zi, k, :, pl.ds(zrow, 16), :].astype(F32) for k in range(4)]
+                begin = start[zi, :, pl.ds(zrow, 16), :]
             acc = None
             for k in range(4):
                 term = scale[k] * eps[:, k * 128 : k * 128 + 128].reshape(8, 8, 128)
@@ -373,7 +383,7 @@
                 sino[at, :] = sino[at, :] + sums[v * WIN : (v + 1) * WIN]
         return carry
 
-    lax.fori_loop(0, 8, forward, 0)
+    lax.fori_loop(0, 8, forward, 0, unroll=2)
 
     whole = meas[...]
     whole_hi = whole.astype(BF16).astype(F32)
@@ -436,7 +446,7 @@
             out[pl.ds(at + 16, 16), :] = jnp.where(low, pltpu.roll(a, 64, 1), b)
         return carry
 
-    lax.fori_loop(0, 8, backward, 0)
+    lax.fori_loop(0, 8, backward, 0, unroll=4)
 
 
 def project(base, off, cosv, sinv, got):
@@ -458,33 +468,48 @@
     )(base, off, cosv, sinv, got)
 
 
-def final_kernel(dec, odd, back, one, two, outer, mine, theirs, new):
-    k = pl.program_id(0)
-    columns = jnp.concatenate([back[pl.ds(4 * i + k, 32, stride=16), :] for i in range(4)], axis=0)
-    cells = columns.T
-    for z in range(4):
-        guide = jnp.concatenate([cells[z * 16 : z * 16 + 16], cells[64 + z * 16 : 80 + z * 16]], axis=0)
-        for c in range(8):
-            own = (one, two)[z - 1][0, c, 0] if z in (1, 2) else outer[0, c, z // 3]
-            before = jnp.where(odd[0] == c // 4, mine[c % 4, z], theirs[c % 4, z])
-            new[0, c, z] = own + before - dec[c] * guide
+def final_kernel(dec, odd, back, one, two, outer, mine_from, theirs_from, new, held, mine, theirs, sems):
+    parts = [
+        pltpu.make_async_copy(mine_from, mine, sems.at[4]),
+        pltpu.make_async_copy(theirs_from, theirs, sems.at[5]),
+    ]
+    for part in parts:
+        part.start()
+    copies = []
+    for k in range(4):
+        columns = jnp.concatenate([back[pl.ds(4 * i + k, 32, stride=16), :] for i in range(4)], axis=0)
+        cells = columns.T
+        if k == 0:
+            for part in parts:
+                part.wait()
+        for z in range(4):
+            guide = jnp.concatenate([cells[z * 16 : z * 16 + 16], cells[64 + z * 16 : 80 + z * 16]], axis=0)
+            for c in range(8):
+                own = (one, two)[z - 1][k, c, 0] if z in (1, 2) else outer[k, c, z // 3]
+                before = jnp.where(odd[0] == c // 4, mine[c % 4, z], theirs[c % 4, z])
+                held[k, c, z] = own + before - dec[c] * guide
+        copies.append(pltpu.make_async_copy(held.at[k], new.at[k], sems.at[k]))
+        copies[k].start()
+    for copy in copies:
+        copy.wait()
 
 
 def final(dec, odd, back, one, two, outer, mine, theirs):
-    whole = pl.BlockSpec((512, 128), lambda k: (0, 0))
-    part = pl.BlockSpec((1, 8, 2, 32, 128), lambda k: (k, 0, 0, 0, 0))
-    single = pl.BlockSpec((1, 8, 1, 32, 128), lambda k: (k, 0, 0, 0, 0))
-    half = pl.BlockSpec((4, 4, 32, 128), lambda k: (0, 0, 0, 0))
     return pl.pallas_call(
         final_kernel,
-        grid=(4,),
         out_shape=jax.ShapeDtypeStruct((4, 8, 4, 32, 128), F32),
-        in_specs=[SMEM, SMEM, whole, single, single, part, half, half],
-        out_specs=pl.BlockSpec((1, 8, 4, 32, 128), lambda k: (k, 0, 0, 0, 0)),
-        compiler_params=params(16),
+        in_specs=[SMEM, SMEM] + [VMEM] * 4 + [ANY, ANY],
+        out_specs=HBM,
+        scratch_shapes=[
+            pltpu.VMEM((4, 8, 4, 32, 128), F32),
+            pltpu.VMEM((4, 4, 32, 128), F32),
+            pltpu.VMEM((4, 4, 32, 128), F32),
+            pltpu.SemaphoreType.DMA((6,)),
+        ],
+        compiler_params=params(8),
         cost_estimate=cost(2_000_000, 5_000_000),
         name="final",
-    )(*in_hbm(dec), odd, back, one, two, outer, *in_hbm(mine), theirs)
+    )(*in_hbm(dec), odd, back, one, two, outer, mine, theirs)
 
 
 def add_kernel(a, b, held, out, passed):

time: 104 us -> 103 us (level)
  Pallas kernels: 39.2 us -> 35.6 us
    pallas_call x1, Pallas kernels: 13.7 us -> 11.4 us  [project(): pl.pallas_call(project_kernel, out_shape=jax.ShapeDtypeStruct((512, 128),...]
  transfers between devices with their start and end apart: 12 -> 12, of which waited for: 3 -> 3; matrix products, arithmetic and copies ran while one was open for 1% -> 1% of each run, Pallas kernels for 31% -> 28%
where the time goes in v4:
time: 103 us; the launch traced here: 102 us
  starting transfers between devices  45.4 us (44%)
  Pallas kernels  35.6 us (35%)
  waiting for transfers between devices  17.8 us (17%)
  local copies, waits for them, and re-layouts  1.9 us (2%)
    ppermute x7, starting transfers between devices, shifted(): lax.ppermute(value, axis, [(i, i + step) for i in range(count) if 0 <= i...  25.4 us
    pallas_call x3, Pallas kernels, conv(): pl.pallas_call(functools.partial(conv_kernel, zs, refs_of, len(planes)),...  15.1 us
    all_to_all x1, starting transfers between devices, on_device(): got = lax.all_to_all(msg.reshape(32, MSG, 128), 'space', 0, 0, tiled=True)  12.4 us
    pallas_call x1, Pallas kernels, project(): pl.pallas_call(project_kernel, out_shape=jax.ShapeDtypeStruct((512, 128),...  11.4 us
    all_to_all x1, waiting for transfers between devices, on_device(): back = lax.all_to_all(back.reshape(32, 16, 128), 'space', 0, 0, tiled=True)  11.1 us
    all_to_all x1, starting transfers between devices, on_device(): back = lax.all_to_all(back.reshape(32, 16, 128), 'space', 0, 0, tiled=True)  7.41 us
    all_to_all x1, waiting for transfers between devices, on_device(): got = lax.all_to_all(msg.reshape(32, MSG, 128), 'space', 0, 0, tiled=True)  5.46 us
    pallas_call x1, Pallas kernels, prep(): pl.pallas_call(prep_kernel, out_shape=(jax.ShapeDtypeStruct((4, 4, 256, 1...  3.72 us
  transfers between devices with their start and end apart: 12, of which 3 were waited for; matrix products, arithmetic and copies ran while one was open for 1% of the time, Pallas kernels for 28%

profile of v4, /device:TPU:6, one launch (start us, length us, event | category | flops | bytes accessed | tf_op | source)
XLA Modules:
  0.0 102.0 jit_solution(10915767321435343566)
XLA Ops:
  0.0 3.7 %prep.1 = (bf16[4,4,256,128]{3,2,1,0:T(8,128)(2,1)S(1)}, bf16[4,256,128]{2,1,0:T(8,128)(2,1)}, bf16[4,256,128]{2,1,0:T(8,128)(2,1)S(1)}, f32[4,128,128]{2,1,0:T(...) custom-call(f32[8]{0:T(128)} %dec.1, f32[4]{0:T(128)} %scale.7, ...), custom_call_target="tpu_custom_call" | custom-call | flops 4000000 | bytes 2600000 | tf_op jit(solution)/shard_map/prep/pallas_call | solution.py:114
  3.7 0.0 copy-start.2
  3.7 0.1 collective-permute-start.2
  3.8 3.5 %collective-permute-start = (bf16[4,256,128]{2,1,0:T(8,128)(2,1)}, bf16[4,256,128]{2,1,0:T(8,128)(2,1)}, u32[]{:S(2)}, u32[]{:S(2)}) collective-permute-start(bf16[4,256,128]{2,1,0:T(8,128)(2,1)} %get-tuple-element.23), channel_id=1, source_target_pairs={{0,1},{1,2},{2,3},{3,4},{4,5},{5,6},{6,7},{7,8},{8,9},{9,10},{10,1... | collective-permute-start | bytes 786440 | tf_op jit(solution)/shard_map/ppermute | solution.py:553
  7.3 4.5 %collective-permute-start.1 = (bf16[4,256,128]{2,1,0:T(8,128)(2,1)S(1)}, bf16[4,256,128]{2,1,0:T(8,128)(2,1)}, u32[]{:S(2)}, u32[]{:S(2)}) collective-permute-start(bf16[4,256,128]{2,1,0:T(8,128)(2,1)S(1)} %get-tuple-element.24), channel_id=1, source_target_pairs={{1,0},{2,1},{3,2},{4,3},{5,4},{6,5},{7,6},{8,7},{9,8},{10,9},{11,1... | collective-permute-start | bytes 786440 | tf_op jit(solution)/shard_map/ppermute | solution.py:553
  11.8 0.7 multiply_minimum_fusion.1
  12.5 3.9 %conv_1.1.refs_7_.one = f32[4,8,1,32,128]{4,3,2,1,0:T(8,128)S(1)} custom-call(f32[4]{0:T(128)} %scale.7, f32[4]{0:T(128)} %nscale.5, bf16[4,4,256,128]{3,2,1,0:T(8,128)(2,1)S(1)} %get-tuple-element.22.refs_0_, bf16[256,448]{1,0:T(8,128)(2,1)S(1)} %get-tuple-element.25.refs_1_.refs_3_, bf16[64,512]{1,0:T(8,128)(2,1)S(1)} %get-tuple-element.26.refs_2_.refs_4_, ...), custom_call_target="tpu_custom_call" | custom-call | flops 3000000000 | bytes 2000000 | tf_op jit(solution)/shard_map/conv_1/pallas_call | solution.py:316
  16.4 0.0 collective-permute-done.2.other
  16.4 3.8 %collective-permute-start.3 = (f32[136,128]{1,0:T(8,128)S(1)}, f32[136,128]{1,0:T(8,128)S(1)}, u32[]{:S(2)}, u32[]{:S(2)}) collective-permute-start(f32[136,128]{1,0:T(8,128)S(1)} %add.77.refs_5_), channel_id=1, source_target_pairs={{0,64},{32,96},{64,128},{96,160},{128,192},{160,224},{1,65},{33,97... | collective-permute-start | bytes 208904 | tf_op jit(solution)/shard_map/ppermute | solution.py:553
  20.3 5.2 %collective-permute-start.4 = (f32[136,128]{1,0:T(8,128)S(1)}, f32[136,128]{1,0:T(8,128)S(1)}, u32[]{:S(2)}, u32[]{:S(2)}) collective-permute-start(f32[136,128]{1,0:T(8,128)S(1)} %add.77.refs_5_), channel_id=1, source_target_pairs={{0,128},{32,160},{64,192},{96,224},{1,129},{33,161},{65,193},{97,2... | collective-permute-start | bytes 208904 | tf_op jit(solution)/shard_map/ppermute | solution.py:553
  25.5 1.3 %collective-permute-start.5 = (f32[136,128]{1,0:T(8,128)S(1)}, f32[136,128]{1,0:T(8,128)S(1)}, u32[]{:S(2)}, u32[]{:S(2)}) collective-permute-start(f32[136,128]{1,0:T(8,128)S(1)} %add.77.refs_5_), channel_id=1, source_target_pairs={{0,192},{32,224},{1,193},{33,225},{2,194},{34,226},{3,195},{35,227... | collective-permute-start | bytes 208904 | tf_op jit(solution)/shard_map/ppermute | solution.py:553
  26.8 3.9 %conv_2.1.after.refs_8_.two = f32[4,8,1,32,128]{4,3,2,1,0:T(8,128)S(1)} custom-call(f32[4]{0:T(128)} %scale.7, f32[4]{0:T(128)} %nscale.5, bf16[4,4,256,128]{3,2,1,0:T(8,128)(2,1)S(1)} %get-tuple-element.22.refs_0_, bf16[256,448]{1,0:T(8,128)(2,1)S(1)} %get-tuple-element.25.refs_1_.refs_3_, bf16[64,512]{1,0:T(8,128)(2,1)S(1)} %get-tuple-element.26.refs_2_.refs_4_, ...), custom_call_target="tpu_custom_call" | custom-call | flops 3000000000 | bytes 2000000 | tf_op jit(solution)/shard_map/conv_2/pallas_call | solution.py:316
  30.7 1.6 %message.1.refs_10_ = f32[768,128]{1,0:T(8,128)} custom-call(f32[4]{0:T(128)} %scale.7, f32[4]{0:T(128)} %guide.1, s32[1]{0:T(128)} %bitcast.odd.refs_9_, f32[4,128,128]{2,1,0:T(8,128)S(1)} %get-tuple-element.28.cum, f32[136,128]{1,0:T(8,128)S(1)} %collective-permute-done.2.other, f32[136,128]{1,0:T(8,128)S(1)} %collective-permute-done.3.one, ...), custom_call_target="tpu_custom_call" | custom-call | flops 100000 | bytes 900000 | tf_op jit(solution)/shard_map/message/pallas_call | solution.py:164
  32.3 12.4 %all-to-all-start = ((f32[32,24,128]{2,1,0:T(8,128)}), f32[32,24,128]{2,1,0:T(8,128)S(1)}, u32[]{:S(2)}, u32[]{:S(2)}) async-start(f32[32,24,128]{2,1,0:T(8,128)} %bitcast.2), calls=%async_computation | async-start | bytes 786432 | tf_op jit(solution)/shard_map/all_to_all | solution.py:601
  44.7 7.3 %conv_outer.1 = (f32[4,8,2,32,128]{4,3,2,1,0:T(8,128)S(1)}, f32[4,4,32,128]{3,2,1,0:T(8,128)S(1)}, f32[4,4,32,128]{3,2,1,0:T(8,128)S(1)}) custom-call(f32[4]{0:T(128)} %scale.7, f32[4]{0:T(128)} %nscale.5, bf16[4,4,256,128]{3,2,1,0:T(8,128)(2,1)} %copy-done.2, bf16[4,256,128]{2,1,0:T(8,128)(2,1)} %collective-permute-done.refs_1_, ...), custom_call_target="tpu_custom_call" | custom-call | flops 6000000000 | bytes 4000000 | tf_op jit(solution)/shard_map/conv_outer/pallas_call | solution.py:316
  52.1 0.1 collective-permute-start.6
  52.2 0.1 add_add_fusion
  52.2 0.1 add.82
  52.3 0.1 add.84
  52.4 0.1 add.87
  52.5 1.2 %collective-permute-done.6.b.given = f32[4,4,32,128]{3,2,1,0:T(8,128)S(1)} collective-permute-done((f32[4,4,32,128]{3,2,1,0:T(8,128)S(1)}, f32[4,4,32,128]{3,2,1,0:T(8,128)S(1)}, u32[]{:S(2)}, u32[]{:S(2)}) %collective-permute-start.6) | collective-permute-done | bytes 262176 | tf_op jit(solution)/shard_map/ppermute | solution.py:557
  53.7 5.5 %all-to-all-done.held = f32[32,24,128]{2,1,0:T(8,128)S(1)} async-done(((f32[32,24,128]{2,1,0:T(8,128)}), f32[32,24,128]{2,1,0:T(8,128)S(1)}, u32[]{:S(2)}, u32[]{:S(2)}) %all-to-all-start) | async-done | bytes 393248 | tf_op jit(solution)/shard_map/all_to_all | solution.py:601
  59.2 2.7 %collective-permute-start.7 = (f32[4,4,32,128]{3,2,1,0:T(8,128)S(1)}, f32[4,4,32,128]{3,2,1,0:T(8,128)S(1)}, u32[]{:S(2)}, u32[]{:S(2)}) collective-permute-start(f32[4,4,32,128]{3,2,1,0:T(8,128)S(1)} %get-tuple-element.32.a), channel_id=1, source_target_pairs={{0,64},{32,96},{64,128},{96,160},{128,192},{160,224},{1,65},{33,97... | collective-permute-start | bytes 786440 | tf_op jit(solution)/shard_map/ppermute | solution.py:553
  61.9 11.4 %project.1.held = f32[512,128]{1,0:T(8,128)} custom-call(s32[512]{0:T(512)S(1)} %get-tuple-element.40.base, f32[512]{0:T(512)S(1)} %get-tuple-element.39.off, f32[32]{0:T(128)S(1)} %get-tuple-element.44.cosv, f32[32]{0:T(128)S(1)} %get-tuple-element.43.sinv, f32[768,128]{1,0:T(8,128)S(1)} %bitcast.6), custom_call_target="tpu_custom_call" | custom-call | flops 8000000000 | bytes 2000000 | tf_op jit(solution)/shard_map/project/pallas_call | solution.py:453
  73.3 0.7 add_then.3
  74.1 4.5 %collective-permute-start.8 = (f32[4,4,32,128]{3,2,1,0:T(8,128)}, f32[4,4,32,128]{3,2,1,0:T(8,128)S(1)}, u32[]{:S(2)}, u32[]{:S(2)}) collective-permute-start(f32[4,4,32,128]{3,2,1,0:T(8,128)} %get-tuple-element.36), channel_id=1, source_target_pairs={{0,128},{32,160},{64,192},{96,224},{1,129},{33,161},{65,193},{97,2... | collective-permute-start | bytes 786440 | tf_op jit(solution)/shard_map/ppermute | solution.py:553
  78.5 7.4 %all-to-all-start.1 = ((f32[32,16,128]{2,1,0:T(8,128)}), f32[32,16,128]{2,1,0:T(8,128)S(1)}, u32[]{:S(2)}, u32[]{:S(2)}) async-start(f32[32,16,128]{2,1,0:T(8,128)} %bitcast.4), calls=%async_computation.1 | async-start | bytes 524288 | tf_op jit(solution)/shard_map/all_to_all | solution.py:611
  86.0 0.8 send_on.1
  86.7 0.7 copy-done
  87.4 11.1 %all-to-all-done.1 = f32[32,16,128]{2,1,0:T(8,128)S(1)} async-done(((f32[32,16,128]{2,1,0:T(8,128)}), f32[32,16,128]{2,1,0:T(8,128)S(1)}, u32[]{:S(2)}, u32[]{:S(2)}) %all-to-all-start.1) | async-done | bytes 262176 | tf_op jit(solution)/shard_map/all_to_all | solution.py:611
  98.5 0.9 copy-done.1
  99.5 2.3 %final.1 = f32[4,8,4,32,128]{4,3,2,1,0:T(8,128)} custom-call(f32[8]{0:T(128)} %dec.1, s32[1]{0:T(128)} %bitcast.odd.refs_9_, f32[512,128]{1,0:T(8,128)S(1)} %bitcast.7, f32[4,8,1,32,128]{4,3,2,1,0:T(8,128)S(1)} %conv_1.1.refs_7_.one, f32[4,8,1,32,128]{4,3,2,1,0:T(8,128)S(1)} %conv_2.1.after.refs_8_.two, f32[4,8,2,32,128]{4,3,2,1,0:T(8,128)S(1)} %get-tuple-element.35.outer, ...), custom_call_target="tpu_custom_call" | custom-call | flops 2000000 | bytes 5000000 | tf_op jit(solution)/shard_map/final/pallas_call | solution.py:498
  (22 shorter events, 0.1 us)
Async XLA Ops:
  3.7 23.0 %copy-start.2 = (bf16[4,4,256,128]{3,2,1,0:T(8,128)(2,1)}, bf16[4,4,256,128]{3,2,1,0:T(8,128)(2,1)S(1)}, u32[]{:S(2)}) copy-start(bf16[4,4,256,128]{3,2,1,0:T(8,128)(2,1)S(1)} %get-tuple-element.22.refs_0_) | copy-start | bytes 3145732
  3.7 23.0 %copy-start.3 = (bf16[64,512]{1,0:T(8,128)(2,1)}, bf16[64,512]{1,0:T(8,128)(2,1)S(1)}, u32[]{:S(2)}) copy-start(bf16[64,512]{1,0:T(8,128)(2,1)S(1)} %get-tuple-element.26.refs_2_.refs_4_) | copy-start | bytes 196612
  3.7 12.7 %collective-permute-start.2 = (f32[136,128]{1,0:T(8,128)S(1)}, f32[136,128]{1,0:T(8,128)S(1)}, u32[]{:S(2)}, u32[]{:S(2)}) collective-permute-start(f32[136,128]{1,0:T(8,128)S(1)} %get-tuple-element.27), channel_id=1, source_target_pairs={{0,32},{32,0},{64,96},{96,64},{128,160},{160,128},{192,224},{224,1... | collective-permute-start | bytes 208904 | tf_op jit(solution)/shard_map/ppermute | solution.py:557
  3.8 40.8 %collective-permute-start = (bf16[4,256,128]{2,1,0:T(8,128)(2,1)}, bf16[4,256,128]{2,1,0:T(8,128)(2,1)}, u32[]{:S(2)}, u32[]{:S(2)}) collective-permute-start(bf16[4,256,128]{2,1,0:T(8,128)(2,1)} %get-tuple-element.23), channel_id=1, source_target_pairs={{0,1},{1,2},{2,3},{3,4},{4,5},{5,6},{6,7},{7,8},{8,9},{9,10},{10,1... | collective-permute-start | bytes 786440 | tf_op jit(solution)/shard_map/ppermute | solution.py:553
  7.3 37.4 %collective-permute-start.1 = (bf16[4,256,128]{2,1,0:T(8,128)(2,1)S(1)}, bf16[4,256,128]{2,1,0:T(8,128)(2,1)}, u32[]{:S(2)}, u32[]{:S(2)}) collective-permute-start(bf16[4,256,128]{2,1,0:T(8,128)(2,1)S(1)} %get-tuple-element.24), channel_id=1, source_target_pairs={{1,0},{2,1},{3,2},{4,3},{5,4},{6,5},{7,6},{8,7},{9,8},{10,9},{11,1... | collective-permute-start | bytes 786440 | tf_op jit(solution)/shard_map/ppermute | solution.py:553
  16.4 14.2 %collective-permute-start.3 = (f32[136,128]{1,0:T(8,128)S(1)}, f32[136,128]{1,0:T(8,128)S(1)}, u32[]{:S(2)}, u32[]{:S(2)}) collective-permute-start(f32[136,128]{1,0:T(8,128)S(1)} %add.77.refs_5_), channel_id=1, source_target_pairs={{0,64},{32,96},{64,128},{96,160},{128,192},{160,224},{1,65},{33,97... | collective-permute-start | bytes 208904 | tf_op jit(solution)/shard_map/ppermute | solution.py:553
  20.3 10.4 %collective-permute-start.4 = (f32[136,128]{1,0:T(8,128)S(1)}, f32[136,128]{1,0:T(8,128)S(1)}, u32[]{:S(2)}, u32[]{:S(2)}) collective-permute-start(f32[136,128]{1,0:T(8,128)S(1)} %add.77.refs_5_), channel_id=1, source_target_pairs={{0,128},{32,160},{64,192},{96,224},{1,129},{33,161},{65,193},{97,2... | collective-permute-start | bytes 208904 | tf_op jit(solution)/shard_map/ppermute | solution.py:553
  25.5 5.2 %collective-permute-start.5 = (f32[136,128]{1,0:T(8,128)S(1)}, f32[136,128]{1,0:T(8,128)S(1)}, u32[]{:S(2)}, u32[]{:S(2)}) collective-permute-start(f32[136,128]{1,0:T(8,128)S(1)} %add.77.refs_5_), channel_id=1, source_target_pairs={{0,192},{32,224},{1,193},{33,225},{2,194},{34,226},{3,195},{35,227... | collective-permute-start | bytes 208904 | tf_op jit(solution)/shard_map/ppermute | solution.py:553
  30.7 14.1 %copy-start.4 = (bf16[64,512]{1,0:T(8,128)(2,1)S(1)}, bf16[64,512]{1,0:T(8,128)(2,1)}, u32[]{:S(2)}) copy-start(bf16[64,512]{1,0:T(8,128)(2,1)} %copy-done.3) | copy-start | bytes 196612
  32.3 26.9 %all-to-all-start = ((f32[32,24,128]{2,1,0:T(8,128)}), f32[32,24,128]{2,1,0:T(8,128)S(1)}, u32[]{:S(2)}, u32[]{:S(2)}) async-start(f32[32,24,128]{2,1,0:T(8,128)} %bitcast.2), calls=%async_computation | async-start | bytes 786432 | tf_op jit(solution)/shard_map/all_to_all | solution.py:601
  52.1 1.6 %collective-permute-start.6 = (f32[4,4,32,128]{3,2,1,0:T(8,128)S(1)}, f32[4,4,32,128]{3,2,1,0:T(8,128)S(1)}, u32[]{:S(2)}, u32[]{:S(2)}) collective-permute-start(f32[4,4,32,128]{3,2,1,0:T(8,128)S(1)} %get-tuple-element.31), channel_id=1, source_target_pairs={{0,32},{32,0},{64,96},{96,64},{128,160},{160,128},{192,224},{224,1... | collective-permute-start | bytes 786440 | tf_op jit(solution)/shard_map/ppermute | solution.py:557
  59.2 14.1 %collective-permute-start.7 = (f32[4,4,32,128]{3,2,1,0:T(8,128)S(1)}, f32[4,4,32,128]{3,2,1,0:T(8,128)S(1)}, u32[]{:S(2)}, u32[]{:S(2)}) collective-permute-start(f32[4,4,32,128]{3,2,1,0:T(8,128)S(1)} %get-tuple-element.32.a), channel_id=1, source_target_pairs={{0,64},{32,96},{64,128},{96,160},{128,192},{160,224},{1,65},{33,97... | collective-permute-start | bytes 786440 | tf_op jit(solution)/shard_map/ppermute | solution.py:553
  74.1 11.9 %collective-permute-start.8 = (f32[4,4,32,128]{3,2,1,0:T(8,128)}, f32[4,4,32,128]{3,2,1,0:T(8,128)S(1)}, u32[]{:S(2)}, u32[]{:S(2)}) collective-permute-start(f32[4,4,32,128]{3,2,1,0:T(8,128)} %get-tuple-element.36), channel_id=1, source_target_pairs={{0,128},{32,160},{64,192},{96,224},{1,129},{33,161},{65,193},{97,2... | collective-permute-start | bytes 786440 | tf_op jit(solution)/shard_map/ppermute | solution.py:553
  78.5 20.0 %all-to-all-start.1 = ((f32[32,16,128]{2,1,0:T(8,128)}), f32[32,16,128]{2,1,0:T(8,128)S(1)}, u32[]{:S(2)}, u32[]{:S(2)}) async-start(f32[32,16,128]{2,1,0:T(8,128)} %bitcast.4), calls=%async_computation.1 | async-start | bytes 524288 | tf_op jit(solution)/shard_map/all_to_all | solution.py:611
  86.7 0.7 copy-start
  87.4 11.1 %collective-permute-start.9 = (f32[4,4,32,128]{3,2,1,0:T(8,128)}, f32[4,4,32,128]{3,2,1,0:T(8,128)S(1)}, u32[]{:S(2)}, u32[]{:S(2)}) collective-permute-start(f32[4,4,32,128]{3,2,1,0:T(8,128)} %get-tuple-element.38), channel_id=1, source_target_pairs={{0,32},{32,0},{64,96},{96,64},{128,160},{160,128},{192,224},{224,1... | collective-permute-start | bytes 786440 | tf_op jit(solution)/shard_map/ppermute | solution.py:557
  98.5 1.0 copy-start.1

commit v5 on v4

--- a/solution.py
+++ b/solution.py
@@ -509,7 +509,7 @@
         compiler_params=params(8),
         cost_estimate=cost(2_000_000, 5_000_000),
         name="final",
-    )(*in_hbm(dec), odd, back, one, two, outer, mine, theirs)
+    )(*in_hbm(dec), odd, back, one, two, outer, *in_hbm(mine), theirs)
 
 
 def add_kernel(a, b, held, out, passed):

time: 103 us -> 102 us (level)
  no operation moved by 1% of the time
where the time goes in v5:
time: 102 us
  starting transfers between devices  45.4 us (45%)
  Pallas kernels  36.4 us (36%)
  waiting for transfers between devices  17.8 us (17%)
    ppermute x7, starting transfers between devices, shifted(): lax.ppermute(value, axis, [(i, i + step) for i in range(count) if 0 <= i...  25.4 us
    pallas_call x3, Pallas kernels, conv(): pl.pallas_call(functools.partial(conv_kernel, zs, refs_of, len(planes)),...  15.1 us
    all_to_all x1, starting transfers between devices, on_device(): got = lax.all_to_all(msg.reshape(32, MSG, 128), 'space', 0, 0, tiled=True)  12.4 us
    pallas_call x1, Pallas kernels, project(): pl.pallas_call(project_kernel, out_shape=jax.ShapeDtypeStruct((512, 128),...  11.4 us
    all_to_all x1, waiting for transfers between devices, on_device(): back = lax.all_to_all(back.reshape(32, 16, 128), 'space', 0, 0, tiled=True)  11.1 us
    all_to_all x1, starting transfers between devices, on_device(): back = lax.all_to_all(back.reshape(32, 16, 128), 'space', 0, 0, tiled=True)  7.41 us
    all_to_all x1, waiting for transfers between devices, on_device(): got = lax.all_to_all(msg.reshape(32, MSG, 128), 'space', 0, 0, tiled=True)  5.44 us
    pallas_call x1, Pallas kernels, prep(): pl.pallas_call(prep_kernel, out_shape=(jax.ShapeDtypeStruct((4, 4, 256, 1...  3.72 us
  transfers between devices with their start and end apart: 12, of which 3 were waited for; matrix products, arithmetic and copies ran while one was open for 1% of the time, Pallas kernels for 28%

profile of v5, /device:TPU:6, one launch (start us, length us, event | category | flops | bytes accessed | tf_op | source)
XLA Modules:
  0.0 101.8 jit_solution(9043937191850731068)
XLA Ops:
  0.0 3.7 %prep.1 = (bf16[4,4,256,128]{3,2,1,0:T(8,128)(2,1)S(1)}, bf16[4,256,128]{2,1,0:T(8,128)(2,1)}, bf16[4,256,128]{2,1,0:T(8,128)(2,1)S(1)}, f32[4,128,128]{2,1,0:T(...) custom-call(f32[8]{0:T(128)} %dec.1, f32[4]{0:T(128)} %scale.7, ...), custom_call_target="tpu_custom_call" | custom-call | flops 4000000 | bytes 2600000 | tf_op jit(solution)/shard_map/prep/pallas_call | solution.py:114
  3.7 0.0 copy-start.1
  3.8 0.1 collective-permute-start.2
  3.9 3.5 %collective-permute-start = (bf16[4,256,128]{2,1,0:T(8,128)(2,1)}, bf16[4,256,128]{2,1,0:T(8,128)(2,1)}, u32[]{:S(2)}, u32[]{:S(2)}) collective-permute-start(bf16[4,256,128]{2,1,0:T(8,128)(2,1)} %get-tuple-element.23), channel_id=1, source_target_pairs={{0,1},{1,2},{2,3},{3,4},{4,5},{5,6},{6,7},{7,8},{8,9},{9,10},{10,1... | collective-permute-start | bytes 786440 | tf_op jit(solution)/shard_map/ppermute | solution.py:553
  7.3 4.5 %collective-permute-start.1 = (bf16[4,256,128]{2,1,0:T(8,128)(2,1)S(1)}, bf16[4,256,128]{2,1,0:T(8,128)(2,1)}, u32[]{:S(2)}, u32[]{:S(2)}) collective-permute-start(bf16[4,256,128]{2,1,0:T(8,128)(2,1)S(1)} %get-tuple-element.24), channel_id=1, source_target_pairs={{1,0},{2,1},{3,2},{4,3},{5,4},{6,5},{7,6},{8,7},{9,8},{10,9},{11,1... | collective-permute-start | bytes 786440 | tf_op jit(solution)/shard_map/ppermute | solution.py:553
  11.8 0.7 multiply_minimum_fusion.1
  12.5 3.9 %conv_1.1.refs_7_.one = f32[4,8,1,32,128]{4,3,2,1,0:T(8,128)S(1)} custom-call(f32[4]{0:T(128)} %scale.7, f32[4]{0:T(128)} %nscale.5, bf16[4,4,256,128]{3,2,1,0:T(8,128)(2,1)S(1)} %get-tuple-element.22.refs_0_, bf16[256,448]{1,0:T(8,128)(2,1)S(1)} %get-tuple-element.25.refs_1_.refs_3_, bf16[64,512]{1,0:T(8,128)(2,1)S(1)} %get-tuple-element.26.refs_2_.refs_4_, ...), custom_call_target="tpu_custom_call" | custom-call | flops 3000000000 | bytes 2000000 | tf_op jit(solution)/shard_map/conv_1/pallas_call | solution.py:316
  16.4 0.0 collective-permute-done.2.other
  16.4 3.8 %collective-permute-start.3 = (f32[136,128]{1,0:T(8,128)S(1)}, f32[136,128]{1,0:T(8,128)S(1)}, u32[]{:S(2)}, u32[]{:S(2)}) collective-permute-start(f32[136,128]{1,0:T(8,128)S(1)} %add.77.refs_5_), channel_id=1, source_target_pairs={{0,64},{32,96},{64,128},{96,160},{128,192},{160,224},{1,65},{33,97... | collective-permute-start | bytes 208904 | tf_op jit(solution)/shard_map/ppermute | solution.py:553
  20.3 5.2 %collective-permute-start.4 = (f32[136,128]{1,0:T(8,128)S(1)}, f32[136,128]{1,0:T(8,128)S(1)}, u32[]{:S(2)}, u32[]{:S(2)}) collective-permute-start(f32[136,128]{1,0:T(8,128)S(1)} %add.77.refs_5_), channel_id=1, source_target_pairs={{0,128},{32,160},{64,192},{96,224},{1,129},{33,161},{65,193},{97,2... | collective-permute-start | bytes 208904 | tf_op jit(solution)/shard_map/ppermute | solution.py:553
  25.5 1.3 %collective-permute-start.5 = (f32[136,128]{1,0:T(8,128)S(1)}, f32[136,128]{1,0:T(8,128)S(1)}, u32[]{:S(2)}, u32[]{:S(2)}) collective-permute-start(f32[136,128]{1,0:T(8,128)S(1)} %add.77.refs_5_), channel_id=1, source_target_pairs={{0,192},{32,224},{1,193},{33,225},{2,194},{34,226},{3,195},{35,227... | collective-permute-start | bytes 208904 | tf_op jit(solution)/shard_map/ppermute | solution.py:553
  26.8 3.9 %conv_2.1.after.refs_8_.two = f32[4,8,1,32,128]{4,3,2,1,0:T(8,128)S(1)} custom-call(f32[4]{0:T(128)} %scale.7, f32[4]{0:T(128)} %nscale.5, bf16[4,4,256,128]{3,2,1,0:T(8,128)(2,1)S(1)} %get-tuple-element.22.refs_0_, bf16[256,448]{1,0:T(8,128)(2,1)S(1)} %get-tuple-element.25.refs_1_.refs_3_, bf16[64,512]{1,0:T(8,128)(2,1)S(1)} %get-tuple-element.26.refs_2_.refs_4_, ...), custom_call_target="tpu_custom_call" | custom-call | flops 3000000000 | bytes 2000000 | tf_op jit(solution)/shard_map/conv_2/pallas_call | solution.py:316
  30.7 0.0 collective-permute-done.3.one
  30.7 1.6 %message.1.refs_10_ = f32[768,128]{1,0:T(8,128)} custom-call(f32[4]{0:T(128)} %scale.7, f32[4]{0:T(128)} %guide.1, s32[1]{0:T(128)} %bitcast.odd.refs_9_, f32[4,128,128]{2,1,0:T(8,128)S(1)} %get-tuple-element.28.cum, f32[136,128]{1,0:T(8,128)S(1)} %collective-permute-done.2.other, f32[136,128]{1,0:T(8,128)S(1)} %collective-permute-done.3.one, ...), custom_call_target="tpu_custom_call" | custom-call | flops 100000 | bytes 900000 | tf_op jit(solution)/shard_map/message/pallas_call | solution.py:164
  32.3 12.4 %all-to-all-start = ((f32[32,24,128]{2,1,0:T(8,128)}), f32[32,24,128]{2,1,0:T(8,128)S(1)}, u32[]{:S(2)}, u32[]{:S(2)}) async-start(f32[32,24,128]{2,1,0:T(8,128)} %bitcast.2), calls=%async_computation | async-start | bytes 786432 | tf_op jit(solution)/shard_map/all_to_all | solution.py:601
  44.7 7.3 %conv_outer.1 = (f32[4,8,2,32,128]{4,3,2,1,0:T(8,128)S(1)}, f32[4,4,32,128]{3,2,1,0:T(8,128)S(1)}, f32[4,4,32,128]{3,2,1,0:T(8,128)S(1)}) custom-call(f32[4]{0:T(128)} %scale.7, f32[4]{0:T(128)} %nscale.5, bf16[4,4,256,128]{3,2,1,0:T(8,128)(2,1)} %copy-done.1, bf16[4,256,128]{2,1,0:T(8,128)(2,1)} %collective-permute-done.refs_1_, ...), custom_call_target="tpu_custom_call" | custom-call | flops 6000000000 | bytes 4000000 | tf_op jit(solution)/shard_map/conv_outer/pallas_call | solution.py:316
  52.1 0.1 collective-permute-start.6
  52.2 0.1 add_add_fusion
  52.2 0.1 add.82
  52.3 0.1 add.84
  52.4 0.1 add.87
  52.5 1.2 %collective-permute-done.6.b.given = f32[4,4,32,128]{3,2,1,0:T(8,128)S(1)} collective-permute-done((f32[4,4,32,128]{3,2,1,0:T(8,128)S(1)}, f32[4,4,32,128]{3,2,1,0:T(8,128)S(1)}, u32[]{:S(2)}, u32[]{:S(2)}) %collective-permute-start.6) | collective-permute-done | bytes 262176 | tf_op jit(solution)/shard_map/ppermute | solution.py:557
  53.7 5.4 %all-to-all-done.held = f32[32,24,128]{2,1,0:T(8,128)S(1)} async-done(((f32[32,24,128]{2,1,0:T(8,128)}), f32[32,24,128]{2,1,0:T(8,128)S(1)}, u32[]{:S(2)}, u32[]{:S(2)}) %all-to-all-start) | async-done | bytes 393248 | tf_op jit(solution)/shard_map/all_to_all | solution.py:601
  59.2 2.7 %collective-permute-start.7 = (f32[4,4,32,128]{3,2,1,0:T(8,128)S(1)}, f32[4,4,32,128]{3,2,1,0:T(8,128)S(1)}, u32[]{:S(2)}, u32[]{:S(2)}) collective-permute-start(f32[4,4,32,128]{3,2,1,0:T(8,128)S(1)} %get-tuple-element.32.a), channel_id=1, source_target_pairs={{0,64},{32,96},{64,128},{96,160},{128,192},{160,224},{1,65},{33,97... | collective-permute-start | bytes 786440 | tf_op jit(solution)/shard_map/ppermute | solution.py:553
  61.9 11.4 %project.1.held = f32[512,128]{1,0:T(8,128)} custom-call(s32[512]{0:T(512)S(1)} %get-tuple-element.40.base, f32[512]{0:T(512)S(1)} %get-tuple-element.39.off, f32[32]{0:T(128)S(1)} %get-tuple-element.44.cosv, f32[32]{0:T(128)S(1)} %get-tuple-element.43.sinv, f32[768,128]{1,0:T(8,128)S(1)} %bitcast.6), custom_call_target="tpu_custom_call" | custom-call | flops 8000000000 | bytes 2000000 | tf_op jit(solution)/shard_map/project/pallas_call | solution.py:453
  73.3 0.7 add_then.3
  74.0 4.5 %collective-permute-start.8 = (f32[4,4,32,128]{3,2,1,0:T(8,128)}, f32[4,4,32,128]{3,2,1,0:T(8,128)S(1)}, u32[]{:S(2)}, u32[]{:S(2)}) collective-permute-start(f32[4,4,32,128]{3,2,1,0:T(8,128)} %get-tuple-element.36), channel_id=1, source_target_pairs={{0,128},{32,160},{64,192},{96,224},{1,129},{33,161},{65,193},{97,2... | collective-permute-start | bytes 786440 | tf_op jit(solution)/shard_map/ppermute | solution.py:553
  78.5 7.4 %all-to-all-start.1 = ((f32[32,16,128]{2,1,0:T(8,128)}), f32[32,16,128]{2,1,0:T(8,128)S(1)}, u32[]{:S(2)}, u32[]{:S(2)}) async-start(f32[32,16,128]{2,1,0:T(8,128)} %bitcast.4), calls=%async_computation.1 | async-start | bytes 524288 | tf_op jit(solution)/shard_map/all_to_all | solution.py:611
  85.9 0.8 send_on.1
  86.7 0.7 copy-done
  87.4 11.1 %all-to-all-done.1 = f32[32,16,128]{2,1,0:T(8,128)S(1)} async-done(((f32[32,16,128]{2,1,0:T(8,128)}), f32[32,16,128]{2,1,0:T(8,128)S(1)}, u32[]{:S(2)}, u32[]{:S(2)}) %all-to-all-start.1) | async-done | bytes 262176 | tf_op jit(solution)/shard_map/all_to_all | solution.py:611
  98.5 3.1 %final.1 = f32[4,8,4,32,128]{4,3,2,1,0:T(8,128)} custom-call(f32[8]{0:T(128)} %dec.1, s32[1]{0:T(128)} %bitcast.odd.refs_9_, f32[512,128]{1,0:T(8,128)S(1)} %bitcast.7, f32[4,8,1,32,128]{4,3,2,1,0:T(8,128)S(1)} %conv_1.1.refs_7_.one, f32[4,8,1,32,128]{4,3,2,1,0:T(8,128)S(1)} %conv_2.1.after.refs_8_.two, f32[4,8,2,32,128]{4,3,2,1,0:T(8,128)S(1)} %get-tuple-element.35.outer, ...), custom_call_target="tpu_custom_call" | custom-call | flops 2000000 | bytes 5000000 | tf_op jit(solution)/shard_map/final/pallas_call | solution.py:498
  (20 shorter events, 0.1 us)
Async XLA Ops:
  3.7 23.0 %copy-start.1 = (bf16[4,4,256,128]{3,2,1,0:T(8,128)(2,1)}, bf16[4,4,256,128]{3,2,1,0:T(8,128)(2,1)S(1)}, u32[]{:S(2)}) copy-start(bf16[4,4,256,128]{3,2,1,0:T(8,128)(2,1)S(1)} %get-tuple-element.22.refs_0_) | copy-start | bytes 3145732
  3.7 23.0 %copy-start.2 = (bf16[64,512]{1,0:T(8,128)(2,1)}, bf16[64,512]{1,0:T(8,128)(2,1)S(1)}, u32[]{:S(2)}) copy-start(bf16[64,512]{1,0:T(8,128)(2,1)S(1)} %get-tuple-element.26.refs_2_.refs_4_) | copy-start | bytes 196612
  3.8 12.7 %collective-permute-start.2 = (f32[136,128]{1,0:T(8,128)S(1)}, f32[136,128]{1,0:T(8,128)S(1)}, u32[]{:S(2)}, u32[]{:S(2)}) collective-permute-start(f32[136,128]{1,0:T(8,128)S(1)} %get-tuple-element.27), channel_id=1, source_target_pairs={{0,32},{32,0},{64,96},{96,64},{128,160},{160,128},{192,224},{224,1... | collective-permute-start | bytes 208904 | tf_op jit(solution)/shard_map/ppermute | solution.py:557
  3.9 40.8 %collective-permute-start = (bf16[4,256,128]{2,1,0:T(8,128)(2,1)}, bf16[4,256,128]{2,1,0:T(8,128)(2,1)}, u32[]{:S(2)}, u32[]{:S(2)}) collective-permute-start(bf16[4,256,128]{2,1,0:T(8,128)(2,1)} %get-tuple-element.23), channel_id=1, source_target_pairs={{0,1},{1,2},{2,3},{3,4},{4,5},{5,6},{6,7},{7,8},{8,9},{9,10},{10,1... | collective-permute-start | bytes 786440 | tf_op jit(solution)/shard_map/ppermute | solution.py:553
  7.3 37.4 %collective-permute-start.1 = (bf16[4,256,128]{2,1,0:T(8,128)(2,1)S(1)}, bf16[4,256,128]{2,1,0:T(8,128)(2,1)}, u32[]{:S(2)}, u32[]{:S(2)}) collective-permute-start(bf16[4,256,128]{2,1,0:T(8,128)(2,1)S(1)} %get-tuple-element.24), channel_id=1, source_target_pairs={{1,0},{2,1},{3,2},{4,3},{5,4},{6,5},{7,6},{8,7},{9,8},{10,9},{11,1... | collective-permute-start | bytes 786440 | tf_op jit(solution)/shard_map/ppermute | solution.py:553
  16.4 14.2 %collective-permute-start.3 = (f32[136,128]{1,0:T(8,128)S(1)}, f32[136,128]{1,0:T(8,128)S(1)}, u32[]{:S(2)}, u32[]{:S(2)}) collective-permute-start(f32[136,128]{1,0:T(8,128)S(1)} %add.77.refs_5_), channel_id=1, source_target_pairs={{0,64},{32,96},{64,128},{96,160},{128,192},{160,224},{1,65},{33,97... | collective-permute-start | bytes 208904 | tf_op jit(solution)/shard_map/ppermute | solution.py:553
  20.3 10.4 %collective-permute-start.4 = (f32[136,128]{1,0:T(8,128)S(1)}, f32[136,128]{1,0:T(8,128)S(1)}, u32[]{:S(2)}, u32[]{:S(2)}) collective-permute-start(f32[136,128]{1,0:T(8,128)S(1)} %add.77.refs_5_), channel_id=1, source_target_pairs={{0,128},{32,160},{64,192},{96,224},{1,129},{33,161},{65,193},{97,2... | collective-permute-start | bytes 208904 | tf_op jit(solution)/shard_map/ppermute | solution.py:553
  25.5 5.2 %collective-permute-start.5 = (f32[136,128]{1,0:T(8,128)S(1)}, f32[136,128]{1,0:T(8,128)S(1)}, u32[]{:S(2)}, u32[]{:S(2)}) collective-permute-start(f32[136,128]{1,0:T(8,128)S(1)} %add.77.refs_5_), channel_id=1, source_target_pairs={{0,192},{32,224},{1,193},{33,225},{2,194},{34,226},{3,195},{35,227... | collective-permute-start | bytes 208904 | tf_op jit(solution)/shard_map/ppermute | solution.py:553
  30.7 14.1 %copy-start.3 = (bf16[64,512]{1,0:T(8,128)(2,1)S(1)}, bf16[64,512]{1,0:T(8,128)(2,1)}, u32[]{:S(2)}) copy-start(bf16[64,512]{1,0:T(8,128)(2,1)} %copy-done.2) | copy-start | bytes 196612
  32.3 26.9 %all-to-all-start = ((f32[32,24,128]{2,1,0:T(8,128)}), f32[32,24,128]{2,1,0:T(8,128)S(1)}, u32[]{:S(2)}, u32[]{:S(2)}) async-start(f32[32,24,128]{2,1,0:T(8,128)} %bitcast.2), calls=%async_computation | async-start | bytes 786432 | tf_op jit(solution)/shard_map/all_to_all | solution.py:601
  52.1 1.6 %collective-permute-start.6 = (f32[4,4,32,128]{3,2,1,0:T(8,128)S(1)}, f32[4,4,32,128]{3,2,1,0:T(8,128)S(1)}, u32[]{:S(2)}, u32[]{:S(2)}) collective-permute-start(f32[4,4,32,128]{3,2,1,0:T(8,128)S(1)} %get-tuple-element.31), channel_id=1, source_target_pairs={{0,32},{32,0},{64,96},{96,64},{128,160},{160,128},{192,224},{224,1... | collective-permute-start | bytes 786440 | tf_op jit(solution)/shard_map/ppermute | solution.py:557
  59.2 14.1 %collective-permute-start.7 = (f32[4,4,32,128]{3,2,1,0:T(8,128)S(1)}, f32[4,4,32,128]{3,2,1,0:T(8,128)S(1)}, u32[]{:S(2)}, u32[]{:S(2)}) collective-permute-start(f32[4,4,32,128]{3,2,1,0:T(8,128)S(1)} %get-tuple-element.32.a), channel_id=1, source_target_pairs={{0,64},{32,96},{64,128},{96,160},{128,192},{160,224},{1,65},{33,97... | collective-permute-start | bytes 786440 | tf_op jit(solution)/shard_map/ppermute | solution.py:553
  74.0 11.9 %collective-permute-start.8 = (f32[4,4,32,128]{3,2,1,0:T(8,128)}, f32[4,4,32,128]{3,2,1,0:T(8,128)S(1)}, u32[]{:S(2)}, u32[]{:S(2)}) collective-permute-start(f32[4,4,32,128]{3,2,1,0:T(8,128)} %get-tuple-element.36), channel_id=1, source_target_pairs={{0,128},{32,160},{64,192},{96,224},{1,129},{33,161},{65,193},{97,2... | collective-permute-start | bytes 786440 | tf_op jit(solution)/shard_map/ppermute | solution.py:553
  78.5 20.0 %all-to-all-start.1 = ((f32[32,16,128]{2,1,0:T(8,128)}), f32[32,16,128]{2,1,0:T(8,128)S(1)}, u32[]{:S(2)}, u32[]{:S(2)}) async-start(f32[32,16,128]{2,1,0:T(8,128)} %bitcast.4), calls=%async_computation.1 | async-start | bytes 524288 | tf_op jit(solution)/shard_map/all_to_all | solution.py:611
  86.7 0.7 copy-start
  87.4 11.1 %collective-permute-start.9 = (f32[4,4,32,128]{3,2,1,0:T(8,128)}, f32[4,4,32,128]{3,2,1,0:T(8,128)S(1)}, u32[]{:S(2)}, u32[]{:S(2)}) collective-permute-start(f32[4,4,32,128]{3,2,1,0:T(8,128)} %get-tuple-element.38), channel_id=1, source_target_pairs={{0,32},{32,0},{64,96},{96,64},{128,160},{160,128},{192,224},{224,1... | collective-permute-start | bytes 786440 | tf_op jit(solution)/shard_map/ppermute | solution.py:557
